TPU v7x, 32 devices: a whole 2x2x4 slice. The times are simulated.
32 devices in a mesh: cfg: 2 (over y), prow: 8 (over z, x), pcol: 2 (over core).
Axes of the slice: x: 2, y: 2, z: 4, core: 2. Of those that a mesh axis runs over, the one named last changes fastest.
Arguments:
- sigma_top: float32 [2048, 1024], P(('cfg', 'prow'), 'pcol'), parts along dimension 0, as said below
- panel_l: float32 [2048, 4096], P(('cfg', 'pcol'), 'prow'), parts along dimension 0, may hold values from -0.4 to 0.4
- diag_inv: float32 [32, 256, 256], P(('cfg', 'prow')), parts along dimension 0, may hold values from -0.375 to 0.375
- pattern: int32 [32, 8], P(('cfg', 'prow')), parts along dimension 0, may hold values 0 or 1
Outputs:
- sigma_panel: float32 [2048, 4096], P(('cfg', 'pcol'), 'prow'), parts along dimension 0
- sigma_diag: float32 [32, 256, 256], P(('cfg', 'prow')), parts along dimension 0
There are 2 independent parts, one for each index of `cfg`. A program takes and returns all parts, laid end to end along the dimension named above; each array names one. Nothing has to cross between parts.
Inputs may be any that keep to these rules, and one draw needn't show every extreme that they name: sigma_top is symmetric.
All inputs are finite; a program needn't handle non-finite values. No bound on the sum of `pattern` on one device may be relied on, other than what follows from the above.
Results may differ from a plain program's by a relative error of at most 0.000078.
Values sent between devices are 32-bit elements; how exact they have to be, the bound alone decides.
No kernel may reach another device: no remote copies, remote signals or barrier semaphores. Data moves between devices by JAX's collectives and lax.ppermute only.
A program may use at most 64 MiB of HBM per device.

v0:
```python
import jax
import jax.numpy as jnp
from jax import lax
from jax.sharding import PartitionSpec as P

W = 1024


def local(sigma_top, panel_l, diag_inv, pattern):
    half_rows = panel_l.shape[0]
    local_sn = diag_inv.shape[0]
    width_sn = diag_inv.shape[1]
    row_mask = jnp.repeat(pattern.astype(jnp.float32), W // 8, axis=1)
    row_mask = lax.dynamic_slice_in_dim(row_mask, lax.axis_index("pcol") * half_rows, half_rows, 1)
    panel_three = (
        panel_l.reshape(half_rows, local_sn, width_sn) * jnp.transpose(row_mask)[:, :, None]
    )
    factor = jnp.einsum("wns,nst->wnt", panel_three, diag_inv, precision=lax.Precision.HIGHEST)
    factor_flat = factor.reshape(half_rows, local_sn * width_sn)
    gathered = lax.all_gather(sigma_top, "prow", axis=0, tiled=True)
    sigma_flat = lax.psum_scatter(
        -jnp.dot(
            gathered,
            factor_flat,
            precision=lax.Precision.HIGHEST,
            preferred_element_type=jnp.float32,
        ),
        "pcol",
        scatter_dimension=0,
        tiled=True,
    )
    sigma_three = sigma_flat.reshape(half_rows, local_sn, width_sn)
    cross_local = jnp.einsum("wnr,wnt->nrt", factor, sigma_three, precision=lax.Precision.HIGHEST)
    cross_part = lax.psum(cross_local, "pcol")
    own_part = jnp.einsum("nsr,nst->nrt", diag_inv, diag_inv, precision=lax.Precision.HIGHEST)
    return (sigma_flat, own_part - cross_part)


def solution(mesh):
    in_specs = (
        P(("cfg", "prow"), "pcol"),
        P(("cfg", "pcol"), "prow"),
        P(("cfg", "prow"), None, None),
        P(("cfg", "prow"), None),
    )
    out_specs = (P(("cfg", "pcol"), "prow"), P(("cfg", "prow"), None, None))
    return jax.shard_map(local, mesh=mesh, in_specs=in_specs, out_specs=out_specs, check_vma=False)
```

profile of v0, /device:TPU:1, one launch (start us, length us, event | category | flops | bytes accessed | tf_op | source)
XLA Modules:
  0.0 109.5 jit_solution(7687906963028621222)
XLA Ops:
  7.2 0.0 copy-start
  7.2 0.0 all-gather.2.cloned.1.call-start
  7.2 0.7 all-gather.2.cloned.1.call-update
  7.9 0.0 reduce-scatter.2.cloned.1.call-start
  8.0 0.7 convert_element_type.3
  8.6 0.1 broadcast_bitcast_fusion
  8.7 0.0 copy-done
  8.7 2.5 %fusion = f32[2,512,256]{1,2,0:T(8,128)S(1)} fusion(f32[2,256,256]{2,1,0:T(8,128)S(1)} %copy-done, f32[64,2,8,256]{3,2,1,0:T(8,128)} %bitcast.27, f32[512,2]{0,1:T(2,128)S(1)} %dynamic-slice_bitcast_fusion), kind=kOutput, calls=%fused_computation.3 | convolution fusion | flops 805568512 | bytes 2625536 | tf_op jit(solution)/shard_map/wns,nst->wnt/dot_general | solution.py:18
  11.3 49.2 %all-gather.2.cloned.1.call-done = f32[1024,512]{1,0:T(8,128)} async-done(((f32[128,512]{1,0:T(8,128)}), f32[1024,512]{1,0:T(8,128)}) %all-gather.2.cloned.1.call-update) | async-done | bytes 2097168 | tf_op jit(solution)/shard_map/all_gather | solution.py:20
  60.4 6.5 %negate_bitcast_fusion = f32[1024,512]{0,1:T(8,128)} fusion(f32[512,512]{0,1:T(8,128)S(1)} %bitcast.25, f32[1024,512]{1,0:T(8,128)} %all-gather.2.cloned.1.call-done), kind=kOutput, calls=%fused_computation | convolution fusion | flops 3221749760 | bytes 5242880 | tf_op jit(solution)/shard_map/dot_general | solution.py:22
  66.9 0.0 reduce-scatter.2.cloned.1.call-update
  67.0 0.0 all-reduce.2.cloned.1.call-start
  67.0 9.7 %reduce-scatter.2.cloned.1.call-done = f32[512,512]{0,1:T(8,128)} async-done(((f32[1024,512]{0,1:T(8,128)}), f32[512,512]{0,1:T(8,128)}) %reduce-scatter.2.cloned.1.call-update) | async-done | bytes 1048592 | tf_op jit(solution)/shard_map/reduce_scatter | solution.py:21
  76.7 0.0 copy-start.1
  76.7 3.3 %fusion.2 = f32[2,256,256]{2,1,0:T(8,128)} fusion(f32[512,2,256]{0,2,1:T(8,128)} %bitcast.26, f32[2,512,256]{1,2,0:T(8,128)S(1)} %fusion), kind=kOutput, calls=%fused_computation.5 | convolution fusion | flops 805306368 | bytes 2621440 | tf_op jit(solution)/shard_map/wnr,wnt->nrt/dot_general | solution.py:33
  79.9 0.0 all-reduce.2.cloned.1.call-update
  80.0 0.0 copy-done.1
  80.0 1.3 %copy.10 = f32[512,512]{1,0:T(8,128)} copy(f32[512,512]{0,1:T(8,128)S(1)} %copy-done.1) | data formatting | bytes 2097152
  81.3 18.7 %all-reduce.2.cloned.1.call-done = f32[2,256,256]{2,1,0:T(8,128)} async-done(((f32[2,256,256]{2,1,0:T(8,128)}), f32[2,256,256]{2,1,0:T(8,128)}) %all-reduce.2.cloned.1.call-update) | async-done | bytes 524304 | tf_op jit(solution)/shard_map/psum | solution.py:34
  100.0 2.9 %convolution_subtract_fusion = f32[2,256,256]{2,1,0:T(8,128)} fusion(f32[2,256,256]{2,1,0:T(8,128)} %all-reduce.2.cloned.1.call-done, f32[2,256,256]{2,1,0:T(8,128)S(1)} %copy-done), kind=kOutput, calls=%fused_computation.1 | convolution fusion | flops 402784256 | bytes 1572864 | tf_op jit(solution)/shard_map/nsr,nst->nrt/dot_general | solution.py:35
  (2 shorter events, 0.0 us)
Async XLA Ops:
  7.2 1.6 %copy-start = (f32[2,256,256]{2,1,0:T(8,128)S(1)}, f32[2,256,256]{2,1,0:T(8,128)}, u32[]{:S(2)}) copy-start(f32[2,256,256]{2,1,0:T(8,128)} %param.6) | copy-start | bytes 1572868
  7.2 53.3 %all-gather.2.cloned.1.call-start = ((), (), s32[]{:S(2)}) async-start(), calls=%async_computation.1 | async-start | bytes 2359296 | tf_op jit(solution)/shard_map/all_gather | solution.py:20
  7.9 68.8 %reduce-scatter.2.cloned.1.call-start = ((), (), s32[]{:S(2)}) async-start(), calls=%async_computation.2 | async-start | bytes 3145728 | tf_op jit(solution)/shard_map/reduce_scatter | solution.py:21
  67.0 33.1 %all-reduce.2.cloned.1.call-start = ((), (), s32[]{:S(2)}) async-start(), calls=%async_computation.3 | async-start | bytes 1048576 | tf_op jit(solution)/shard_map/psum | solution.py:34
  76.7 3.3 %copy-start.1 = (f32[512,512]{0,1:T(8,128)S(1)}, f32[512,512]{0,1:T(8,128)}, u32[]{:S(2)}) copy-start(f32[512,512]{0,1:T(8,128)} %reduce-scatter.2.cloned.1.call-done) | copy-start | bytes 3145732
Sparse Core Ops, SparseCore 0:
  10.1 50.2 all-gather.1
  67.1 9.5 reduce-scatter.1
  80.1 19.9 all-reduce.1
where the time goes:
time: 110 us; the launch traced here: 109 us
  waiting for transfers between devices  78.3 us (71%)
  matrix products  15.2 us (14%)
  between operations  13.8 us (13%)
  local copies, waits for them, and re-layouts  1.41 us (1%)
    all_gather x1, waiting for transfers between devices, local(): gathered = lax.all_gather(sigma_top, 'prow', axis=0, tiled=True)  49.2 us
    psum x1, waiting for transfers between devices, local(): cross_part = lax.psum(cross_local, 'pcol')  18.7 us
    reduce_scatter x1, waiting for transfers between devices, local(): lax.psum_scatter(-jnp.dot(gathered, factor_flat, precision=lax.Precision....  9.69 us
    dot_general x1, matrix products, local(): jnp.dot(gathered, factor_flat, precision=lax.Precision.HIGHEST, preferred...  6.49 us
    dot_general x1, matrix products, local(): jnp.einsum('wnr,wnt->nrt', factor, sigma_three, precision=lax.Precision.H...  3.25 us
    dot_general x1, matrix products, local(): jnp.einsum('nsr,nst->nrt', diag_inv, diag_inv, precision=lax.Precision.HI...  2.89 us
    dot_general x1, matrix products, local(): jnp.einsum('wns,nst->wnt', panel_three, diag_inv, precision=lax.Precision...  2.53 us
  transfers between devices with their start and end apart: 3, of which 3 were waited for; matrix products, arithmetic and copies ran while one was open for 4% of the time, Pallas kernels for 0%

commit v1 on v0

v1 whole, which is shorter than its diff:
```python
import functools

import jax
import jax.numpy as jnp
from jax import lax
from jax.experimental import pallas as pl
from jax.experimental.pallas import tpu as pltpu
from jax.sharding import PartitionSpec as P

W = 1024
BLOCK_ROWS = 8
AXES = ("cfg", "prow", "pcol")
VMEM = pl.BlockSpec(memory_space=pltpu.VMEM)
SMEM = pl.BlockSpec(memory_space=pltpu.SMEM)


def split(value):
    high = value.astype(jnp.bfloat16)
    low = (value - high.astype(jnp.float32)).astype(jnp.bfloat16)
    return high, low


def product(left, right, dims):
    dot = functools.partial(lax.dot_general, dimension_numbers=(dims, ((), ())), preferred_element_type=jnp.float32)
    return dot(left[0], right[0]) + (dot(left[0], right[1]) + dot(left[1], right[0]))


PLAIN = ((1,), (0,))
FIRST = ((0,), (0,))


def factor_kernel(pattern, panel, diag_inv, factor, own_part):
    core = lax.axis_index("pcol")
    rows, width = panel.shape[0], diag_inv.shape[1]
    block = W // BLOCK_ROWS
    for j in range(diag_inv.shape[0]):
        columns = pl.ds(j * width, width)
        inverse = split(diag_inv[j])
        masked = jnp.concatenate(
            [
                panel[pl.ds(r * block, block), columns]
                * pattern[j, core * (rows // block) + r].astype(jnp.float32)
                for r in range(rows // block)
            ],
            axis=0,
        )
        factor[:, columns] = product(split(masked), inverse, PLAIN)
        own_part[j] = product(inverse, inverse, FIRST)


def half_kernel(own, first, second, third, factor, factor_other, gathered, partial):
    prow = lax.axis_index("prow")
    place = lax.rem(prow, 4)
    diagonal = lax.div(prow, 4) == lax.axis_index("pcol")
    rows = own.shape[0]
    x_place = place + 1 - 2 * lax.rem(place, 2)
    z_place = lax.rem(place + 2, 4)
    both = lax.rem(x_place + 2, 4)
    for value, at in (
        (own, place),
        (first, jnp.where(diagonal, z_place, x_place)),
        (second, jnp.where(diagonal, x_place, z_place)),
        (third, both),
    ):
        gathered[pl.ds(pl.multiple_of(at * rows, rows), rows), :] = value[...]

    @pl.when(diagonal)
    def _():
        partial[...] = product(split(gathered[...]), split(factor[...]), FIRST)

    @pl.when(jnp.logical_not(diagonal))
    def _():
        partial[...] = product(split(gathered[...]), split(factor_other[...]), FIRST)


def panel_kernel(near_z, near_x, far_z, far_x, beside, partial, factor, factor_other, sigma, cross, block):
    prow = lax.axis_index("prow")
    place = lax.rem(prow, 4)
    diagonal = lax.div(prow, 4) == lax.axis_index("pcol")
    rows = near_z.shape[0]
    x_place = place + 1 - 2 * lax.rem(place, 2)
    z_place = lax.rem(place + 2, 4)
    both = lax.rem(x_place + 2, 4)
    own_factor = split(factor[...])

    @pl.when(diagonal)
    def _():
        sigma[...] = -(partial[...] + product(split(beside[...]), split(factor_other[...]), PLAIN))

    @pl.when(jnp.logical_not(diagonal))
    def _():
        for value, at in ((near_z, place), (near_x, x_place), (far_z, z_place), (far_x, both)):
            block[pl.ds(pl.multiple_of(at * rows, rows), rows), :] = value[...]
        sigma[...] = -(partial[...] + product(split(block[...]), own_factor, PLAIN))

    width = cross.shape[1]
    sigma_split = split(sigma[...])
    for j in range(cross.shape[0]):
        columns = slice(j * width, (j + 1) * width)
        cross[j] = product(
            tuple(part[:, columns] for part in own_factor), tuple(part[:, columns] for part in sigma_split), FIRST
        )


def call(kernel, out_shapes, flops, *args, smem=0, scratch=()):
    moved = sum(a.size * 4 for a in args) + sum(4 * o.size for o in out_shapes)
    return pl.pallas_call(
        kernel,
        out_shape=out_shapes,
        in_specs=[SMEM] * smem + [VMEM] * (len(args) - smem),
        out_specs=[VMEM] * len(out_shapes),
        scratch_shapes=scratch,
        cost_estimate=pl.CostEstimate(flops=flops, bytes_accessed=moved, transcendentals=0),
        compiler_params=pltpu.CompilerParams(vmem_limit_bytes=32 * 1024 * 1024),
    )(*args)


def permute(value, mesh, diagonal_step, other_step, swap=False):
    cfgs, prows, cores = (mesh.shape[axis] for axis in AXES)
    pairs = []
    for c in range(cfgs):
        for p in range(prows):
            for k in range(cores):
                step = diagonal_step if (p >= prows // 2) == (k == 1) else other_step
                if step is None:
                    continue
                to = 1 - k if swap else k
                pairs.append(((c * prows + p) * cores + k, (c * prows + (p ^ step)) * cores + to))
    return lax.ppermute(value, AXES, pairs)


def local_eight(mesh, sigma_top, panel_l, diag_inv, pattern):
    f32 = jnp.float32
    half_rows, own_columns = panel_l.shape
    shape = lambda *dims: jax.ShapeDtypeStruct(dims, f32)
    first = permute(sigma_top, mesh, 2, 1)
    near_z = permute(sigma_top, mesh, 4, None)
    far_z = permute(sigma_top, mesh, 6, None)
    second = permute(sigma_top, mesh, 1, 2)
    factor, own_part = call(
        factor_kernel,
        [shape(half_rows, own_columns), shape(*diag_inv.shape)],
        2 * half_rows * own_columns * diag_inv.shape[1],
        pattern,
        panel_l,
        diag_inv,
        smem=1,
    )
    factor_other = permute(factor, mesh, 0, 0, swap=True)
    third = permute(first, mesh, 1, 2)
    near_x = permute(near_z, mesh, None, 1)
    far_x = permute(far_z, mesh, None, 1)
    gathered, partial = call(
        half_kernel,
        [shape(half_rows, sigma_top.shape[1]), shape(half_rows, own_columns)],
        2 * half_rows * half_rows * own_columns,
        sigma_top,
        first,
        second,
        third,
        factor,
        factor_other,
    )
    beside = permute(gathered, mesh, None, 0, swap=True)
    sigma, cross = call(
        panel_kernel,
        [shape(half_rows, own_columns), shape(*diag_inv.shape)],
        2 * half_rows * half_rows * own_columns,
        near_z,
        near_x,
        far_z,
        far_x,
        beside,
        partial,
        factor,
        factor_other,
        scratch=[pltpu.VMEM((half_rows, half_rows), f32)],
    )
    cross_other = permute(cross, mesh, 0, 0, swap=True)
    return sigma, own_part - (cross + cross_other)


def local_any(sigma_top, panel_l, diag_inv, pattern):
    half_rows = panel_l.shape[0]
    local_sn, width = diag_inv.shape[:2]
    row_mask = jnp.repeat(pattern.astype(jnp.float32), W // BLOCK_ROWS, axis=1)
    row_mask = lax.dynamic_slice_in_dim(row_mask, lax.axis_index("pcol") * half_rows, half_rows, 1)
    masked = panel_l.reshape(half_rows, local_sn, width) * jnp.transpose(row_mask)[:, :, None]
    factor = jnp.einsum("wns,nst->wnt", masked, diag_inv, precision=lax.Precision.HIGHEST)
    factor_flat = factor.reshape(half_rows, local_sn * width)
    whole = lax.all_gather(factor_flat, "pcol", axis=0, tiled=True)
    gathered = lax.all_gather(sigma_top, "prow", axis=0, tiled=True)
    sigma = -jnp.einsum("wv,wt->vt", gathered, whole, precision=lax.Precision.HIGHEST)
    sigma_three = sigma.reshape(half_rows, local_sn, width)
    cross = lax.psum(jnp.einsum("wnr,wnt->nrt", factor, sigma_three, precision=lax.Precision.HIGHEST), "pcol")
    own_part = jnp.einsum("nsr,nst->nrt", diag_inv, diag_inv, precision=lax.Precision.HIGHEST)
    return sigma, own_part - cross


def solution(mesh):
    in_specs = (
        P(("cfg", "prow"), "pcol"),
        P(("cfg", "pcol"), "prow"),
        P(("cfg", "prow"), None, None),
        P(("cfg", "prow"), None),
    )
    out_specs = (P(("cfg", "pcol"), "prow"), P(("cfg", "prow"), None, None))
    local = functools.partial(local_eight, mesh) if mesh.shape["prow"] == 8 else local_any
    return jax.shard_map(local, mesh=mesh, in_specs=in_specs, out_specs=out_specs, check_vma=False)
```

time: 110 us -> 53.8 us (0.49)
  waiting for transfers between devices: 78.3 us -> 23.5 us
  starting transfers between devices: 0.12 us -> 20.7 us
  matrix products: 15.2 us -> 0 us
  between operations: 13.8 us -> 0.71 us
  Pallas kernels: 0 us -> 4.7 us
  local copies, waits for them, and re-layouts: 1.41 us -> 2.94 us
    all_gather x1 -> x0, waiting for transfers between devices: 49.2 us -> none  [local(): gathered = lax.all_gather(sigma_top, 'prow', axis=0, tiled=True)]
    ppermute x0 -> x10, waiting for transfers between devices: none -> 23.5 us  [permute(): return lax.ppermute(value, AXES, pairs)]
    ppermute x0 -> x10, starting transfers between devices: none -> 20.7 us  [permute(): return lax.ppermute(value, AXES, pairs)]
    psum x1 -> x0, waiting for transfers between devices: 18.7 us -> none  [local(): cross_part = lax.psum(cross_local, 'pcol')]
    dot_general x4 -> x0, matrix products: 15.2 us -> none  [the longest x1 6.49 us: local(): jnp.dot(gathered, factor_flat, precision=lax.Precision.HIGHEST, preferred...]
    reduce_scatter x1 -> x0, waiting for transfers between devices: 9.69 us -> none  [local(): lax.psum_scatter(-jnp.dot(gathered, factor_flat, precision=lax.Precision....]
    pallas_call x0 -> x3, Pallas kernels: none -> 4.7 us  [call(): pl.pallas_call(kernel, out_shape=out_shapes, in_specs=[SMEM] * smem + [VM...]
    unnamed x7 -> x8, local copies, waits for them, and re-layouts: 1.4 us -> 2.94 us
  transfers between devices with their start and end apart: 3 -> 10, of which waited for: 3 -> 6; matrix products, arithmetic and copies ran while one was open for 4% -> 0% of each run, Pallas kernels for 0% -> 0%
where the time goes in v1:
time: 53.8 us; the launch traced here: 53.4 us
  waiting for transfers between devices  23.5 us (44%)
  starting transfers between devices  20.7 us (38%)
  Pallas kernels  4.7 us (9%)
  local copies, waits for them, and re-layouts  2.94 us (5%)
  other arithmetic  0.89 us (2%)
  between operations  0.71 us (1%)
    ppermute x10, waiting for transfers between devices, permute(): return lax.ppermute(value, AXES, pairs)  23.5 us
    ppermute x10, starting transfers between devices, permute(): return lax.ppermute(value, AXES, pairs)  20.7 us
    pallas_call x3, Pallas kernels, call(): pl.pallas_call(kernel, out_shape=out_shapes, in_specs=[SMEM] * smem + [VM...  4.7 us
    unnamed x8, local copies, waits for them, and re-layouts  2.94 us
  transfers between devices with their start and end apart: 10, of which 6 were waited for; matrix products, arithmetic and copies ran while one was open for 0% of the time, Pallas kernels for 0%

profile of v1, /device:TPU:1, one launch (start us, length us, event | category | flops | bytes accessed | tf_op | source)
XLA Modules:
  0.0 53.4 jit_solution(9250918096303471677)
XLA Ops:
  0.6 0.0 copy-start
  0.6 1.2 %copy-done = f32[512,512]{1,0:T(8,128)S(1)} copy-done((f32[512,512]{1,0:T(8,128)S(1)}, f32[512,512]{1,0:T(8,128)}, u32[]{:S(2)}) %copy-start) | copy-done | bytes 1048600
  1.9 0.0 copy-start.1
  1.9 1.0 %copy-done.1 = f32[2,256,256]{2,1,0:T(8,128)S(1)} copy-done((f32[2,256,256]{2,1,0:T(8,128)S(1)}, f32[2,256,256]{2,1,0:T(8,128)}, u32[]{:S(2)}) %copy-start.1) | copy-done | bytes 524312
  2.9 0.0 copy-start.3
  2.9 0.7 %copy-done.3 = s32[2,8]{1,0:T(2,128)S(1)} copy-done((s32[2,8]{1,0:T(2,128)S(1)}, s32[2,8]{1,0:T(2,128)}, u32[]{:S(2)}) %copy-start.3) | copy-done | bytes 88
  3.6 0.0 copy-start.2
  3.6 1.4 %shard_map.59 = (f32[512,512]{1,0:T(8,128)S(1)}, f32[2,256,256]{2,1,0:T(8,128)S(1)}) custom-call(s32[2,8]{1,0:T(2,128)S(1)} %copy-done.3, f32[512,512]{1,0:T(8,128)S(1)} %copy-done, f32[2,256,256]{2,1,0:T(8,128)S(1)} %copy-done.1), custom_call_target="tpu_custom_call" | custom-call | flops 134217728 | bytes 3145792 | tf_op jit(solution)/shard_map/pallas_call | solution.py:107
  4.9 0.1 collective-permute-start.7
  5.1 0.0 copy-done.2
  5.1 2.7 %collective-permute-start.4 = (f32[128,512]{1,0:T(8,128)S(1)}, f32[128,512]{1,0:T(8,128)S(1)}, u32[]{:S(2)}, u32[]{:S(2)}) collective-permute-start(f32[128,512]{1,0:T(8,128)S(1)} %copy-done.2), channel_id=1, source_target_pairs={{0,4},{1,3},{2,6},{3,1},{4,0},{5,7},{6,2},{7,5},{8,10},{9,13},{10,... | collective-permute-start | bytes 786440 | tf_op jit(solution)/shard_map/ppermute | solution.py:129
  7.7 1.3 %collective-permute-start.5 = (f32[128,512]{1,0:T(8,128)S(1)}, f32[128,512]{1,0:T(8,128)S(1)}, u32[]{:S(2)}, u32[]{:S(2)}) collective-permute-start(f32[128,512]{1,0:T(8,128)S(1)} %copy-done.2), channel_id=1, source_target_pairs={{0,2},{1,5},{2,0},{3,7},{4,6},{5,1},{6,4},{7,3},{8,12},{9,11},{10,... | collective-permute-start | bytes 786440 | tf_op jit(solution)/shard_map/ppermute | solution.py:129
  9.0 3.1 %collective-permute-done.4.first = f32[128,512]{1,0:T(8,128)S(1)} collective-permute-done((f32[128,512]{1,0:T(8,128)S(1)}, f32[128,512]{1,0:T(8,128)S(1)}, u32[]{:S(2)}, u32[]{:S(2)}) %collective-permute-start.4) | collective-permute-done | bytes 262176 | tf_op jit(solution)/shard_map/ppermute | solution.py:129
  12.1 3.4 %collective-permute-start.6 = (f32[128,512]{1,0:T(8,128)S(1)}, f32[128,512]{1,0:T(8,128)S(1)}, u32[]{:S(2)}, u32[]{:S(2)}) collective-permute-start(f32[128,512]{1,0:T(8,128)S(1)} %collective-permute-done.4.first), channel_id=1, source_target_pairs={{0,2},{1,5},{2,0},{3,7},{4,6},{5,1},{6,4},{7,3},{8,12},{9,11},{10,... | collective-permute-start | bytes 786440 | tf_op jit(solution)/shard_map/ppermute | solution.py:129
  15.6 0.0 collective-permute-done.5.second
  15.6 4.1 %collective-permute-done.6.third = f32[128,512]{1,0:T(8,128)S(1)} collective-permute-done((f32[128,512]{1,0:T(8,128)S(1)}, f32[128,512]{1,0:T(8,128)S(1)}, u32[]{:S(2)}, u32[]{:S(2)}) %collective-permute-start.6) | collective-permute-done | bytes 262176 | tf_op jit(solution)/shard_map/ppermute | solution.py:129
  19.6 0.0 collective-permute-done.7.factor_other
  19.6 1.1 %shard_map.60 = (f32[512,512]{1,0:T(8,128)S(1)}, f32[512,512]{1,0:T(8,128)S(1)}) custom-call(f32[128,512]{1,0:T(8,128)S(1)} %copy-done.2, f32[128,512]{1,0:T(8,128)S(1)} %collective-permute-done.4.first, f32[128,512]{1,0:T(8,128)S(1)} %collective-permute-done.5.second, f32[128,512]{1,0:T(8,128)S(1)} %collective-permute-done.6.third, ...), custom_call_target="tpu_custom_call" | custom-call | flops 268435456 | bytes 5242880 | tf_op jit(solution)/shard_map/pallas_call | solution.py:107
  20.8 3.5 %collective-permute-start.8 = (f32[512,512]{1,0:T(8,128)S(1)}, f32[512,512]{1,0:T(8,128)S(1)}, u32[]{:S(2)}, u32[]{:S(2)}) collective-permute-start(f32[512,512]{1,0:T(8,128)S(1)} %get-tuple-element.9), channel_id=1, source_target_pairs={{1,0},{3,2},{5,4},{7,6},{8,9},{10,11},{12,13},{14,15},{17,16},{19,... | collective-permute-start | bytes 3145736 | tf_op jit(solution)/shard_map/ppermute | solution.py:129
  24.3 1.3 %collective-permute-start.2 = (f32[128,512]{1,0:T(8,128)S(1)}, f32[128,512]{1,0:T(8,128)S(1)}, u32[]{:S(2)}, u32[]{:S(2)}) collective-permute-start(f32[128,512]{1,0:T(8,128)S(1)} %copy-done.2), channel_id=1, source_target_pairs={{0,12},{2,14},{4,8},{6,10},{9,5},{11,7},{13,1},{15,3},{16,28},{18,... | collective-permute-start | bytes 786440 | tf_op jit(solution)/shard_map/ppermute | solution.py:129
  25.6 1.3 %collective-permute-start = (f32[128,512]{1,0:T(8,128)S(1)}, f32[128,512]{1,0:T(8,128)S(1)}, u32[]{:S(2)}, u32[]{:S(2)}) collective-permute-start(f32[128,512]{1,0:T(8,128)S(1)} %copy-done.2), channel_id=1, source_target_pairs={{0,8},{2,10},{4,12},{6,14},{9,1},{11,3},{13,5},{15,7},{16,24},{18,... | collective-permute-start | bytes 786440 | tf_op jit(solution)/shard_map/ppermute | solution.py:129
  26.9 6.4 %collective-permute-done.2.far_z = f32[128,512]{1,0:T(8,128)S(1)} collective-permute-done((f32[128,512]{1,0:T(8,128)S(1)}, f32[128,512]{1,0:T(8,128)S(1)}, u32[]{:S(2)}, u32[]{:S(2)}) %collective-permute-start.2) | collective-permute-done | bytes 262176 | tf_op jit(solution)/shard_map/ppermute | solution.py:129
  33.3 3.6 %collective-permute-start.3 = (f32[128,512]{1,0:T(8,128)S(1)}, f32[128,512]{1,0:T(8,128)S(1)}, u32[]{:S(2)}, u32[]{:S(2)}) collective-permute-start(f32[128,512]{1,0:T(8,128)S(1)} %collective-permute-done.2.far_z), channel_id=1, source_target_pairs={{1,3},{3,1},{5,7},{7,5},{8,10},{10,8},{12,14},{14,12},{17,19},{19,... | collective-permute-start | bytes 786440 | tf_op jit(solution)/shard_map/ppermute | solution.py:129
  36.9 4.3 %collective-permute-done.near_z = f32[128,512]{1,0:T(8,128)S(1)} collective-permute-done((f32[128,512]{1,0:T(8,128)S(1)}, f32[128,512]{1,0:T(8,128)S(1)}, u32[]{:S(2)}, u32[]{:S(2)}) %collective-permute-start) | collective-permute-done | bytes 262176 | tf_op jit(solution)/shard_map/ppermute | solution.py:129
  41.2 3.4 %collective-permute-start.1 = (f32[128,512]{1,0:T(8,128)S(1)}, f32[128,512]{1,0:T(8,128)S(1)}, u32[]{:S(2)}, u32[]{:S(2)}) collective-permute-start(f32[128,512]{1,0:T(8,128)S(1)} %collective-permute-done.near_z), channel_id=1, source_target_pairs={{1,3},{3,1},{5,7},{7,5},{8,10},{10,8},{12,14},{14,12},{17,19},{19,... | collective-permute-start | bytes 786440 | tf_op jit(solution)/shard_map/ppermute | solution.py:129
  44.6 0.0 collective-permute-done.3.far_x
  44.7 3.7 %collective-permute-done.1.near_x = f32[128,512]{1,0:T(8,128)S(1)} collective-permute-done((f32[128,512]{1,0:T(8,128)S(1)}, f32[128,512]{1,0:T(8,128)S(1)}, u32[]{:S(2)}, u32[]{:S(2)}) %collective-permute-start.1) | collective-permute-done | bytes 262176 | tf_op jit(solution)/shard_map/ppermute | solution.py:129
  48.4 0.0 collective-permute-done.8.beside
  48.4 2.2 %shard_map.61 = (f32[512,512]{1,0:T(8,128)}, f32[2,256,256]{2,1,0:T(8,128)S(1)}) custom-call(f32[128,512]{1,0:T(8,128)S(1)} %collective-permute-done.near_z, f32[128,512]{1,0:T(8,128)S(1)} %collective-permute-done.1.near_x, f32[128,512]{1,0:T(8,128)S(1)} %collective-permute-done.2.far_z, f32[128,512]{1,0:T(8,128)S(1)} %collective-permute-done.3.far_x, ...), custom_call_target="tpu_custom_call" | custom-call | flops 268435456 | bytes 6815744 | tf_op jit(solution)/shard_map/pallas_call | solution.py:107
  50.6 0.0 collective-permute-start.9
  50.6 1.9 %collective-permute-done.9 = f32[2,256,256]{2,1,0:T(8,128)S(1)} collective-permute-done((f32[2,256,256]{2,1,0:T(8,128)S(1)}, f32[2,256,256]{2,1,0:T(8,128)S(1)}, u32[]{:S(2)}, u32[]{:S(2)}) %collective-permute-start.9) | collective-permute-done | bytes 524320 | tf_op jit(solution)/shard_map/ppermute | solution.py:129
  52.5 0.9 %add_subtract_fusion = f32[2,256,256]{2,1,0:T(8,128)} fusion(f32[2,256,256]{2,1,0:T(8,128)S(1)} %get-tuple-element.12, f32[2,256,256]{2,1,0:T(8,128)S(1)} %get-tuple-element.13, f32[2,256,256]{2,1,0:T(8,128)S(1)} %collective-permute-done.9), kind=kLoop, calls=%fused_computation | loop fusion | flops 262144 | bytes 2097152 | tf_op jit(solution)/shard_map/sub | solution.py:180
Async XLA Ops:
  0.6 1.2 %copy-start = (f32[512,512]{1,0:T(8,128)S(1)}, f32[512,512]{1,0:T(8,128)}, u32[]{:S(2)}) copy-start(f32[512,512]{1,0:T(8,128)} %panel.1) | copy-start | bytes 3145732
  1.9 1.0 %copy-start.1 = (f32[2,256,256]{2,1,0:T(8,128)S(1)}, f32[2,256,256]{2,1,0:T(8,128)}, u32[]{:S(2)}) copy-start(f32[2,256,256]{2,1,0:T(8,128)} %diag_inv.1) | copy-start | bytes 1572868
  2.9 0.7 %copy-start.3 = (s32[2,8]{1,0:T(2,128)S(1)}, s32[2,8]{1,0:T(2,128)}, u32[]{:S(2)}) copy-start(s32[2,8]{1,0:T(2,128)} %pattern.1) | copy-start | bytes 196
  3.6 1.5 %copy-start.2 = (f32[128,512]{1,0:T(8,128)S(1)}, f32[128,512]{1,0:T(8,128)}, u32[]{:S(2)}) copy-start(f32[128,512]{1,0:T(8,128)} %own.1) | copy-start | bytes 786436
  4.9 14.7 %collective-permute-start.7 = (f32[512,512]{1,0:T(8,128)S(1)}, f32[512,512]{1,0:T(8,128)S(1)}, u32[]{:S(2)}, u32[]{:S(2)}) collective-permute-start(f32[512,512]{1,0:T(8,128)S(1)} %get-tuple-element.8.factor), channel_id=1, source_target_pairs={{0,1},{1,0},{2,3},{3,2},{4,5},{5,4},{6,7},{7,6},{8,9},{9,8},{10,11... | collective-permute-start | bytes 3145736 | tf_op jit(solution)/shard_map/ppermute | solution.py:129
  5.1 7.1 %collective-permute-start.4 = (f32[128,512]{1,0:T(8,128)S(1)}, f32[128,512]{1,0:T(8,128)S(1)}, u32[]{:S(2)}, u32[]{:S(2)}) collective-permute-start(f32[128,512]{1,0:T(8,128)S(1)} %copy-done.2), channel_id=1, source_target_pairs={{0,4},{1,3},{2,6},{3,1},{4,0},{5,7},{6,2},{7,5},{8,10},{9,13},{10,... | collective-permute-start | bytes 786440 | tf_op jit(solution)/shard_map/ppermute | solution.py:129
  7.7 7.9 %collective-permute-start.5 = (f32[128,512]{1,0:T(8,128)S(1)}, f32[128,512]{1,0:T(8,128)S(1)}, u32[]{:S(2)}, u32[]{:S(2)}) collective-permute-start(f32[128,512]{1,0:T(8,128)S(1)} %copy-done.2), channel_id=1, source_target_pairs={{0,2},{1,5},{2,0},{3,7},{4,6},{5,1},{6,4},{7,3},{8,12},{9,11},{10,... | collective-permute-start | bytes 786440 | tf_op jit(solution)/shard_map/ppermute | solution.py:129
  12.1 7.5 %collective-permute-start.6 = (f32[128,512]{1,0:T(8,128)S(1)}, f32[128,512]{1,0:T(8,128)S(1)}, u32[]{:S(2)}, u32[]{:S(2)}) collective-permute-start(f32[128,512]{1,0:T(8,128)S(1)} %collective-permute-done.4.first), channel_id=1, source_target_pairs={{0,2},{1,5},{2,0},{3,7},{4,6},{5,1},{6,4},{7,3},{8,12},{9,11},{10,... | collective-permute-start | bytes 786440 | tf_op jit(solution)/shard_map/ppermute | solution.py:129
  20.8 27.6 %collective-permute-start.8 = (f32[512,512]{1,0:T(8,128)S(1)}, f32[512,512]{1,0:T(8,128)S(1)}, u32[]{:S(2)}, u32[]{:S(2)}) collective-permute-start(f32[512,512]{1,0:T(8,128)S(1)} %get-tuple-element.9), channel_id=1, source_target_pairs={{1,0},{3,2},{5,4},{7,6},{8,9},{10,11},{12,13},{14,15},{17,16},{19,... | collective-permute-start | bytes 3145736 | tf_op jit(solution)/shard_map/ppermute | solution.py:129
  24.3 9.0 %collective-permute-start.2 = (f32[128,512]{1,0:T(8,128)S(1)}, f32[128,512]{1,0:T(8,128)S(1)}, u32[]{:S(2)}, u32[]{:S(2)}) collective-permute-start(f32[128,512]{1,0:T(8,128)S(1)} %copy-done.2), channel_id=1, source_target_pairs={{0,12},{2,14},{4,8},{6,10},{9,5},{11,7},{13,1},{15,3},{16,28},{18,... | collective-permute-start | bytes 786440 | tf_op jit(solution)/shard_map/ppermute | solution.py:129
  25.6 15.6 %collective-permute-start = (f32[128,512]{1,0:T(8,128)S(1)}, f32[128,512]{1,0:T(8,128)S(1)}, u32[]{:S(2)}, u32[]{:S(2)}) collective-permute-start(f32[128,512]{1,0:T(8,128)S(1)} %copy-done.2), channel_id=1, source_target_pairs={{0,8},{2,10},{4,12},{6,14},{9,1},{11,3},{13,5},{15,7},{16,24},{18,... | collective-permute-start | bytes 786440 | tf_op jit(solution)/shard_map/ppermute | solution.py:129
  33.3 11.4 %collective-permute-start.3 = (f32[128,512]{1,0:T(8,128)S(1)}, f32[128,512]{1,0:T(8,128)S(1)}, u32[]{:S(2)}, u32[]{:S(2)}) collective-permute-start(f32[128,512]{1,0:T(8,128)S(1)} %collective-permute-done.2.far_z), channel_id=1, source_target_pairs={{1,3},{3,1},{5,7},{7,5},{8,10},{10,8},{12,14},{14,12},{17,19},{19,... | collective-permute-start | bytes 786440 | tf_op jit(solution)/shard_map/ppermute | solution.py:129
  41.2 7.2 %collective-permute-start.1 = (f32[128,512]{1,0:T(8,128)S(1)}, f32[128,512]{1,0:T(8,128)S(1)}, u32[]{:S(2)}, u32[]{:S(2)}) collective-permute-start(f32[128,512]{1,0:T(8,128)S(1)} %collective-permute-done.near_z), channel_id=1, source_target_pairs={{1,3},{3,1},{5,7},{7,5},{8,10},{10,8},{12,14},{14,12},{17,19},{19,... | collective-permute-start | bytes 786440 | tf_op jit(solution)/shard_map/ppermute | solution.py:129
  50.6 1.9 %collective-permute-start.9 = (f32[2,256,256]{2,1,0:T(8,128)S(1)}, f32[2,256,256]{2,1,0:T(8,128)S(1)}, u32[]{:S(2)}, u32[]{:S(2)}) collective-permute-start(f32[2,256,256]{2,1,0:T(8,128)S(1)} %get-tuple-element.13), channel_id=1, source_target_pairs={{0,1},{1,0},{2,3},{3,2},{4,5},{5,4},{6,7},{7,6},{8,9},{9,8},{10,11... | collective-permute-start | bytes 1572872 | tf_op jit(solution)/shard_map/ppermute | solution.py:129

commit v2 on v1

--- a/solution.py
+++ b/solution.py
@@ -48,50 +48,114 @@
         own_part[j] = product(inverse, inverse, FIRST)
 
 
-def half_kernel(own, first, second, third, factor, factor_other, gathered, partial):
+def own_place():
     prow = lax.axis_index("prow")
-    place = lax.rem(prow, 4)
-    diagonal = lax.div(prow, 4) == lax.axis_index("pcol")
-    rows = own.shape[0]
-    x_place = place + 1 - 2 * lax.rem(place, 2)
-    z_place = lax.rem(place + 2, 4)
-    both = lax.rem(x_place + 2, 4)
-    for value, at in (
-        (own, place),
-        (first, jnp.where(diagonal, z_place, x_place)),
-        (second, jnp.where(diagonal, x_place, z_place)),
-        (third, both),
-    ):
-        gathered[pl.ds(pl.multiple_of(at * rows, rows), rows), :] = value[...]
-
-    @pl.when(diagonal)
-    def _():
-        partial[...] = product(split(gathered[...]), split(factor[...]), FIRST)
-
-    @pl.when(jnp.logical_not(diagonal))
-    def _():
-        partial[...] = product(split(gathered[...]), split(factor_other[...]), FIRST)
-
-
-def panel_kernel(near_z, near_x, far_z, far_x, beside, partial, factor, factor_other, sigma, cross, block):
-    prow = lax.axis_index("prow")
-    place = lax.rem(prow, 4)
-    diagonal = lax.div(prow, 4) == lax.axis_index("pcol")
-    rows = near_z.shape[0]
-    x_place = place + 1 - 2 * lax.rem(place, 2)
-    z_place = lax.rem(place + 2, 4)
-    both = lax.rem(x_place + 2, 4)
+    return lax.rem(prow, 4), lax.div(prow, 4) == lax.axis_index("pcol")
+
+
+def places(place):
+    beside = place + 1 - 2 * lax.rem(place, 2)
+    return beside, lax.rem(place + 2, 4), lax.rem(beside + 2, 4)
+
+
+def at(place, block):
+    return pl.ds(pl.multiple_of(place * block, block), block)
+
+
+def pieces_kernel(own, first, second):
+    place, diagonal = own_place()
+    block = own.shape[0]
+    half = block // 2
+
+    @pl.when(diagonal)
+    def _():
+        opposite = at(lax.rem(place + 2, 4), block)
+        for piece in (first, second):
+            piece[pl.ds(0, block), :] = own[:, at(place, block)]
+            piece[pl.ds(block, block), :] = own[:, at(lax.rem(place + 1, 4), block)]
+
+        @pl.when(place < 2)
+        def _():
+            for piece in (first, second):
+                piece[pl.ds(2 * block, half), :] = own[pl.ds(0, half), opposite]
+
+        @pl.when(place >= 2)
+        def _():
+            turned = own[:, opposite].T
+            for piece in (first, second):
+                piece[pl.ds(2 * block, half), :] = turned[half:]
+
+    @pl.when(jnp.logical_not(diagonal))
+    def _():
+        for n, piece in enumerate((first, second)):
+            for b in range(2):
+                piece[pl.ds(b * block, block), :] = own[:, pl.ds((2 * n + b) * block, block)]
+            piece[pl.ds(2 * block, half), :] = jnp.zeros((half, block), jnp.float32)
+
+
+def symmetric(quadrant, pieces):
+    block = quadrant.shape[0] // 4
+    half = block // 2
+    for piece, place in pieces:
+        rows = at(place, block)
+        quadrant[rows, at(place, block)] = piece[pl.ds(0, block), :]
+        quadrant[rows, at(lax.rem(place + 1, 4), block)] = piece[pl.ds(block, block), :]
+        low = lax.rem(place, 2)
+        quadrant[
+            pl.ds(pl.multiple_of(low * block + lax.div(place, 2) * half, half), half), at(low + 2, block)
+        ] = piece[pl.ds(2 * block, half), :]
+    for row, column in ((0, 1), (1, 2), (2, 3), (3, 0), (0, 2), (1, 3)):
+        rows, columns = pl.ds(row * block, block), pl.ds(column * block, block)
+        quadrant[columns, rows] = quadrant[rows, columns].T
+
+
+def quadrant_kernel(mine_a, mine_b, got1, got2, got3, got4, got5, got6, got7, quadrant):
+    place, diagonal = own_place()
+    beside, over, across = places(place)
+    block = quadrant.shape[0] // 4
+
+    @pl.when(diagonal)
+    def _():
+        symmetric(quadrant, ((got1, place), (got2, over), (got5, beside), (got7, across)))
+
+    @pl.when(jnp.logical_not(diagonal))
+    def _():
+        for where, halves in (
+            (place, (mine_a, mine_b)),
+            (beside, (got1, got4)),
+            (over, (got2, got3)),
+            (across, (got5, got6)),
+        ):
+            for n, piece in enumerate(halves):
+                for b in range(2):
+                    quadrant[at(where, block), pl.ds((2 * n + b) * block, block)] = piece[pl.ds(b * block, block), :]
+
+
+def near_kernel(mine, got3, got4, got6, quadrant, factor, factor_other, partial, own_quadrant):
+    place, diagonal = own_place()
+    beside, over, across = places(place)
+
+    @pl.when(diagonal)
+    def _():
+        symmetric(own_quadrant, ((mine, place), (got3, beside), (got4, over), (got6, across)))
+        partial[...] = product(split(own_quadrant[...]), split(factor[...]), PLAIN)
+
+    @pl.when(jnp.logical_not(diagonal))
+    def _():
+        partial[...] = product(split(quadrant[...]), split(factor_other[...]), FIRST)
+
+
+def panel_kernel(quadrant, partial, factor, factor_other, sigma, cross):
+    _, diagonal = own_place()
     own_factor = split(factor[...])
 
     @pl.when(diagonal)
     def _():
-        sigma[...] = -(partial[...] + product(split(beside[...]), split(factor_other[...]), PLAIN))
-
-    @pl.when(jnp.logical_not(diagonal))
-    def _():
-        for value, at in ((near_z, place), (near_x, x_place), (far_z, z_place), (far_x, both)):
-            block[pl.ds(pl.multiple_of(at * rows, rows), rows), :] = value[...]
-        sigma[...] = -(partial[...] + product(split(block[...]), own_factor, PLAIN))
+        sigma[...] = -(partial[...] + product(split(quadrant[...]), split(factor_other[...]), PLAIN))
+
+    @pl.when(jnp.logical_not(diagonal))
+    def _():
+        sigma[...] = -(partial[...] + product(split(quadrant[...]), own_factor, PLAIN))
 
     width = cross.shape[1]
     sigma_split = split(sigma[...])
@@ -115,28 +179,37 @@
     )(*args)
 
 
-def permute(value, mesh, diagonal_step, other_step, swap=False):
+def permute(value, mesh, diagonal_step, other_step=None):
     cfgs, prows, cores = (mesh.shape[axis] for axis in AXES)
     pairs = []
     for c in range(cfgs):
         for p in range(prows):
             for k in range(cores):
-                step = diagonal_step if (p >= prows // 2) == (k == 1) else other_step
-                if step is None:
-                    continue
-                to = 1 - k if swap else k
-                pairs.append(((c * prows + p) * cores + k, (c * prows + (p ^ step)) * cores + to))
+                to = p ^ (diagonal_step if p // 4 == k else other_step)
+                pairs.append(((c * prows + p) * cores + k, (c * prows + to) * cores + (k ^ (p // 4) ^ (to // 4))))
     return lax.ppermute(value, AXES, pairs)
+
+
+def exchange(value, mesh):
+    cfgs, prows, cores = (mesh.shape[axis] for axis in AXES)
+    return lax.ppermute(value, AXES, [(d, d ^ 1) for d in range(cfgs * prows * cores)])
 
 
 def local_eight(mesh, sigma_top, panel_l, diag_inv, pattern):
     f32 = jnp.float32
     half_rows, own_columns = panel_l.shape
+    block = sigma_top.shape[0]
     shape = lambda *dims: jax.ShapeDtypeStruct(dims, f32)
-    first = permute(sigma_top, mesh, 2, 1)
-    near_z = permute(sigma_top, mesh, 4, None)
-    far_z = permute(sigma_top, mesh, 6, None)
-    second = permute(sigma_top, mesh, 1, 2)
+    piece = shape(2 * block + block // 2, block)
+    mine_a, mine_b = call(pieces_kernel, [piece, piece], 1, sigma_top)
+    got1 = permute(mine_a, mesh, 4, 1)
+    got2 = permute(mine_a, mesh, 6, 2)
+    got3 = permute(mine_b, mesh, 1, 2)
+    got4 = permute(mine_b, mesh, 2, 1)
+    got5 = permute(got1, mesh, 1, 2)
+    got6 = permute(got4, mesh, 1, 2)
+    got7 = permute(got2, mesh, 1, 1)
+
     factor, own_part = call(
         factor_kernel,
         [shape(half_rows, own_columns), shape(*diag_inv.shape)],
@@ -146,37 +219,28 @@
         diag_inv,
         smem=1,
     )
-    factor_other = permute(factor, mesh, 0, 0, swap=True)
-    third = permute(first, mesh, 1, 2)
-    near_x = permute(near_z, mesh, None, 1)
-    far_x = permute(far_z, mesh, None, 1)
-    gathered, partial = call(
-        half_kernel,
-        [shape(half_rows, sigma_top.shape[1]), shape(half_rows, own_columns)],
+    factor_other = exchange(factor, mesh)
+    (quadrant,) = call(
+        quadrant_kernel,
+        [shape(half_rows, half_rows)],
+        1,
+        mine_a, mine_b, got1, got2, got3, got4, got5, got6, got7,
+    )
+    quadrant_other = exchange(quadrant, mesh)
+    (partial,) = call(
+        near_kernel,
+        [shape(half_rows, own_columns)],
         2 * half_rows * half_rows * own_columns,
-        sigma_top,
-        first,
-        second,
-        third,
-        factor,
-        factor_other,
-    )
-    beside = permute(gathered, mesh, None, 0, swap=True)
+        mine_a, got3, got4, got6, quadrant, factor, factor_other,
+        scratch=[pltpu.VMEM((half_rows, half_rows), f32)],
+    )
     sigma, cross = call(
         panel_kernel,
         [shape(half_rows, own_columns), shape(*diag_inv.shape)],
         2 * half_rows * half_rows * own_columns,
-        near_z,
-        near_x,
-        far_z,
-        far_x,
-        beside,
-        partial,
-        factor,
-        factor_other,
-        scratch=[pltpu.VMEM((half_rows, half_rows), f32)],
-    )
-    cross_other = permute(cross, mesh, 0, 0, swap=True)
+        quadrant_other, partial, factor, factor_other,
+    )
+    cross_other = exchange(cross, mesh)
     return sigma, own_part - (cross + cross_other)
 
 

time: 53.8 us -> 30.7 us (0.57)
  waiting for transfers between devices: 23.5 us -> 5.75 us
  starting transfers between devices: 20.7 us -> 14.9 us
    ppermute x10 -> x7, waiting for transfers between devices: 23.5 us -> 1.89 us  [permute(): return lax.ppermute(value, AXES, pairs)]
    ppermute x10 -> x7, starting transfers between devices: 20.7 us -> 8.42 us  [permute(): return lax.ppermute(value, AXES, pairs)]
    ppermute x0 -> x3, starting transfers between devices: none -> 6.51 us  [exchange(): lax.ppermute(value, AXES, [(d, d ^ 1) for d in range(cfgs * prows * cores)])]
    ppermute x0 -> x3, waiting for transfers between devices: none -> 3.86 us  [exchange(): lax.ppermute(value, AXES, [(d, d ^ 1) for d in range(cfgs * prows * cores)])]
    pallas_call x3 -> x5, Pallas kernels: 4.7 us -> 4.72 us  [call(): pl.pallas_call(kernel, out_shape=out_shapes, in_specs=[SMEM] * smem + [VM...]
  transfers between devices with their start and end apart: 10 -> 10, of which waited for: 6 -> 6; matrix products, arithmetic and copies ran while one was open for 0% -> 0% of each run, Pallas kernels for 0% -> 8%
where the time goes in v2:
time: 30.7 us; the launch traced here: 30.2 us
  starting transfers between devices  14.9 us (49%)
  waiting for transfers between devices  5.75 us (19%)
  Pallas kernels  4.72 us (15%)
  local copies, waits for them, and re-layouts  3.22 us (10%)
  other arithmetic  0.89 us (3%)
  between operations  0.69 us (2%)
    ppermute x7, starting transfers between devices, permute(): return lax.ppermute(value, AXES, pairs)  8.42 us
    ppermute x3, starting transfers between devices, exchange(): lax.ppermute(value, AXES, [(d, d ^ 1) for d in range(cfgs * prows * cores)])  6.51 us
    pallas_call x5, Pallas kernels, call(): pl.pallas_call(kernel, out_shape=out_shapes, in_specs=[SMEM] * smem + [VM...  4.72 us
    ppermute x3, waiting for transfers between devices, exchange(): lax.ppermute(value, AXES, [(d, d ^ 1) for d in range(cfgs * prows * cores)])  3.86 us
    unnamed x8, local copies, waits for them, and re-layouts  3.22 us
    ppermute x7, waiting for transfers between devices, permute(): return lax.ppermute(value, AXES, pairs)  1.89 us
    sub x1, other arithmetic, local_eight(): return (sigma, own_part - (cross + cross_other))  0.89 us
  transfers between devices with their start and end apart: 10, of which 6 were waited for; matrix products, arithmetic and copies ran while one was open for 0% of the time, Pallas kernels for 8%

profile of v2, /device:TPU:1, one launch (start us, length us, event | category | flops | bytes accessed | tf_op | source)
XLA Modules:
  0.0 30.2 jit_solution(5416732957694190671)
XLA Ops:
  0.6 0.0 copy-start.2
  0.6 0.9 %copy-done.2 = f32[128,512]{1,0:T(8,128)S(1)} copy-done((f32[128,512]{1,0:T(8,128)S(1)}, f32[128,512]{1,0:T(8,128)}, u32[]{:S(2)}) %copy-start.2) | copy-done | bytes 262168
  1.6 0.0 copy-start.3
  1.6 2.1 %collective-permute-start.3 = (f32[320,128]{1,0:T(8,128)S(1)}, f32[320,128]{1,0:T(8,128)S(1)}, u32[]{:S(2)}, u32[]{:S(2)}) collective-permute-start(f32[320,128]{1,0:T(8,128)S(1)} %get-tuple-element.9.mine_b), channel_id=1, source_target_pairs={{0,4},{1,3},{2,6},{3,1},{4,0},{5,7},{6,2},{7,5},{8,10},{9,13},{10,... | collective-permute-start | bytes 491528 | tf_op jit(solution)/shard_map/ppermute | solution.py:190
  3.7 0.1 collective-permute-start
  3.8 1.5 %collective-permute-start.1 = (f32[320,128]{1,0:T(8,128)S(1)}, f32[320,128]{1,0:T(8,128)S(1)}, u32[]{:S(2)}, u32[]{:S(2)}) collective-permute-start(f32[320,128]{1,0:T(8,128)S(1)} %get-tuple-element.8.mine_a.mine), channel_id=1, source_target_pairs={{0,13},{1,5},{2,15},{3,7},{4,9},{5,1},{6,11},{7,3},{8,12},{9,4},{1... | collective-permute-start | bytes 491528 | tf_op jit(solution)/shard_map/ppermute | solution.py:190
  5.3 0.0 collective-permute-start.2
  5.3 1.4 %collective-permute-done.3.got4 = f32[320,128]{1,0:T(8,128)S(1)} collective-permute-done((f32[320,128]{1,0:T(8,128)S(1)}, f32[320,128]{1,0:T(8,128)S(1)}, u32[]{:S(2)}, u32[]{:S(2)}) %collective-permute-start.3) | collective-permute-done | bytes 163872 | tf_op jit(solution)/shard_map/ppermute | solution.py:190
  6.7 1.5 %collective-permute-start.5 = (f32[320,128]{1,0:T(8,128)S(1)}, f32[320,128]{1,0:T(8,128)S(1)}, u32[]{:S(2)}, u32[]{:S(2)}) collective-permute-start(f32[320,128]{1,0:T(8,128)S(1)} %collective-permute-done.3.got4), channel_id=1, source_target_pairs={{0,2},{1,5},{2,0},{3,7},{4,6},{5,1},{6,4},{7,3},{8,12},{9,11},{10,... | collective-permute-start | bytes 491528 | tf_op jit(solution)/shard_map/ppermute | solution.py:190
  8.3 0.2 collective-permute-done.got1
  8.5 1.5 %collective-permute-start.4 = (f32[320,128]{1,0:T(8,128)S(1)}, f32[320,128]{1,0:T(8,128)S(1)}, u32[]{:S(2)}, u32[]{:S(2)}) collective-permute-start(f32[320,128]{1,0:T(8,128)S(1)} %collective-permute-done.got1), channel_id=1, source_target_pairs={{0,2},{1,5},{2,0},{3,7},{4,6},{5,1},{6,4},{7,3},{8,12},{9,11},{10,... | collective-permute-start | bytes 491528 | tf_op jit(solution)/shard_map/ppermute | solution.py:190
  10.0 0.3 collective-permute-done.1.got2
  10.3 1.6 %collective-permute-start.6 = (f32[320,128]{1,0:T(8,128)S(1)}, f32[320,128]{1,0:T(8,128)S(1)}, u32[]{:S(2)}, u32[]{:S(2)}) collective-permute-start(f32[320,128]{1,0:T(8,128)S(1)} %collective-permute-done.1.got2), channel_id=1, source_target_pairs={{0,2},{1,3},{2,0},{3,1},{4,6},{5,7},{6,4},{7,5},{8,10},{9,11},{10,... | collective-permute-start | bytes 491528 | tf_op jit(solution)/shard_map/ppermute | solution.py:190
  11.9 0.0 copy-done.3
  11.9 0.0 copy-start
  11.9 1.2 %copy-done = f32[512,512]{1,0:T(8,128)S(1)} copy-done((f32[512,512]{1,0:T(8,128)S(1)}, f32[512,512]{1,0:T(8,128)}, u32[]{:S(2)}) %copy-start) | copy-done | bytes 1048600
  13.1 1.0 %copy-done.1 = f32[2,256,256]{2,1,0:T(8,128)S(1)} copy-done((f32[2,256,256]{2,1,0:T(8,128)S(1)}, f32[2,256,256]{2,1,0:T(8,128)}, u32[]{:S(2)}) %copy-start.1) | copy-done | bytes 524312
  14.2 1.4 %shard_map.61 = (f32[512,512]{1,0:T(8,128)S(1)}, f32[2,256,256]{2,1,0:T(8,128)S(1)}) custom-call(s32[2,8]{1,0:T(2,128)S(1)} %copy-done.3, f32[512,512]{1,0:T(8,128)S(1)} %copy-done, f32[2,256,256]{2,1,0:T(8,128)S(1)} %copy-done.1), custom_call_target="tpu_custom_call" | custom-call | flops 134217728 | bytes 3145792 | tf_op jit(solution)/shard_map/pallas_call | solution.py:171
  15.6 5.9 %collective-permute-start.8 = (f32[512,512]{1,0:T(8,128)S(1)}, f32[512,512]{1,0:T(8,128)S(1)}, u32[]{:S(2)}, u32[]{:S(2)}) collective-permute-start(f32[512,512]{1,0:T(8,128)S(1)} %get-tuple-element.10.factor), channel_id=1, source_target_pairs={{0,1},{1,0},{2,3},{3,2},{4,5},{5,4},{6,7},{7,6},{8,9},{9,8},{10,11... | collective-permute-start | bytes 3145736 | tf_op jit(solution)/shard_map/ppermute | solution.py:195
  21.4 0.0 collective-permute-done.2.got3
  21.4 0.0 collective-permute-done.5.got6
  21.4 0.0 collective-permute-done.4.got5
  21.4 0.0 collective-permute-done.6.got7
  21.4 0.1 shard_map.60.quadrant
  21.6 0.3 collective-permute-start.7
  21.9 1.8 %collective-permute-done.8.factor_other = f32[512,512]{1,0:T(8,128)S(1)} collective-permute-done((f32[512,512]{1,0:T(8,128)S(1)}, f32[512,512]{1,0:T(8,128)S(1)}, u32[]{:S(2)}, u32[]{:S(2)}) %collective-permute-start.8) | collective-permute-done | bytes 1048608 | tf_op jit(solution)/shard_map/ppermute | solution.py:195
  23.7 1.0 %shard_map.62.partial = f32[512,512]{1,0:T(8,128)S(1)} custom-call(f32[320,128]{1,0:T(8,128)S(1)} %get-tuple-element.8.mine_a.mine, f32[320,128]{1,0:T(8,128)S(1)} %collective-permute-done.2.got3, f32[320,128]{1,0:T(8,128)S(1)} %collective-permute-done.3.got4, f32[320,128]{1,0:T(8,128)S(1)} %collective-permute-done.5.got6, ...), custom_call_target="tpu_custom_call" | custom-call | flops 268435456 | bytes 4849664 | tf_op jit(solution)/shard_map/pallas_call | solution.py:171
  24.7 0.5 %collective-permute-done.7.quadrant = f32[512,512]{1,0:T(8,128)S(1)} collective-permute-done((f32[512,512]{1,0:T(8,128)S(1)}, f32[512,512]{1,0:T(8,128)S(1)}, u32[]{:S(2)}, u32[]{:S(2)}) %collective-permute-start.7) | collective-permute-done | bytes 1048608 | tf_op jit(solution)/shard_map/ppermute | solution.py:195
  25.2 2.2 %shard_map.63 = (f32[512,512]{1,0:T(8,128)}, f32[2,256,256]{2,1,0:T(8,128)S(1)}) custom-call(f32[512,512]{1,0:T(8,128)S(1)} %collective-permute-done.7.quadrant, f32[512,512]{1,0:T(8,128)S(1)} %shard_map.62.partial, f32[512,512]{1,0:T(8,128)S(1)} %get-tuple-element.10.factor, f32[512,512]{1,0:T(8,128)S(1)} %collective-permute-done.8.factor_other), custom_call_target="tpu_custom_call" | custom-call | flops 268435456 | bytes 5767168 | tf_op jit(solution)/shard_map/pallas_call | solution.py:171
  27.4 0.4 %collective-permute-start.9 = (f32[2,256,256]{2,1,0:T(8,128)S(1)}, f32[2,256,256]{2,1,0:T(8,128)S(1)}, u32[]{:S(2)}, u32[]{:S(2)}) collective-permute-start(f32[2,256,256]{2,1,0:T(8,128)S(1)} %get-tuple-element.13), channel_id=1, source_target_pairs={{0,1},{1,0},{2,3},{3,2},{4,5},{5,4},{6,7},{7,6},{8,9},{9,8},{10,11... | collective-permute-start | bytes 1572872 | tf_op jit(solution)/shard_map/ppermute | solution.py:195
  27.8 1.5 %collective-permute-done.9 = f32[2,256,256]{2,1,0:T(8,128)S(1)} collective-permute-done((f32[2,256,256]{2,1,0:T(8,128)S(1)}, f32[2,256,256]{2,1,0:T(8,128)S(1)}, u32[]{:S(2)}, u32[]{:S(2)}) %collective-permute-start.9) | collective-permute-done | bytes 524320 | tf_op jit(solution)/shard_map/ppermute | solution.py:195
  29.3 0.9 %add_subtract_fusion = f32[2,256,256]{2,1,0:T(8,128)} fusion(f32[2,256,256]{2,1,0:T(8,128)S(1)} %get-tuple-element.12, f32[2,256,256]{2,1,0:T(8,128)S(1)} %get-tuple-element.13, f32[2,256,256]{2,1,0:T(8,128)S(1)} %collective-permute-done.9), kind=kLoop, calls=%fused_computation | loop fusion | flops 262144 | bytes 2097152 | tf_op jit(solution)/shard_map/sub | solution.py:244
  (2 shorter events, 0.0 us)
Async XLA Ops:
  0.6 1.0 %copy-start.2 = (f32[128,512]{1,0:T(8,128)S(1)}, f32[128,512]{1,0:T(8,128)}, u32[]{:S(2)}) copy-start(f32[128,512]{1,0:T(8,128)} %own.1) | copy-start | bytes 786436
  1.6 10.3 %copy-start.3 = (s32[2,8]{1,0:T(2,128)S(1)}, s32[2,8]{1,0:T(2,128)}, u32[]{:S(2)}) copy-start(s32[2,8]{1,0:T(2,128)} %pattern.1) | copy-start | bytes 196
  1.6 5.1 %collective-permute-start.3 = (f32[320,128]{1,0:T(8,128)S(1)}, f32[320,128]{1,0:T(8,128)S(1)}, u32[]{:S(2)}, u32[]{:S(2)}) collective-permute-start(f32[320,128]{1,0:T(8,128)S(1)} %get-tuple-element.9.mine_b), channel_id=1, source_target_pairs={{0,4},{1,3},{2,6},{3,1},{4,0},{5,7},{6,2},{7,5},{8,10},{9,13},{10,... | collective-permute-start | bytes 491528 | tf_op jit(solution)/shard_map/ppermute | solution.py:190
  3.7 4.8 %collective-permute-start = (f32[320,128]{1,0:T(8,128)S(1)}, f32[320,128]{1,0:T(8,128)S(1)}, u32[]{:S(2)}, u32[]{:S(2)}) collective-permute-start(f32[320,128]{1,0:T(8,128)S(1)} %get-tuple-element.8.mine_a.mine), channel_id=1, source_target_pairs={{0,9},{1,3},{2,11},{3,1},{4,13},{5,7},{6,15},{7,5},{8,10},{9,0},{1... | collective-permute-start | bytes 491528 | tf_op jit(solution)/shard_map/ppermute | solution.py:190
  3.8 6.5 %collective-permute-start.1 = (f32[320,128]{1,0:T(8,128)S(1)}, f32[320,128]{1,0:T(8,128)S(1)}, u32[]{:S(2)}, u32[]{:S(2)}) collective-permute-start(f32[320,128]{1,0:T(8,128)S(1)} %get-tuple-element.8.mine_a.mine), channel_id=1, source_target_pairs={{0,13},{1,5},{2,15},{3,7},{4,9},{5,1},{6,11},{7,3},{8,12},{9,4},{1... | collective-permute-start | bytes 491528 | tf_op jit(solution)/shard_map/ppermute | solution.py:190
  5.3 16.1 %collective-permute-start.2 = (f32[320,128]{1,0:T(8,128)S(1)}, f32[320,128]{1,0:T(8,128)S(1)}, u32[]{:S(2)}, u32[]{:S(2)}) collective-permute-start(f32[320,128]{1,0:T(8,128)S(1)} %get-tuple-element.9.mine_b), channel_id=1, source_target_pairs={{0,2},{1,5},{2,0},{3,7},{4,6},{5,1},{6,4},{7,3},{8,12},{9,11},{10,... | collective-permute-start | bytes 491528 | tf_op jit(solution)/shard_map/ppermute | solution.py:190
  6.7 14.7 %collective-permute-start.5 = (f32[320,128]{1,0:T(8,128)S(1)}, f32[320,128]{1,0:T(8,128)S(1)}, u32[]{:S(2)}, u32[]{:S(2)}) collective-permute-start(f32[320,128]{1,0:T(8,128)S(1)} %collective-permute-done.3.got4), channel_id=1, source_target_pairs={{0,2},{1,5},{2,0},{3,7},{4,6},{5,1},{6,4},{7,3},{8,12},{9,11},{10,... | collective-permute-start | bytes 491528 | tf_op jit(solution)/shard_map/ppermute | solution.py:190
  8.5 12.9 %collective-permute-start.4 = (f32[320,128]{1,0:T(8,128)S(1)}, f32[320,128]{1,0:T(8,128)S(1)}, u32[]{:S(2)}, u32[]{:S(2)}) collective-permute-start(f32[320,128]{1,0:T(8,128)S(1)} %collective-permute-done.got1), channel_id=1, source_target_pairs={{0,2},{1,5},{2,0},{3,7},{4,6},{5,1},{6,4},{7,3},{8,12},{9,11},{10,... | collective-permute-start | bytes 491528 | tf_op jit(solution)/shard_map/ppermute | solution.py:190
  10.3 11.1 %collective-permute-start.6 = (f32[320,128]{1,0:T(8,128)S(1)}, f32[320,128]{1,0:T(8,128)S(1)}, u32[]{:S(2)}, u32[]{:S(2)}) collective-permute-start(f32[320,128]{1,0:T(8,128)S(1)} %collective-permute-done.1.got2), channel_id=1, source_target_pairs={{0,2},{1,3},{2,0},{3,1},{4,6},{5,7},{6,4},{7,5},{8,10},{9,11},{10,... | collective-permute-start | bytes 491528 | tf_op jit(solution)/shard_map/ppermute | solution.py:190
  11.9 1.2 %copy-start = (f32[512,512]{1,0:T(8,128)S(1)}, f32[512,512]{1,0:T(8,128)}, u32[]{:S(2)}) copy-start(f32[512,512]{1,0:T(8,128)} %panel.1) | copy-start | bytes 3145732
  13.1 1.0 %copy-start.1 = (f32[2,256,256]{2,1,0:T(8,128)S(1)}, f32[2,256,256]{2,1,0:T(8,128)}, u32[]{:S(2)}) copy-start(f32[2,256,256]{2,1,0:T(8,128)} %diag_inv.1) | copy-start | bytes 1572868
  15.6 8.1 %collective-permute-start.8 = (f32[512,512]{1,0:T(8,128)S(1)}, f32[512,512]{1,0:T(8,128)S(1)}, u32[]{:S(2)}, u32[]{:S(2)}) collective-permute-start(f32[512,512]{1,0:T(8,128)S(1)} %get-tuple-element.10.factor), channel_id=1, source_target_pairs={{0,1},{1,0},{2,3},{3,2},{4,5},{5,4},{6,7},{7,6},{8,9},{9,8},{10,11... | collective-permute-start | bytes 3145736 | tf_op jit(solution)/shard_map/ppermute | solution.py:195
  21.6 3.6 %collective-permute-start.7 = (f32[512,512]{1,0:T(8,128)S(1)}, f32[512,512]{1,0:T(8,128)S(1)}, u32[]{:S(2)}, u32[]{:S(2)}) collective-permute-start(f32[512,512]{1,0:T(8,128)S(1)} %shard_map.60.quadrant), channel_id=1, source_target_pairs={{0,1},{1,0},{2,3},{3,2},{4,5},{5,4},{6,7},{7,6},{8,9},{9,8},{10,11... | collective-permute-start | bytes 3145736 | tf_op jit(solution)/shard_map/ppermute | solution.py:195
  27.4 1.9 %collective-permute-start.9 = (f32[2,256,256]{2,1,0:T(8,128)S(1)}, f32[2,256,256]{2,1,0:T(8,128)S(1)}, u32[]{:S(2)}, u32[]{:S(2)}) collective-permute-start(f32[2,256,256]{2,1,0:T(8,128)S(1)} %get-tuple-element.13), channel_id=1, source_target_pairs={{0,1},{1,0},{2,3},{3,2},{4,5},{5,4},{6,7},{7,6},{8,9},{9,8},{10,11... | collective-permute-start | bytes 1572872 | tf_op jit(solution)/shard_map/ppermute | solution.py:195

commit v3 on v2

v3 whole, which is shorter than its diff:
```python
import functools

import jax
import jax.numpy as jnp
from jax import lax
from jax.experimental import pallas as pl
from jax.experimental.pallas import tpu as pltpu
from jax.sharding import PartitionSpec as P

W = 1024
BLOCK_ROWS = 8
AXES = ("cfg", "prow", "pcol")
VMEM = pl.BlockSpec(memory_space=pltpu.VMEM)
SMEM = pl.BlockSpec(memory_space=pltpu.SMEM)


def split(value):
    high = value.astype(jnp.bfloat16)
    low = (value - high.astype(jnp.float32)).astype(jnp.bfloat16)
    return high, low


def product(left, right, dims):
    dot = functools.partial(lax.dot_general, dimension_numbers=(dims, ((), ())), preferred_element_type=jnp.float32)
    return dot(left[0], right[0]) + (dot(left[0], right[1]) + dot(left[1], right[0]))


PLAIN = ((1,), (0,))
FIRST = ((0,), (0,))


def factor_kernel(mask, panel, diag_inv, factor):
    children, width = diag_inv.shape[:2]
    here = mask.shape[0] // children
    block = panel.shape[0] // here
    for j in range(children):
        columns = pl.ds(j * width, width)
        masked = jnp.concatenate(
            [panel[pl.ds(r * block, block), columns] * mask[pl.ds(j * here + r, 1), :] for r in range(here)], axis=0
        )
        factor[:, columns] = product(split(masked), split(diag_inv[j]), PLAIN)


def own_place():
    prow = lax.axis_index("prow")
    return lax.rem(prow, 4), lax.div(prow, 4) == lax.axis_index("pcol")


def places(place):
    beside = place + 1 - 2 * lax.rem(place, 2)
    return beside, lax.rem(place + 2, 4), lax.rem(beside + 2, 4)


def at(place, block):
    return pl.ds(pl.multiple_of(place * block, block), block)


def pieces_kernel(
    sigma_top, pattern, panel, diag_inv, first, second, mask, panel_here, inverse_here, own, pattern_here, sems
):
    place, diagonal = own_place()
    loads = [
        pltpu.make_async_copy(source, here, sems.at[n])
        for n, (source, here) in enumerate(
            ((sigma_top, own), (pattern, pattern_here), (panel, panel_here), (diag_inv, inverse_here))
        )
    ]
    for load in loads:
        load.start()
    loads[0].wait()
    block = own.shape[0]
    half = block // 2

    @pl.when(diagonal)
    def _():
        opposite = at(lax.rem(place + 2, 4), block)
        for piece in (first, second):
            piece[pl.ds(0, block), :] = own[:, at(place, block)]
            piece[pl.ds(block, block), :] = own[:, at(lax.rem(place + 1, 4), block)]

        @pl.when(place < 2)
        def _():
            for piece in (first, second):
                piece[pl.ds(2 * block, half), :] = own[pl.ds(0, half), opposite]

        @pl.when(place >= 2)
        def _():
            turned = own[:, opposite].T
            for piece in (first, second):
                piece[pl.ds(2 * block, half), :] = turned[half:]

    @pl.when(jnp.logical_not(diagonal))
    def _():
        for n, piece in enumerate((first, second)):
            for b in range(2):
                piece[pl.ds(b * block, block), :] = own[:, pl.ds((2 * n + b) * block, block)]
            piece[pl.ds(2 * block, half), :] = jnp.zeros((half, block), jnp.float32)

    loads[1].wait()
    core = lax.axis_index("pcol")
    here = mask.shape[0] // pattern.shape[0]
    for j in range(pattern.shape[0]):
        for r in range(here):
            kept = pattern_here[j, core * here + r].astype(jnp.float32)
            mask[pl.ds(j * here + r, 1), :] = jnp.full((1, mask.shape[1]), kept, jnp.float32)
    loads[2].wait()
    loads[3].wait()


def parts(piece):
    block = piece.shape[1]
    return [piece.at[pl.ds(n * block, min(block, piece.shape[0] - n * block))] for n in range(3)]


def symmetric(quadrant, pieces):
    block = quadrant.shape[0] // 4
    half = block // 2
    for piece, place in pieces:
        rows = at(place, block)
        here, following, opposite = piece
        quadrant[rows, at(place, block)] = here[...]
        quadrant[rows, at(lax.rem(place + 1, 4), block)] = following[...]
        low = lax.rem(place, 2)
        quadrant[
            pl.ds(pl.multiple_of(low * block + lax.div(place, 2) * half, half), half), at(low + 2, block)
        ] = opposite[...]
    for row, column in ((0, 1), (1, 2), (2, 3), (3, 0), (0, 2), (1, 3)):
        rows, columns = pl.ds(row * block, block), pl.ds(column * block, block)
        quadrant[columns, rows] = quadrant[rows, columns].T


def row_blocks(quadrant, where, halves):
    block = quadrant.shape[0] // 4
    for n, piece in enumerate(halves):
        for b in range(2):
            quadrant[at(where, block), pl.ds((2 * n + b) * block, block)] = piece[pl.ds(b * block, block), :]


def own_half_kernel(mine_a, mine_b, got1, got2, got3, got4, got5, got6, quadrant, sent_a, sent_b):
    place, diagonal = own_place()
    beside, over, across = places(place)
    rows, block = sent_a.shape[0], quadrant.shape[0] // 4

    @pl.when(diagonal)
    def _():
        symmetric(
            quadrant,
            ((parts(mine_a), place), (parts(got3), beside), (parts(got4), over), (parts(got6), across)),
        )
        for n, piece in enumerate((got1, got5, got2)):
            rest = piece.shape[0] - rows
            sent_a[:, pl.ds(n * block, block)] = piece[pl.ds(0, rows), :]
            sent_a[pl.ds(n * rest, rest), pl.ds(3 * block, block)] = piece[pl.ds(rows, rest), :]

    @pl.when(jnp.logical_not(diagonal))
    def _():
        row_blocks(quadrant, place, (mine_a, mine_b))
        row_blocks(quadrant, beside, (got1, got4))
        row_blocks(quadrant, over, (got2, got3))
        row_blocks(quadrant, across, (got5, got6))
        sent_a[...] = quadrant[pl.ds(0, rows), :]
        sent_b[...] = quadrant[pl.ds(rows, rows), :]


def columns_of(value, j, width):
    return tuple(part[:, j * width : (j + 1) * width] for part in value)


def near_kernel(
    quadrant, factor, factor_other, diag_inv, partial, cross, base, far_high, far_low, turned_high, turned_low
):
    _, diagonal = own_place()
    width = cross.shape[1]

    def half(near, far):
        far_high[...], far_low[...] = split(far[...])
        turned_high[...], turned_low[...] = split(far[...].T)
        partial[...] = product(split(quadrant[...]), split(near[...]), FIRST)

    @pl.when(diagonal)
    def _():
        half(factor, factor_other)
        own, value = split(factor[...]), split(partial[...])
        for j in range(cross.shape[0]):
            cross[j] = product(columns_of(own, j, width), columns_of(value, j, width), FIRST)

    @pl.when(jnp.logical_not(diagonal))
    def _():
        half(factor_other, factor)
        value = split(partial[...])
        for j in range(cross.shape[0]):
            rows = pl.ds(j * width, width)
            mixed = product((turned_high[rows, :], turned_low[rows, :]), columns_of(value, j, width), PLAIN)
            cross[j] = mixed + mixed.T

    for j in range(cross.shape[0]):
        inverse = split(diag_inv[j])
        base[j] = cross[j] + product(inverse, inverse, FIRST)


def far_kernel(got1, got2, got5, got7, far_high, far_low, turned_high, turned_low, cross, quadrant):
    place, diagonal = own_place()
    beside, over, across = places(place)
    width = cross.shape[1]

    @pl.when(diagonal)
    def _():
        symmetric(
            quadrant,
            ((parts(got1), place), (parts(got2), over), (parts(got5), beside), (parts(got7), across)),
        )
        value = split(product(split(quadrant[...]), (far_high[...], far_low[...]), PLAIN))
        for j in range(cross.shape[0]):
            rows = pl.ds(j * width, width)
            cross[j] = product((turned_high[rows, :], turned_low[rows, :]), columns_of(value, j, width), PLAIN)


def panel_kernel(
    early_a, early_b, late, partial, far_high, far_low, turned_high, turned_low, base, near_other, far,
    sigma, diag, quadrant, sigma_here, diag_here, sigma_sems, diag_sems,
):
    place, diagonal = own_place()
    beside, over, across = places(place)
    width = diag.shape[1]
    children = range(diag.shape[0])
    chunk = sigma.shape[0] // sigma_sems.shape[0]
    chunks = [pl.ds(c * chunk, chunk) for c in range(sigma_sems.shape[0])]
    sigma_stores = [
        pltpu.make_async_copy(sigma_here.at[rows], sigma.at[rows], sigma_sems.at[c]) for c, rows in enumerate(chunks)
    ]
    diag_stores = [pltpu.make_async_copy(diag_here.at[j], diag.at[j], diag_sems.at[j]) for j in children]

    @pl.when(diagonal)
    def _():
        for j in children:
            diag_here[j] = base[j] + (near_other[j] + far[j])
            diag_stores[j].start()
        far_rows = far_high[...], far_low[...]
        early = [ref[pl.ds(c * chunk, chunk), :] for ref in (early_a, early_b) for c in range(ref.shape[0] // chunk)]
        for rows, store, here in zip(chunks, sigma_stores, early):
            sigma_here[rows, :] = -(partial[rows, :] + product(split(here), far_rows, PLAIN))
            store.start()

    @pl.when(jnp.logical_not(diagonal))
    def _():
        block = late.shape[1]
        half = block // 2
        pieces = [
            [early_a.at[pl.ds(m * block, block), pl.ds(n * block, block)] for m in range(2)]
            + [early_a.at[pl.ds(n * half, half), pl.ds(3 * block, block)]]
            for n in range(3)
        ]
        symmetric(
            quadrant, ((pieces[0], place), (pieces[1], beside), (pieces[2], over), (parts(late), across))
        )
        far_rows = far_high[...], far_low[...]
        values = []
        for rows, store in zip(chunks, sigma_stores):
            last = product(split(quadrant[rows, :]), far_rows, PLAIN)
            sigma_here[rows, :] = -(partial[rows, :] + last)
            store.start()
            values.append(split(last))
        value = tuple(jnp.concatenate(parts, axis=0) for parts in zip(*values))
        for j in children:
            turned = pl.ds(j * width, width)
            inner = product((turned_high[turned, :], turned_low[turned, :]), columns_of(value, j, width), PLAIN)
            diag_here[j] = (base[j] + near_other[j]) + inner
            diag_stores[j].start()

    for store in (*sigma_stores, *diag_stores):
        store.wait()


def call(kernel, out_shapes, flops, *args, specs=None, out_specs=None, scratch=()):
    moved = sum(a.size * a.dtype.itemsize for a in (*args, *out_shapes))
    return pl.pallas_call(
        kernel,
        out_shape=out_shapes,
        in_specs=specs or [VMEM] * len(args),
        out_specs=out_specs or [VMEM] * len(out_shapes),
        scratch_shapes=scratch,
        cost_estimate=pl.CostEstimate(flops=flops, bytes_accessed=moved, transcendentals=0),
        compiler_params=pltpu.CompilerParams(vmem_limit_bytes=32 * 1024 * 1024),
    )(*args)


def permute(value, mesh, diagonal_step, other_step=None):
    cfgs, prows, cores = (mesh.shape[axis] for axis in AXES)
    pairs = []
    for c in range(cfgs):
        for p in range(prows):
            for k in range(cores):
                to = p ^ (diagonal_step if p // 4 == k else other_step)
                pairs.append(((c * prows + p) * cores + k, (c * prows + to) * cores + (k ^ (p // 4) ^ (to // 4))))
    return lax.ppermute(value, AXES, pairs)


def exchange(value, mesh):
    cfgs, prows, cores = (mesh.shape[axis] for axis in AXES)
    return lax.ppermute(value, AXES, [(d, d ^ 1) for d in range(cfgs * prows * cores)])


def local_eight(mesh, sigma_top, panel_l, diag_inv, pattern):
    f32 = jnp.float32
    half_rows, own_columns = panel_l.shape
    block = sigma_top.shape[0]
    local_sn, width = diag_inv.shape[:2]
    shape = lambda *dims: jax.ShapeDtypeStruct(dims, f32)
    size = 2 * block + block // 2
    panel, square = shape(half_rows, own_columns), shape(half_rows, half_rows)
    children = shape(*diag_inv.shape)
    halves = [jax.ShapeDtypeStruct((half_rows, own_columns), jnp.bfloat16)] * 2
    turned = [jax.ShapeDtypeStruct((own_columns, half_rows), jnp.bfloat16)] * 2
    anywhere = pl.BlockSpec(memory_space=pl.ANY)
    in_hbm = lambda value: pltpu.with_memory_space_constraint(value, pltpu.HBM)
    step = 2 * half_rows * half_rows * own_columns
    mine_a, mine_b, mask, panel_here, inverse_here = call(
        pieces_kernel,
        [shape(size, block)] * 2 + [shape(local_sn * (half_rows // block), width), panel, children],
        1,
        in_hbm(sigma_top),
        in_hbm(pattern),
        in_hbm(panel_l),
        in_hbm(diag_inv),
        specs=[anywhere] * 4,
        scratch=[
            pltpu.VMEM(sigma_top.shape, f32),
            pltpu.SMEM(pattern.shape, jnp.int32),
            pltpu.SemaphoreType.DMA((4,)),
        ],
    )
    got1 = permute(mine_a, mesh, 4, 1)
    got2 = permute(mine_a, mesh, 6, 2)
    got3 = permute(mine_b, mesh, 1, 2)
    got4 = permute(mine_b, mesh, 2, 1)
    got5 = permute(got1, mesh, 1, 2)
    got6 = permute(got4, mesh, 1, 2)
    got7 = permute(got2, mesh, 1, 1)
    (factor,) = call(
        factor_kernel,
        [panel],
        1,
        mask,
        panel_here,
        inverse_here,
    )
    factor_other = exchange(factor, mesh)
    own_half, sent_a, sent_b = call(
        own_half_kernel,
        [square, shape(half_rows // 2, half_rows), shape(half_rows // 2, half_rows)],
        36 * step,
        mine_a, mine_b, got1, got2, got3, got4, got5, got6,
    )
    early_a, early_b = exchange(sent_a, mesh), exchange(sent_b, mesh)
    partial, near, base, *far_rows = call(
        near_kernel, [panel, children, children, *halves, *turned], 1, own_half, factor, factor_other, inverse_here
    )
    near_other = exchange(near, mesh)
    late = exchange(got7, mesh)
    (far,) = call(
        far_kernel,
        [children],
        16 * step,
        got1, got2, got5, got7, *far_rows,
        scratch=[pltpu.VMEM(square.shape, f32)],
    )
    return tuple(
        call(
            panel_kernel,
            [panel, children],
            1,
            early_a, early_b, late, partial, *far_rows, base, near_other, far,
            out_specs=[anywhere] * 2,
            scratch=[
                pltpu.VMEM(square.shape, f32),
                pltpu.VMEM(panel.shape, f32),
                pltpu.VMEM(children.shape, f32),
                pltpu.SemaphoreType.DMA((half_rows // block,)),
                pltpu.SemaphoreType.DMA((local_sn,)),
            ],
        )
    )


def local_any(sigma_top, panel_l, diag_inv, pattern):
    half_rows = panel_l.shape[0]
    local_sn, width = diag_inv.shape[:2]
    row_mask = jnp.repeat(pattern.astype(jnp.float32), W // BLOCK_ROWS, axis=1)
    row_mask = lax.dynamic_slice_in_dim(row_mask, lax.axis_index("pcol") * half_rows, half_rows, 1)
    masked = panel_l.reshape(half_rows, local_sn, width) * jnp.transpose(row_mask)[:, :, None]
    factor = jnp.einsum("wns,nst->wnt", masked, diag_inv, precision=lax.Precision.HIGHEST)
    factor_flat = factor.reshape(half_rows, local_sn * width)
    whole = lax.all_gather(factor_flat, "pcol", axis=0, tiled=True)
    gathered = lax.all_gather(sigma_top, "prow", axis=0, tiled=True)
    sigma = -jnp.einsum("wv,wt->vt", gathered, whole, precision=lax.Precision.HIGHEST)
    sigma_three = sigma.reshape(half_rows, local_sn, width)
    cross = lax.psum(jnp.einsum("wnr,wnt->nrt", factor, sigma_three, precision=lax.Precision.HIGHEST), "pcol")
    own_part = jnp.einsum("nsr,nst->nrt", diag_inv, diag_inv, precision=lax.Precision.HIGHEST)
    return sigma, own_part - cross


def solution(mesh):
    in_specs = (
        P(("cfg", "prow"), "pcol"),
        P(("cfg", "pcol"), "prow"),
        P(("cfg", "prow"), None, None),
        P(("cfg", "prow"), None),
    )
    out_specs = (P(("cfg", "pcol"), "prow"), P(("cfg", "prow"), None, None))
    local = functools.partial(local_eight, mesh) if mesh.shape["prow"] == 8 else local_any
    return jax.shard_map(local, mesh=mesh, in_specs=in_specs, out_specs=out_specs, check_vma=False)
```

time: 30.7 us -> 27.8 us (0.906)
  the two profiles are of different devices: /device:TPU:1 before, /device:TPU:11 now
where the time goes in v3:
time: 27.8 us; the launch traced here: 27.7 us
  starting transfers between devices  13.1 us (47%)
  Pallas kernels  7.13 us (26%)
  waiting for transfers between devices  6.8 us (24%)
  between operations  0.68 us (2%)
    ppermute x5, starting transfers between devices, exchange(): lax.ppermute(value, AXES, [(d, d ^ 1) for d in range(cfgs * prows * cores)])  8.27 us
    pallas_call x6, Pallas kernels, call(): pl.pallas_call(kernel, out_shape=out_shapes, in_specs=specs or [VMEM] * l...  7.13 us
    ppermute x7, waiting for transfers between devices, permute(): return lax.ppermute(value, AXES, pairs)  5.16 us
    ppermute x7, starting transfers between devices, permute(): return lax.ppermute(value, AXES, pairs)  4.82 us
    ppermute x5, waiting for transfers between devices, exchange(): lax.ppermute(value, AXES, [(d, d ^ 1) for d in range(cfgs * prows * cores)])  1.64 us
  transfers between devices with their start and end apart: 12, of which 5 were waited for; matrix products, arithmetic and copies ran while one was open for 0% of the time, Pallas kernels for 11%

profile of v3, /device:TPU:11, one launch (start us, length us, event | category | flops | bytes accessed | tf_op | source)
XLA Modules:
  0.0 27.7 jit_solution(7574077426667792377)
XLA Ops:
  0.6 1.5 %shard_map.59 = (f32[320,128]{1,0:T(8,128)S(1)}, f32[320,128]{1,0:T(8,128)S(1)}, f32[8,256]{1,0:T(8,128)S(1)}, f32[512,512]{1,0:T(8,128)S(1)}, f32[2,256,256]{2,1,0:T(8,128)S(1)}) custom-call(f32[128,512]{1,0:T(8,128)} %sigma_top.1, s32[2,8]{1,0:T(2,128)} %pattern.1, f32[512,512]{1,0:T(8,128)} %panel.1, f32[2,256,256]{2,1,0:T(8,128)} %diag_inv.1), custom_call_target="tpu_custom_call" | custom-call | flops 1 | bytes 3743808 | tf_op jit(solution)/shard_map/pallas_call | solution.py:276
  2.1 0.3 %collective-permute-start = (f32[320,128]{1,0:T(8,128)S(1)}, f32[320,128]{1,0:T(8,128)S(1)}, u32[]{:S(2)}, u32[]{:S(2)}) collective-permute-start(f32[320,128]{1,0:T(8,128)S(1)} %get-tuple-element.17.mine_a), channel_id=1, source_target_pairs={{0,9},{1,3},{2,11},{3,1},{4,13},{5,7},{6,15},{7,5},{8,10},{9,0},{1... | collective-permute-start | bytes 491528 | tf_op jit(solution)/shard_map/ppermute | solution.py:295
  2.4 1.2 %collective-permute-start.3 = (f32[320,128]{1,0:T(8,128)S(1)}, f32[320,128]{1,0:T(8,128)S(1)}, u32[]{:S(2)}, u32[]{:S(2)}) collective-permute-start(f32[320,128]{1,0:T(8,128)S(1)} %get-tuple-element.18.mine_b), channel_id=1, source_target_pairs={{0,4},{1,3},{2,6},{3,1},{4,0},{5,7},{6,2},{7,5},{8,10},{9,13},{10,... | collective-permute-start | bytes 491528 | tf_op jit(solution)/shard_map/ppermute | solution.py:295
  3.6 0.2 collective-permute-start.1
  3.8 1.3 %collective-permute-start.2 = (f32[320,128]{1,0:T(8,128)S(1)}, f32[320,128]{1,0:T(8,128)S(1)}, u32[]{:S(2)}, u32[]{:S(2)}) collective-permute-start(f32[320,128]{1,0:T(8,128)S(1)} %get-tuple-element.18.mine_b), channel_id=1, source_target_pairs={{0,2},{1,5},{2,0},{3,7},{4,6},{5,1},{6,4},{7,3},{8,12},{9,11},{10,... | collective-permute-start | bytes 491528 | tf_op jit(solution)/shard_map/ppermute | solution.py:295
  5.1 1.5 %collective-permute-done.got1 = f32[320,128]{1,0:T(8,128)S(1)} collective-permute-done((f32[320,128]{1,0:T(8,128)S(1)}, f32[320,128]{1,0:T(8,128)S(1)}, u32[]{:S(2)}, u32[]{:S(2)}) %collective-permute-start) | collective-permute-done | bytes 163872 | tf_op jit(solution)/shard_map/ppermute | solution.py:295
  6.6 0.2 collective-permute-start.4
  6.8 1.3 %collective-permute-done.3.got4 = f32[320,128]{1,0:T(8,128)S(1)} collective-permute-done((f32[320,128]{1,0:T(8,128)S(1)}, f32[320,128]{1,0:T(8,128)S(1)}, u32[]{:S(2)}, u32[]{:S(2)}) %collective-permute-start.3) | collective-permute-done | bytes 163872 | tf_op jit(solution)/shard_map/ppermute | solution.py:295
  8.2 0.4 %collective-permute-start.5 = (f32[320,128]{1,0:T(8,128)S(1)}, f32[320,128]{1,0:T(8,128)S(1)}, u32[]{:S(2)}, u32[]{:S(2)}) collective-permute-start(f32[320,128]{1,0:T(8,128)S(1)} %collective-permute-done.3.got4), channel_id=1, source_target_pairs={{0,2},{1,5},{2,0},{3,7},{4,6},{5,1},{6,4},{7,3},{8,12},{9,11},{10,... | collective-permute-start | bytes 491528 | tf_op jit(solution)/shard_map/ppermute | solution.py:295
  8.6 0.6 %shard_map.61.factor = f32[512,512]{1,0:T(8,128)S(1)} custom-call(f32[8,256]{1,0:T(8,128)S(1)} %get-tuple-element.22.mask, f32[512,512]{1,0:T(8,128)S(1)} %get-tuple-element.23.panel, f32[2,256,256]{2,1,0:T(8,128)S(1)} %get-tuple-element.24.diag_inv), custom_call_target="tpu_custom_call" | custom-call | flops 1 | bytes 2629632 | tf_op jit(solution)/shard_map/pallas_call | solution.py:276
  9.2 5.9 %collective-permute-start.10 = (f32[512,512]{1,0:T(8,128)S(1)}, f32[512,512]{1,0:T(8,128)S(1)}, u32[]{:S(2)}, u32[]{:S(2)}) collective-permute-start(f32[512,512]{1,0:T(8,128)S(1)} %shard_map.61.factor), channel_id=1, source_target_pairs={{0,1},{1,0},{2,3},{3,2},{4,5},{5,4},{6,7},{7,6},{8,9},{9,8},{10,11... | collective-permute-start | bytes 3145736 | tf_op jit(solution)/shard_map/ppermute | solution.py:300
  15.1 0.0 collective-permute-done.1.got2
  15.1 1.2 %collective-permute-start.8 = (f32[320,128]{1,0:T(8,128)S(1)}, f32[320,128]{1,0:T(8,128)S(1)}, u32[]{:S(2)}, u32[]{:S(2)}) collective-permute-start(f32[320,128]{1,0:T(8,128)S(1)} %collective-permute-done.1.got2), channel_id=1, source_target_pairs={{0,2},{1,3},{2,0},{3,1},{4,6},{5,7},{6,4},{7,5},{8,10},{9,11},{10,... | collective-permute-start | bytes 491528 | tf_op jit(solution)/shard_map/ppermute | solution.py:295
  16.4 0.0 collective-permute-done.2.got3
  16.4 0.1 collective-permute-done.4.got5
  16.5 2.2 %collective-permute-done.5.got6 = f32[320,128]{1,0:T(8,128)S(1)} collective-permute-done((f32[320,128]{1,0:T(8,128)S(1)}, f32[320,128]{1,0:T(8,128)S(1)}, u32[]{:S(2)}, u32[]{:S(2)}) %collective-permute-start.5) | collective-permute-done | bytes 163872 | tf_op jit(solution)/shard_map/ppermute | solution.py:295
  18.6 0.2 shard_map.60
  18.8 1.7 %collective-permute-start.6 = (f32[256,512]{1,0:T(8,128)S(1)}, f32[256,512]{1,0:T(8,128)S(1)}, u32[]{:S(2)}, u32[]{:S(2)}) collective-permute-start(f32[256,512]{1,0:T(8,128)S(1)} %get-tuple-element.19), channel_id=1, source_target_pairs={{0,1},{1,0},{2,3},{3,2},{4,5},{5,4},{6,7},{7,6},{8,9},{9,8},{10,11... | collective-permute-start | bytes 1572872 | tf_op jit(solution)/shard_map/ppermute | solution.py:300
  20.5 0.1 collective-permute-start.7
  20.6 0.0 collective-permute-done.10.factor_other
  20.6 2.4 %shard_map.62 = (f32[512,512]{1,0:T(8,128)S(1)}, f32[2,256,256]{2,1,0:T(8,128)S(1)}, f32[2,256,256]{2,1,0:T(8,128)S(1)}, bf16[512,512]{1,0:T(8,128)(2,1)S(1)}, b...) custom-call(f32[512,512]{1,0:T(8,128)S(1)} %get-tuple-element.21.quadrant, ...), custom_call_target="tpu_custom_call" | custom-call | flops 1 | bytes 7864320 | tf_op jit(solution)/shard_map/pallas_call | solution.py:276
  23.0 0.3 %collective-permute-start.11 = (f32[2,256,256]{2,1,0:T(8,128)S(1)}, f32[2,256,256]{2,1,0:T(8,128)S(1)}, u32[]{:S(2)}, u32[]{:S(2)}) collective-permute-start(f32[2,256,256]{2,1,0:T(8,128)S(1)} %get-tuple-element.31), channel_id=1, source_target_pairs={{0,1},{1,0},{2,3},{3,2},{4,5},{5,4},{6,7},{7,6},{8,9},{9,8},{10,11... | collective-permute-start | bytes 1572872 | tf_op jit(solution)/shard_map/ppermute | solution.py:300
  23.3 0.0 collective-permute-done.8.got7
  23.3 0.2 collective-permute-start.9
  23.6 1.6 %collective-permute-done.9.late = f32[320,128]{1,0:T(8,128)S(1)} collective-permute-done((f32[320,128]{1,0:T(8,128)S(1)}, f32[320,128]{1,0:T(8,128)S(1)}, u32[]{:S(2)}, u32[]{:S(2)}) %collective-permute-start.9) | collective-permute-done | bytes 163872 | tf_op jit(solution)/shard_map/ppermute | solution.py:300
  25.2 0.0 collective-permute-done.6.early_a
  25.2 0.0 collective-permute-done.7.early_b
  25.2 0.0 collective-permute-done.11.near_other
  25.2 2.5 %shard_map.64 = (f32[512,512]{1,0:T(8,128)}, f32[2,256,256]{2,1,0:T(8,128)}) custom-call(f32[256,512]{1,0:T(8,128)S(1)} %collective-permute-done.6.early_a, f32[256,512]{1,0:T(8,128)S(1)} %collective-permute-done.7.early_b, f32[320,128]{1,0:T(8,128)S(1)} %collective-permute-done.9.late, f32[512,512]{1,0:T(8,128)S(1)} %get-tuple-element.25.partial, ...), custom_call_target="tpu_custom_call" | custom-call | flops 1 | bytes 7503872 | tf_op jit(solution)/shard_map/pallas_call | solution.py:276
  (1 shorter events, 0.0 us)
Async XLA Ops:
  2.1 4.5 %collective-permute-start = (f32[320,128]{1,0:T(8,128)S(1)}, f32[320,128]{1,0:T(8,128)S(1)}, u32[]{:S(2)}, u32[]{:S(2)}) collective-permute-start(f32[320,128]{1,0:T(8,128)S(1)} %get-tuple-element.17.mine_a), channel_id=1, source_target_pairs={{0,9},{1,3},{2,11},{3,1},{4,13},{5,7},{6,15},{7,5},{8,10},{9,0},{1... | collective-permute-start | bytes 491528 | tf_op jit(solution)/shard_map/ppermute | solution.py:295
  2.4 5.7 %collective-permute-start.3 = (f32[320,128]{1,0:T(8,128)S(1)}, f32[320,128]{1,0:T(8,128)S(1)}, u32[]{:S(2)}, u32[]{:S(2)}) collective-permute-start(f32[320,128]{1,0:T(8,128)S(1)} %get-tuple-element.18.mine_b), channel_id=1, source_target_pairs={{0,4},{1,3},{2,6},{3,1},{4,0},{5,7},{6,2},{7,5},{8,10},{9,13},{10,... | collective-permute-start | bytes 491528 | tf_op jit(solution)/shard_map/ppermute | solution.py:295
  3.6 11.5 %collective-permute-start.1 = (f32[320,128]{1,0:T(8,128)S(1)}, f32[320,128]{1,0:T(8,128)S(1)}, u32[]{:S(2)}, u32[]{:S(2)}) collective-permute-start(f32[320,128]{1,0:T(8,128)S(1)} %get-tuple-element.17.mine_a), channel_id=1, source_target_pairs={{0,13},{1,5},{2,15},{3,7},{4,9},{5,1},{6,11},{7,3},{8,12},{9,4},{1... | collective-permute-start | bytes 491528 | tf_op jit(solution)/shard_map/ppermute | solution.py:295
  3.8 12.5 %collective-permute-start.2 = (f32[320,128]{1,0:T(8,128)S(1)}, f32[320,128]{1,0:T(8,128)S(1)}, u32[]{:S(2)}, u32[]{:S(2)}) collective-permute-start(f32[320,128]{1,0:T(8,128)S(1)} %get-tuple-element.18.mine_b), channel_id=1, source_target_pairs={{0,2},{1,5},{2,0},{3,7},{4,6},{5,1},{6,4},{7,3},{8,12},{9,11},{10,... | collective-permute-start | bytes 491528 | tf_op jit(solution)/shard_map/ppermute | solution.py:295
  6.6 9.8 %collective-permute-start.4 = (f32[320,128]{1,0:T(8,128)S(1)}, f32[320,128]{1,0:T(8,128)S(1)}, u32[]{:S(2)}, u32[]{:S(2)}) collective-permute-start(f32[320,128]{1,0:T(8,128)S(1)} %collective-permute-done.got1), channel_id=1, source_target_pairs={{0,2},{1,5},{2,0},{3,7},{4,6},{5,1},{6,4},{7,3},{8,12},{9,11},{10,... | collective-permute-start | bytes 491528 | tf_op jit(solution)/shard_map/ppermute | solution.py:295
  8.2 10.5 %collective-permute-start.5 = (f32[320,128]{1,0:T(8,128)S(1)}, f32[320,128]{1,0:T(8,128)S(1)}, u32[]{:S(2)}, u32[]{:S(2)}) collective-permute-start(f32[320,128]{1,0:T(8,128)S(1)} %collective-permute-done.3.got4), channel_id=1, source_target_pairs={{0,2},{1,5},{2,0},{3,7},{4,6},{5,1},{6,4},{7,3},{8,12},{9,11},{10,... | collective-permute-start | bytes 491528 | tf_op jit(solution)/shard_map/ppermute | solution.py:295
  9.2 11.4 %collective-permute-start.10 = (f32[512,512]{1,0:T(8,128)S(1)}, f32[512,512]{1,0:T(8,128)S(1)}, u32[]{:S(2)}, u32[]{:S(2)}) collective-permute-start(f32[512,512]{1,0:T(8,128)S(1)} %shard_map.61.factor), channel_id=1, source_target_pairs={{0,1},{1,0},{2,3},{3,2},{4,5},{5,4},{6,7},{7,6},{8,9},{9,8},{10,11... | collective-permute-start | bytes 3145736 | tf_op jit(solution)/shard_map/ppermute | solution.py:300
  15.1 8.2 %collective-permute-start.8 = (f32[320,128]{1,0:T(8,128)S(1)}, f32[320,128]{1,0:T(8,128)S(1)}, u32[]{:S(2)}, u32[]{:S(2)}) collective-permute-start(f32[320,128]{1,0:T(8,128)S(1)} %collective-permute-done.1.got2), channel_id=1, source_target_pairs={{0,2},{1,3},{2,0},{3,1},{4,6},{5,7},{6,4},{7,5},{8,10},{9,11},{10,... | collective-permute-start | bytes 491528 | tf_op jit(solution)/shard_map/ppermute | solution.py:295
  18.8 6.4 %collective-permute-start.6 = (f32[256,512]{1,0:T(8,128)S(1)}, f32[256,512]{1,0:T(8,128)S(1)}, u32[]{:S(2)}, u32[]{:S(2)}) collective-permute-start(f32[256,512]{1,0:T(8,128)S(1)} %get-tuple-element.19), channel_id=1, source_target_pairs={{0,1},{1,0},{2,3},{3,2},{4,5},{5,4},{6,7},{7,6},{8,9},{9,8},{10,11... | collective-permute-start | bytes 1572872 | tf_op jit(solution)/shard_map/ppermute | solution.py:300
  20.5 4.7 %collective-permute-start.7 = (f32[256,512]{1,0:T(8,128)S(1)}, f32[256,512]{1,0:T(8,128)S(1)}, u32[]{:S(2)}, u32[]{:S(2)}) collective-permute-start(f32[256,512]{1,0:T(8,128)S(1)} %get-tuple-element.20), channel_id=1, source_target_pairs={{0,1},{1,0},{2,3},{3,2},{4,5},{5,4},{6,7},{7,6},{8,9},{9,8},{10,11... | collective-permute-start | bytes 1572872 | tf_op jit(solution)/shard_map/ppermute | solution.py:300
  23.0 2.2 %collective-permute-start.11 = (f32[2,256,256]{2,1,0:T(8,128)S(1)}, f32[2,256,256]{2,1,0:T(8,128)S(1)}, u32[]{:S(2)}, u32[]{:S(2)}) collective-permute-start(f32[2,256,256]{2,1,0:T(8,128)S(1)} %get-tuple-element.31), channel_id=1, source_target_pairs={{0,1},{1,0},{2,3},{3,2},{4,5},{5,4},{6,7},{7,6},{8,9},{9,8},{10,11... | collective-permute-start | bytes 1572872 | tf_op jit(solution)/shard_map/ppermute | solution.py:300
  23.3 1.9 %collective-permute-start.9 = (f32[320,128]{1,0:T(8,128)S(1)}, f32[320,128]{1,0:T(8,128)S(1)}, u32[]{:S(2)}, u32[]{:S(2)}) collective-permute-start(f32[320,128]{1,0:T(8,128)S(1)} %collective-permute-done.8.got7), channel_id=1, source_target_pairs={{0,1},{1,0},{2,3},{3,2},{4,5},{5,4},{6,7},{7,6},{8,9},{9,8},{10,11... | collective-permute-start | bytes 491528 | tf_op jit(solution)/shard_map/ppermute | solution.py:300

commit v4 on v3

--- a/solution.py
+++ b/solution.py
@@ -9,6 +9,7 @@
 
 W = 1024
 BLOCK_ROWS = 8
+SPARE = 8
 AXES = ("cfg", "prow", "pcol")
 VMEM = pl.BlockSpec(memory_space=pltpu.VMEM)
 SMEM = pl.BlockSpec(memory_space=pltpu.SMEM)
@@ -55,6 +56,30 @@
     return pl.ds(pl.multiple_of(place * block, block), block)
 
 
+def parts(piece):
+    block = piece.shape[1]
+    half, last = block // 2, 2 * block
+    return [piece.at[pl.ds(start, size)] for start, size in ((0, block), (block, half), (block + half, half), (last, SPARE))]
+
+
+def folded(block):
+    half = block.shape[0] // 2
+    top, bottom = block[:half], block[half:]
+    row, lane = (lax.broadcasted_iota(jnp.int32, top.shape, axis) for axis in (0, 1))
+    top = jnp.where((lane < half) & (row > lane), pltpu.roll(bottom, half, 1), top)
+    return top, jnp.sum(jnp.where(row == lane - half, bottom, 0.0), axis=0, keepdims=True)
+
+
+def unfolded(top, ends):
+    half = top.shape[0]
+    row, lane = (lax.broadcasted_iota(jnp.int32, top.shape, axis) for axis in (0, 1))
+    turned = jnp.concatenate([top, jnp.zeros_like(top)], axis=0).T
+    upper = jnp.where((lane < half) & (row > lane), turned[:half], top)
+    own = jnp.where(row < lane - half, pltpu.roll(turned[:half], half, 1), ends)
+    own = jnp.where(row > lane - half, pltpu.roll(top, half, 1), own)
+    return jnp.concatenate([upper, jnp.where(lane < half, turned[half:], own)], axis=0)
+
+
 def pieces_kernel(
     sigma_top, pattern, panel, diag_inv, first, second, mask, panel_here, inverse_here, own, pattern_here, sems
 ):
@@ -74,27 +99,30 @@
     @pl.when(diagonal)
     def _():
         opposite = at(lax.rem(place + 2, 4), block)
+        top, ends = folded(own[:, at(place, block)])
         for piece in (first, second):
-            piece[pl.ds(0, block), :] = own[:, at(place, block)]
-            piece[pl.ds(block, block), :] = own[:, at(lax.rem(place + 1, 4), block)]
+            following, _, folded_top, folded_ends = parts(piece)
+            following[...] = own[:, at(lax.rem(place + 1, 4), block)]
+            folded_top[...] = top
+            folded_ends[...] = jnp.broadcast_to(ends, folded_ends.shape)
 
         @pl.when(place < 2)
         def _():
             for piece in (first, second):
-                piece[pl.ds(2 * block, half), :] = own[pl.ds(0, half), opposite]
+                parts(piece)[1][...] = own[pl.ds(0, half), opposite]
 
         @pl.when(place >= 2)
         def _():
             turned = own[:, opposite].T
             for piece in (first, second):
-                piece[pl.ds(2 * block, half), :] = turned[half:]
+                parts(piece)[1][...] = turned[half:]
 
     @pl.when(jnp.logical_not(diagonal))
     def _():
         for n, piece in enumerate((first, second)):
             for b in range(2):
                 piece[pl.ds(b * block, block), :] = own[:, pl.ds((2 * n + b) * block, block)]
-            piece[pl.ds(2 * block, half), :] = jnp.zeros((half, block), jnp.float32)
+            piece[pl.ds(2 * block, SPARE), :] = jnp.zeros((SPARE, block), jnp.float32)
 
     loads[1].wait()
     core = lax.axis_index("pcol")
@@ -107,18 +135,13 @@
     loads[3].wait()
 
 
-def parts(piece):
-    block = piece.shape[1]
-    return [piece.at[pl.ds(n * block, min(block, piece.shape[0] - n * block))] for n in range(3)]
-
-
 def symmetric(quadrant, pieces):
     block = quadrant.shape[0] // 4
     half = block // 2
     for piece, place in pieces:
         rows = at(place, block)
-        here, following, opposite = piece
-        quadrant[rows, at(place, block)] = here[...]
+        following, opposite, top, ends = piece
+        quadrant[rows, at(place, block)] = unfolded(top[...], ends[pl.ds(0, 1), :])
         quadrant[rows, at(lax.rem(place + 1, 4), block)] = following[...]
         low = lax.rem(place, 2)
         quadrant[
@@ -166,36 +189,50 @@
     return tuple(part[:, j * width : (j + 1) * width] for part in value)
 
 
-def near_kernel(
-    quadrant, factor, factor_other, diag_inv, partial, cross, base, far_high, far_low, turned_high, turned_low
-):
+def split_kernel(factor, factor_other, diag_inv, far_high, far_low, turned_high, turned_low, own_part):
+    _, diagonal = own_place()
+
+    def write(rows):
+        far_high[...], far_low[...] = split(rows)
+        turned_high[...], turned_low[...] = split(rows.T)
+
+    @pl.when(diagonal)
+    def _():
+        write(factor_other[...])
+
+    @pl.when(jnp.logical_not(diagonal))
+    def _():
+        write(factor[...])
+
+    for j in range(own_part.shape[0]):
+        inverse = split(diag_inv[j])
+        own_part[j] = product(inverse, inverse, FIRST)
+
+
+def near_kernel(quadrant, factor, factor_other, turned_high, turned_low, partial, cross):
     _, diagonal = own_place()
     width = cross.shape[1]
 
-    def half(near, far):
-        far_high[...], far_low[...] = split(far[...])
-        turned_high[...], turned_low[...] = split(far[...].T)
-        partial[...] = product(split(quadrant[...]), split(near[...]), FIRST)
-
-    @pl.when(diagonal)
-    def _():
-        half(factor, factor_other)
-        own, value = split(factor[...]), split(partial[...])
+    @pl.when(diagonal)
+    def _():
+        own = split(factor[...])
+        partial[...] = product(split(quadrant[...]), own, PLAIN)
+        value = split(partial[...])
         for j in range(cross.shape[0]):
             cross[j] = product(columns_of(own, j, width), columns_of(value, j, width), FIRST)
 
     @pl.when(jnp.logical_not(diagonal))
     def _():
-        half(factor_other, factor)
+        partial[...] = product(split(quadrant[...]), split(factor_other[...]), FIRST)
         value = split(partial[...])
         for j in range(cross.shape[0]):
             rows = pl.ds(j * width, width)
             mixed = product((turned_high[rows, :], turned_low[rows, :]), columns_of(value, j, width), PLAIN)
             cross[j] = mixed + mixed.T
 
-    for j in range(cross.shape[0]):
-        inverse = split(diag_inv[j])
-        base[j] = cross[j] + product(inverse, inverse, FIRST)
+
+def again_kernel(got, same):
+    same[...] = got[...]
 
 
 def far_kernel(got1, got2, got5, got7, far_high, far_low, turned_high, turned_low, cross, quadrant):
@@ -216,7 +253,7 @@
 
 
 def panel_kernel(
-    early_a, early_b, late, partial, far_high, far_low, turned_high, turned_low, base, near_other, far,
+    early_a, early_b, late, partial, far_high, far_low, turned_high, turned_low, own_part, near, near_other, far,
     sigma, diag, quadrant, sigma_here, diag_here, sigma_sems, diag_sems,
 ):
     place, diagonal = own_place()
@@ -233,7 +270,7 @@
     @pl.when(diagonal)
     def _():
         for j in children:
-            diag_here[j] = base[j] + (near_other[j] + far[j])
+            diag_here[j] = (own_part[j] + near[j]) + (near_other[j] + far[j])
             diag_stores[j].start()
         far_rows = far_high[...], far_low[...]
         early = [ref[pl.ds(c * chunk, chunk), :] for ref in (early_a, early_b) for c in range(ref.shape[0] // chunk)]
@@ -246,8 +283,11 @@
         block = late.shape[1]
         half = block // 2
         pieces = [
-            [early_a.at[pl.ds(m * block, block), pl.ds(n * block, block)] for m in range(2)]
-            + [early_a.at[pl.ds(n * half, half), pl.ds(3 * block, block)]]
+            [
+                early_a.at[pl.ds(start, size), pl.ds(n * block, block)]
+                for start, size in ((0, block), (block, half), (block + half, half))
+            ]
+            + [early_a.at[pl.ds(n * SPARE, SPARE), pl.ds(3 * block, block)]]
             for n in range(3)
         ]
         symmetric(
@@ -264,7 +304,7 @@
         for j in children:
             turned = pl.ds(j * width, width)
             inner = product((turned_high[turned, :], turned_low[turned, :]), columns_of(value, j, width), PLAIN)
-            diag_here[j] = (base[j] + near_other[j]) + inner
+            diag_here[j] = (own_part[j] + near[j]) + (near_other[j] + inner)
             diag_stores[j].start()
 
     for store in (*sigma_stores, *diag_stores):
@@ -290,8 +330,9 @@
     for c in range(cfgs):
         for p in range(prows):
             for k in range(cores):
-                to = p ^ (diagonal_step if p // 4 == k else other_step)
-                pairs.append(((c * prows + p) * cores + k, (c * prows + to) * cores + (k ^ (p // 4) ^ (to // 4))))
+                step = diagonal_step if p // 4 == k else other_step
+                to_cfg, to = (cfgs - 1 - c, p) if step is None else (c, p ^ step)
+                pairs.append(((c * prows + p) * cores + k, (to_cfg * prows + to) * cores + (k ^ (p // 4) ^ (to // 4))))
     return lax.ppermute(value, AXES, pairs)
 
 
@@ -306,7 +347,7 @@
     block = sigma_top.shape[0]
     local_sn, width = diag_inv.shape[:2]
     shape = lambda *dims: jax.ShapeDtypeStruct(dims, f32)
-    size = 2 * block + block // 2
+    size = 2 * block + SPARE
     panel, square = shape(half_rows, own_columns), shape(half_rows, half_rows)
     children = shape(*diag_inv.shape)
     halves = [jax.ShapeDtypeStruct((half_rows, own_columns), jnp.bfloat16)] * 2
@@ -335,7 +376,8 @@
     got4 = permute(mine_b, mesh, 2, 1)
     got5 = permute(got1, mesh, 1, 2)
     got6 = permute(got4, mesh, 1, 2)
-    got7 = permute(got2, mesh, 1, 1)
+    (got2_again,) = call(again_kernel, [shape(size, block)], 40 * step, got2)
+    got7 = permute(got2_again, mesh, 1)
     (factor,) = call(
         factor_kernel,
         [panel],
@@ -352,9 +394,8 @@
         mine_a, mine_b, got1, got2, got3, got4, got5, got6,
     )
     early_a, early_b = exchange(sent_a, mesh), exchange(sent_b, mesh)
-    partial, near, base, *far_rows = call(
-        near_kernel, [panel, children, children, *halves, *turned], 1, own_half, factor, factor_other, inverse_here
-    )
+    *far_rows, own_part = call(split_kernel, [*halves, *turned, children], 1, factor, factor_other, inverse_here)
+    partial, near = call(near_kernel, [panel, children], 1, own_half, factor, factor_other, *far_rows[2:])
     near_other = exchange(near, mesh)
     late = exchange(got7, mesh)
     (far,) = call(
@@ -369,7 +410,7 @@
             panel_kernel,
             [panel, children],
             1,
-            early_a, early_b, late, partial, *far_rows, base, near_other, far,
+            early_a, early_b, late, partial, *far_rows, own_part, near, near_other, far,
             out_specs=[anywhere] * 2,
             scratch=[
                 pltpu.VMEM(square.shape, f32),

time: 27.8 us -> 25.7 us (0.924)
  the two profiles are of different devices: /device:TPU:11 before, /device:TPU:1 now
where the time goes in v4:
time: 25.7 us; the launch traced here: 25.5 us
  starting transfers between devices  11.6 us (45%)
  Pallas kernels  7.39 us (29%)
  waiting for transfers between devices  5.83 us (23%)
  between operations  0.69 us (3%)
    pallas_call x8, Pallas kernels, call(): pl.pallas_call(kernel, out_shape=out_shapes, in_specs=specs or [VMEM] * l...  7.39 us
    ppermute x7, starting transfers between devices, permute(): return lax.ppermute(value, AXES, pairs)  6.47 us
    ppermute x5, starting transfers between devices, exchange(): lax.ppermute(value, AXES, [(d, d ^ 1) for d in range(cfgs * prows * cores)])  5.13 us
    ppermute x7, waiting for transfers between devices, permute(): return lax.ppermute(value, AXES, pairs)  4.23 us
    ppermute x5, waiting for transfers between devices, exchange(): lax.ppermute(value, AXES, [(d, d ^ 1) for d in range(cfgs * prows * cores)])  1.6 us
  transfers between devices with their start and end apart: 12, of which 4 were waited for; matrix products, arithmetic and copies ran while one was open for 0% of the time, Pallas kernels for 13%

profile of v4, /device:TPU:1, one launch (start us, length us, event | category | flops | bytes accessed | tf_op | source)
XLA Modules:
  0.0 25.5 jit_solution(13013420089444383833)
XLA Ops:
  0.6 1.5 %shard_map.59 = (f32[264,128]{1,0:T(8,128)S(1)}, f32[264,128]{1,0:T(8,128)S(1)}, f32[8,256]{1,0:T(8,128)S(1)}, f32[512,512]{1,0:T(8,128)S(1)}, f32[2,256,256]{2,1,0:T(8,128)S(1)}) custom-call(f32[128,512]{1,0:T(8,128)} %sigma_top.1, s32[2,8]{1,0:T(2,128)} %pattern.1, f32[512,512]{1,0:T(8,128)} %panel.1, f32[2,256,256]{2,1,0:T(8,128)} %diag_inv.1), custom_call_target="tpu_custom_call" | custom-call | flops 1 | bytes 3686464 | tf_op jit(solution)/shard_map/pallas_call | solution.py:316
  2.1 2.1 %collective-permute-start = (f32[264,128]{1,0:T(8,128)S(1)}, f32[264,128]{1,0:T(8,128)S(1)}, u32[]{:S(2)}, u32[]{:S(2)}) collective-permute-start(f32[264,128]{1,0:T(8,128)S(1)} %get-tuple-element.17.mine_a), channel_id=1, source_target_pairs={{0,9},{1,3},{2,11},{3,1},{4,13},{5,7},{6,15},{7,5},{8,10},{9,0},{1... | collective-permute-start | bytes 405512 | tf_op jit(solution)/shard_map/ppermute | solution.py:336
  4.2 0.1 collective-permute-start.3
  4.3 1.5 %collective-permute-start.1 = (f32[264,128]{1,0:T(8,128)S(1)}, f32[264,128]{1,0:T(8,128)S(1)}, u32[]{:S(2)}, u32[]{:S(2)}) collective-permute-start(f32[264,128]{1,0:T(8,128)S(1)} %get-tuple-element.17.mine_a), channel_id=1, source_target_pairs={{0,13},{1,5},{2,15},{3,7},{4,9},{5,1},{6,11},{7,3},{8,12},{9,4},{1... | collective-permute-start | bytes 405512 | tf_op jit(solution)/shard_map/ppermute | solution.py:336
  5.8 0.0 collective-permute-start.2
  5.8 0.6 %shard_map.62.factor = f32[512,512]{1,0:T(8,128)S(1)} custom-call(f32[8,256]{1,0:T(8,128)S(1)} %get-tuple-element.22.mask, f32[512,512]{1,0:T(8,128)S(1)} %get-tuple-element.23.panel, f32[2,256,256]{2,1,0:T(8,128)S(1)} %get-tuple-element.24.diag_inv), custom_call_target="tpu_custom_call" | custom-call | flops 1 | bytes 2629632 | tf_op jit(solution)/shard_map/pallas_call | solution.py:316
  6.4 3.3 %collective-permute-start.10 = (f32[512,512]{1,0:T(8,128)S(1)}, f32[512,512]{1,0:T(8,128)S(1)}, u32[]{:S(2)}, u32[]{:S(2)}) collective-permute-start(f32[512,512]{1,0:T(8,128)S(1)} %shard_map.62.factor), channel_id=1, source_target_pairs={{0,1},{1,0},{2,3},{3,2},{4,5},{5,4},{6,7},{7,6},{8,9},{9,8},{10,11... | collective-permute-start | bytes 3145736 | tf_op jit(solution)/shard_map/ppermute | solution.py:341
  9.7 0.0 collective-permute-done.got1
  9.7 0.4 %collective-permute-start.4 = (f32[264,128]{1,0:T(8,128)S(1)}, f32[264,128]{1,0:T(8,128)S(1)}, u32[]{:S(2)}, u32[]{:S(2)}) collective-permute-start(f32[264,128]{1,0:T(8,128)S(1)} %collective-permute-done.got1), channel_id=1, source_target_pairs={{0,2},{1,5},{2,0},{3,7},{4,6},{5,1},{6,4},{7,3},{8,12},{9,11},{10,... | collective-permute-start | bytes 405512 | tf_op jit(solution)/shard_map/ppermute | solution.py:336
  10.1 0.0 collective-permute-done.3.got4
  10.1 1.1 %collective-permute-start.5 = (f32[264,128]{1,0:T(8,128)S(1)}, f32[264,128]{1,0:T(8,128)S(1)}, u32[]{:S(2)}, u32[]{:S(2)}) collective-permute-start(f32[264,128]{1,0:T(8,128)S(1)} %collective-permute-done.3.got4), channel_id=1, source_target_pairs={{0,2},{1,5},{2,0},{3,7},{4,6},{5,1},{6,4},{7,3},{8,12},{9,11},{10,... | collective-permute-start | bytes 405512 | tf_op jit(solution)/shard_map/ppermute | solution.py:336
  11.2 0.0 collective-permute-done.1.got2.got
  11.2 1.3 %collective-permute-start.8 = (f32[264,128]{1,0:T(8,128)S(1)}, f32[264,128]{1,0:T(8,128)S(1)}, u32[]{:S(2)}, u32[]{:S(2)}) collective-permute-start(f32[264,128]{1,0:T(8,128)S(1)} %shard_map.61), channel_id=1, source_target_pairs={{0,2},{1,17},{2,0},{3,19},{4,6},{5,21},{6,4},{7,23},{8,24},{9,11},... | collective-permute-start | bytes 405512 | tf_op jit(solution)/shard_map/ppermute | solution.py:336
  12.5 0.6 %collective-permute-done.2.got3 = f32[264,128]{1,0:T(8,128)S(1)} collective-permute-done((f32[264,128]{1,0:T(8,128)S(1)}, f32[264,128]{1,0:T(8,128)S(1)}, u32[]{:S(2)}, u32[]{:S(2)}) %collective-permute-start.2) | collective-permute-done | bytes 135200 | tf_op jit(solution)/shard_map/ppermute | solution.py:336
  13.1 1.9 %collective-permute-done.4.got5 = f32[264,128]{1,0:T(8,128)S(1)} collective-permute-done((f32[264,128]{1,0:T(8,128)S(1)}, f32[264,128]{1,0:T(8,128)S(1)}, u32[]{:S(2)}, u32[]{:S(2)}) %collective-permute-start.4) | collective-permute-done | bytes 135200 | tf_op jit(solution)/shard_map/ppermute | solution.py:336
  15.0 1.7 %collective-permute-done.5.got6 = f32[264,128]{1,0:T(8,128)S(1)} collective-permute-done((f32[264,128]{1,0:T(8,128)S(1)}, f32[264,128]{1,0:T(8,128)S(1)}, u32[]{:S(2)}, u32[]{:S(2)}) %collective-permute-start.5) | collective-permute-done | bytes 135200 | tf_op jit(solution)/shard_map/ppermute | solution.py:336
  16.7 0.2 shard_map.60
  16.9 1.2 %collective-permute-start.6 = (f32[256,512]{1,0:T(8,128)S(1)}, f32[256,512]{1,0:T(8,128)S(1)}, u32[]{:S(2)}, u32[]{:S(2)}) collective-permute-start(f32[256,512]{1,0:T(8,128)S(1)} %get-tuple-element.19), channel_id=1, source_target_pairs={{0,1},{1,0},{2,3},{3,2},{4,5},{5,4},{6,7},{7,6},{8,9},{9,8},{10,11... | collective-permute-start | bytes 1572872 | tf_op jit(solution)/shard_map/ppermute | solution.py:341
  18.1 0.1 collective-permute-start.7
  18.2 0.0 collective-permute-done.10.factor_other
  18.2 0.8 %shard_map.63 = (bf16[512,512]{1,0:T(8,128)(2,1)S(1)}, bf16[512,512]{1,0:T(8,128)(2,1)S(1)}, bf16[512,512]{1,0:T(8,128)(2,1)S(1)}, bf16[512,512]{1,0:T(8,128)(2,1)S(1)}, f32[2,256,256]{2,1,0:T(8,128)S(1)}) custom-call(f32[512,512]{1,0:T(8,128)S(1)} %shard_map.62.factor, f32[512,512]{1,0:T(8,128)S(1)} %collective-permute-done.10.factor_other, ...), custom_call_target="tpu_custom_call" | custom-call | flops 1 | bytes 5242880 | tf_op jit(solution)/shard_map/pallas_call | solution.py:316
  19.0 1.7 %shard_map.64 = (f32[512,512]{1,0:T(8,128)S(1)}, f32[2,256,256]{2,1,0:T(8,128)S(1)}) custom-call(f32[512,512]{1,0:T(8,128)S(1)} %get-tuple-element.21.quadrant, f32[512,512]{1,0:T(8,128)S(1)} %shard_map.62.factor, f32[512,512]{1,0:T(8,128)S(1)} %collective-permute-done.10.factor_other, bf16[512,512]{1,0:T(8,128)(2,1)S(1)} %get-tuple-element.25.turned_high, ...), custom_call_target="tpu_custom_call" | custom-call | flops 1 | bytes 5767168 | tf_op jit(solution)/shard_map/pallas_call | solution.py:316
  20.6 0.3 %collective-permute-start.11 = (f32[2,256,256]{2,1,0:T(8,128)S(1)}, f32[2,256,256]{2,1,0:T(8,128)S(1)}, u32[]{:S(2)}, u32[]{:S(2)}) collective-permute-start(f32[2,256,256]{2,1,0:T(8,128)S(1)} %get-tuple-element.31.near), channel_id=1, source_target_pairs={{0,1},{1,0},{2,3},{3,2},{4,5},{5,4},{6,7},{7,6},{8,9},{9,8},{10,11... | collective-permute-start | bytes 1572872 | tf_op jit(solution)/shard_map/ppermute | solution.py:341
  21.0 0.0 collective-permute-done.8.got7
  21.0 0.2 collective-permute-start.9
  21.2 1.6 %collective-permute-done.9.late = f32[264,128]{1,0:T(8,128)S(1)} collective-permute-done((f32[264,128]{1,0:T(8,128)S(1)}, f32[264,128]{1,0:T(8,128)S(1)}, u32[]{:S(2)}, u32[]{:S(2)}) %collective-permute-start.9) | collective-permute-done | bytes 135200 | tf_op jit(solution)/shard_map/ppermute | solution.py:341
  22.8 0.0 collective-permute-done.6.early_a
  22.8 0.0 collective-permute-done.7.early_b
  22.8 0.0 collective-permute-done.11.near_other
  22.8 2.7 %shard_map.66 = (f32[512,512]{1,0:T(8,128)}, f32[2,256,256]{2,1,0:T(8,128)}) custom-call(f32[256,512]{1,0:T(8,128)S(1)} %collective-permute-done.6.early_a, f32[256,512]{1,0:T(8,128)S(1)} %collective-permute-done.7.early_b, f32[264,128]{1,0:T(8,128)S(1)} %collective-permute-done.9.late, f32[512,512]{1,0:T(8,128)S(1)} %get-tuple-element.27.partial, ...), custom_call_target="tpu_custom_call" | custom-call | flops 1 | bytes 7999488 | tf_op jit(solution)/shard_map/pallas_call | solution.py:316
  (2 shorter events, 0.0 us)
Async XLA Ops:
  2.1 7.6 %collective-permute-start = (f32[264,128]{1,0:T(8,128)S(1)}, f32[264,128]{1,0:T(8,128)S(1)}, u32[]{:S(2)}, u32[]{:S(2)}) collective-permute-start(f32[264,128]{1,0:T(8,128)S(1)} %get-tuple-element.17.mine_a), channel_id=1, source_target_pairs={{0,9},{1,3},{2,11},{3,1},{4,13},{5,7},{6,15},{7,5},{8,10},{9,0},{1... | collective-permute-start | bytes 405512 | tf_op jit(solution)/shard_map/ppermute | solution.py:336
  4.2 5.9 %collective-permute-start.3 = (f32[264,128]{1,0:T(8,128)S(1)}, f32[264,128]{1,0:T(8,128)S(1)}, u32[]{:S(2)}, u32[]{:S(2)}) collective-permute-start(f32[264,128]{1,0:T(8,128)S(1)} %get-tuple-element.18.mine_b), channel_id=1, source_target_pairs={{0,4},{1,3},{2,6},{3,1},{4,0},{5,7},{6,2},{7,5},{8,10},{9,13},{10,... | collective-permute-start | bytes 405512 | tf_op jit(solution)/shard_map/ppermute | solution.py:336
  4.3 6.9 %collective-permute-start.1 = (f32[264,128]{1,0:T(8,128)S(1)}, f32[264,128]{1,0:T(8,128)S(1)}, u32[]{:S(2)}, u32[]{:S(2)}) collective-permute-start(f32[264,128]{1,0:T(8,128)S(1)} %get-tuple-element.17.mine_a), channel_id=1, source_target_pairs={{0,13},{1,5},{2,15},{3,7},{4,9},{5,1},{6,11},{7,3},{8,12},{9,4},{1... | collective-permute-start | bytes 405512 | tf_op jit(solution)/shard_map/ppermute | solution.py:336
  5.8 7.3 %collective-permute-start.2 = (f32[264,128]{1,0:T(8,128)S(1)}, f32[264,128]{1,0:T(8,128)S(1)}, u32[]{:S(2)}, u32[]{:S(2)}) collective-permute-start(f32[264,128]{1,0:T(8,128)S(1)} %get-tuple-element.18.mine_b), channel_id=1, source_target_pairs={{0,2},{1,5},{2,0},{3,7},{4,6},{5,1},{6,4},{7,3},{8,12},{9,11},{10,... | collective-permute-start | bytes 405512 | tf_op jit(solution)/shard_map/ppermute | solution.py:336
  6.4 11.8 %collective-permute-start.10 = (f32[512,512]{1,0:T(8,128)S(1)}, f32[512,512]{1,0:T(8,128)S(1)}, u32[]{:S(2)}, u32[]{:S(2)}) collective-permute-start(f32[512,512]{1,0:T(8,128)S(1)} %shard_map.62.factor), channel_id=1, source_target_pairs={{0,1},{1,0},{2,3},{3,2},{4,5},{5,4},{6,7},{7,6},{8,9},{9,8},{10,11... | collective-permute-start | bytes 3145736 | tf_op jit(solution)/shard_map/ppermute | solution.py:341
  9.7 5.3 %collective-permute-start.4 = (f32[264,128]{1,0:T(8,128)S(1)}, f32[264,128]{1,0:T(8,128)S(1)}, u32[]{:S(2)}, u32[]{:S(2)}) collective-permute-start(f32[264,128]{1,0:T(8,128)S(1)} %collective-permute-done.got1), channel_id=1, source_target_pairs={{0,2},{1,5},{2,0},{3,7},{4,6},{5,1},{6,4},{7,3},{8,12},{9,11},{10,... | collective-permute-start | bytes 405512 | tf_op jit(solution)/shard_map/ppermute | solution.py:336
  10.1 6.6 %collective-permute-start.5 = (f32[264,128]{1,0:T(8,128)S(1)}, f32[264,128]{1,0:T(8,128)S(1)}, u32[]{:S(2)}, u32[]{:S(2)}) collective-permute-start(f32[264,128]{1,0:T(8,128)S(1)} %collective-permute-done.3.got4), channel_id=1, source_target_pairs={{0,2},{1,5},{2,0},{3,7},{4,6},{5,1},{6,4},{7,3},{8,12},{9,11},{10,... | collective-permute-start | bytes 405512 | tf_op jit(solution)/shard_map/ppermute | solution.py:336
  11.2 9.8 %collective-permute-start.8 = (f32[264,128]{1,0:T(8,128)S(1)}, f32[264,128]{1,0:T(8,128)S(1)}, u32[]{:S(2)}, u32[]{:S(2)}) collective-permute-start(f32[264,128]{1,0:T(8,128)S(1)} %shard_map.61), channel_id=1, source_target_pairs={{0,2},{1,17},{2,0},{3,19},{4,6},{5,21},{6,4},{7,23},{8,24},{9,11},... | collective-permute-start | bytes 405512 | tf_op jit(solution)/shard_map/ppermute | solution.py:336
  16.9 5.9 %collective-permute-start.6 = (f32[256,512]{1,0:T(8,128)S(1)}, f32[256,512]{1,0:T(8,128)S(1)}, u32[]{:S(2)}, u32[]{:S(2)}) collective-permute-start(f32[256,512]{1,0:T(8,128)S(1)} %get-tuple-element.19), channel_id=1, source_target_pairs={{0,1},{1,0},{2,3},{3,2},{4,5},{5,4},{6,7},{7,6},{8,9},{9,8},{10,11... | collective-permute-start | bytes 1572872 | tf_op jit(solution)/shard_map/ppermute | solution.py:341
  18.1 4.7 %collective-permute-start.7 = (f32[256,512]{1,0:T(8,128)S(1)}, f32[256,512]{1,0:T(8,128)S(1)}, u32[]{:S(2)}, u32[]{:S(2)}) collective-permute-start(f32[256,512]{1,0:T(8,128)S(1)} %get-tuple-element.20), channel_id=1, source_target_pairs={{0,1},{1,0},{2,3},{3,2},{4,5},{5,4},{6,7},{7,6},{8,9},{9,8},{10,11... | collective-permute-start | bytes 1572872 | tf_op jit(solution)/shard_map/ppermute | solution.py:341
  20.6 2.2 %collective-permute-start.11 = (f32[2,256,256]{2,1,0:T(8,128)S(1)}, f32[2,256,256]{2,1,0:T(8,128)S(1)}, u32[]{:S(2)}, u32[]{:S(2)}) collective-permute-start(f32[2,256,256]{2,1,0:T(8,128)S(1)} %get-tuple-element.31.near), channel_id=1, source_target_pairs={{0,1},{1,0},{2,3},{3,2},{4,5},{5,4},{6,7},{7,6},{8,9},{9,8},{10,11... | collective-permute-start | bytes 1572872 | tf_op jit(solution)/shard_map/ppermute | solution.py:341
  21.0 1.8 %collective-permute-start.9 = (f32[264,128]{1,0:T(8,128)S(1)}, f32[264,128]{1,0:T(8,128)S(1)}, u32[]{:S(2)}, u32[]{:S(2)}) collective-permute-start(f32[264,128]{1,0:T(8,128)S(1)} %collective-permute-done.8.got7), channel_id=1, source_target_pairs={{0,1},{1,0},{2,3},{3,2},{4,5},{5,4},{6,7},{7,6},{8,9},{9,8},{10,11... | collective-permute-start | bytes 405512 | tf_op jit(solution)/shard_map/ppermute | solution.py:341

commit v5 on v4

--- a/solution.py
+++ b/solution.py
@@ -159,7 +159,7 @@
             quadrant[at(where, block), pl.ds((2 * n + b) * block, block)] = piece[pl.ds(b * block, block), :]
 
 
-def own_half_kernel(mine_a, mine_b, got1, got2, got3, got4, got5, got6, quadrant, sent_a, sent_b):
+def own_half_kernel(mine_a, mine_b, got1, got2, got3, got4, got5, got6, far_high, far_low, quadrant, sent_a, sent_b):
     place, diagonal = own_place()
     beside, over, across = places(place)
     rows, block = sent_a.shape[0], quadrant.shape[0] // 4
@@ -181,8 +181,9 @@
         row_blocks(quadrant, beside, (got1, got4))
         row_blocks(quadrant, over, (got2, got3))
         row_blocks(quadrant, across, (got5, got6))
-        sent_a[...] = quadrant[pl.ds(0, rows), :]
-        sent_b[...] = quadrant[pl.ds(rows, rows), :]
+        result = product(split(quadrant[...]), (far_high[...], far_low[...]), PLAIN)
+        sent_a[...] = result[:rows]
+        sent_b[...] = result[rows:]
 
 
 def columns_of(value, j, width):
@@ -204,12 +205,12 @@
     def _():
         write(factor[...])
 
-    for j in range(own_part.shape[0]):
-        inverse = split(diag_inv[j])
-        own_part[j] = product(inverse, inverse, FIRST)
-
-
-def near_kernel(quadrant, factor, factor_other, turned_high, turned_low, partial, cross):
+        for j in range(own_part.shape[0]):
+            inverse = split(diag_inv[j])
+            own_part[j] = product(inverse, inverse, FIRST)
+
+
+def near_kernel(quadrant, factor, factor_other, turned_high, turned_low, own_part, partial, cross):
     _, diagonal = own_place()
     width = cross.shape[1]
 
@@ -228,14 +229,26 @@
         for j in range(cross.shape[0]):
             rows = pl.ds(j * width, width)
             mixed = product((turned_high[rows, :], turned_low[rows, :]), columns_of(value, j, width), PLAIN)
-            cross[j] = mixed + mixed.T
+            cross[j] = own_part[j] + (mixed + mixed.T)
 
 
 def again_kernel(got, same):
     same[...] = got[...]
 
 
-def far_kernel(got1, got2, got5, got7, far_high, far_low, turned_high, turned_low, cross, quadrant):
+def early_parts(early, block):
+    half = block // 2
+    return [
+        [
+            early.at[pl.ds(start, size), pl.ds(n * block, block)]
+            for start, size in ((0, block), (block, half), (block + half, half))
+        ]
+        + [early.at[pl.ds(n * SPARE, SPARE), pl.ds(3 * block, block)]]
+        for n in range(3)
+    ]
+
+
+def far_kernel(got1, got2, got5, got7, early, far_high, far_low, turned_high, turned_low, cross, first, quadrant):
     place, diagonal = own_place()
     beside, over, across = places(place)
     width = cross.shape[1]
@@ -251,10 +264,16 @@
             rows = pl.ds(j * width, width)
             cross[j] = product((turned_high[rows, :], turned_low[rows, :]), columns_of(value, j, width), PLAIN)
 
+    @pl.when(jnp.logical_not(diagonal))
+    def _():
+        quadrant[...] = jnp.zeros_like(quadrant)
+        symmetric(quadrant, zip(early_parts(early, got1.shape[1]), (place, beside, over)))
+        first[...] = product(split(quadrant[...]), (far_high[...], far_low[...]), PLAIN)
+
 
 def panel_kernel(
-    early_a, early_b, late, partial, far_high, far_low, turned_high, turned_low, own_part, near, near_other, far,
-    sigma, diag, quadrant, sigma_here, diag_here, sigma_sems, diag_sems,
+    early_a, early_b, late, partial, far_high, far_low, turned_high, turned_low, near, near_other, far, first,
+    sigma, diag, total, sigma_here, diag_here, sigma_sems, diag_sems,
 ):
     place, diagonal = own_place()
     beside, over, across = places(place)
@@ -270,41 +289,44 @@
     @pl.when(diagonal)
     def _():
         for j in children:
-            diag_here[j] = (own_part[j] + near[j]) + (near_other[j] + far[j])
+            diag_here[j] = (near[j] + near_other[j]) + far[j]
             diag_stores[j].start()
-        far_rows = far_high[...], far_low[...]
         early = [ref[pl.ds(c * chunk, chunk), :] for ref in (early_a, early_b) for c in range(ref.shape[0] // chunk)]
         for rows, store, here in zip(chunks, sigma_stores, early):
-            sigma_here[rows, :] = -(partial[rows, :] + product(split(here), far_rows, PLAIN))
+            sigma_here[rows, :] = -(partial[rows, :] + here)
             store.start()
 
     @pl.when(jnp.logical_not(diagonal))
     def _():
         block = late.shape[1]
         half = block // 2
-        pieces = [
-            [
-                early_a.at[pl.ds(start, size), pl.ds(n * block, block)]
-                for start, size in ((0, block), (block, half), (block + half, half))
-            ]
-            + [early_a.at[pl.ds(n * SPARE, SPARE), pl.ds(3 * block, block)]]
-            for n in range(3)
-        ]
-        symmetric(
-            quadrant, ((pieces[0], place), (pieces[1], beside), (pieces[2], over), (parts(late), across))
-        )
-        far_rows = far_high[...], far_low[...]
+        after, low = lax.rem(across + 1, 4), lax.rem(across, 2)
+        piece_rows = pl.ds(pl.multiple_of(low * block + lax.div(across, 2) * half, half), half)
+
+        def factors(rows):
+            return far_high[rows, :], far_low[rows, :]
+
+        following, opposite, top, ends = parts(late)
+        own = split(unfolded(top[...], ends[pl.ds(0, 1), :]))
+        following, opposite = split(following[...]), split(opposite[...])
+        total[...] = first[...]
+        total[at(across, block), :] += product(own, factors(at(across, block)), PLAIN) + product(
+            following, factors(at(after, block)), PLAIN
+        )
+        total[at(after, block), :] += product(following, factors(at(across, block)), FIRST)
+        total[piece_rows, :] += product(opposite, factors(at(low + 2, block)), PLAIN)
+        total[at(low + 2, block), :] += product(opposite, factors(piece_rows), FIRST)
         values = []
         for rows, store in zip(chunks, sigma_stores):
-            last = product(split(quadrant[rows, :]), far_rows, PLAIN)
+            last = total[rows, :]
             sigma_here[rows, :] = -(partial[rows, :] + last)
             store.start()
             values.append(split(last))
-        value = tuple(jnp.concatenate(parts, axis=0) for parts in zip(*values))
+        value = tuple(jnp.concatenate(rows, axis=0) for rows in zip(*values))
         for j in children:
             turned = pl.ds(j * width, width)
             inner = product((turned_high[turned, :], turned_low[turned, :]), columns_of(value, j, width), PLAIN)
-            diag_here[j] = (own_part[j] + near[j]) + (near_other[j] + inner)
+            diag_here[j] = (near[j] + near_other[j]) + inner
             diag_stores[j].start()
 
     for store in (*sigma_stores, *diag_stores):
@@ -378,6 +400,7 @@
     got6 = permute(got4, mesh, 1, 2)
     (got2_again,) = call(again_kernel, [shape(size, block)], 40 * step, got2)
     got7 = permute(got2_again, mesh, 1)
+    (got7,) = call(again_kernel, [shape(size, block)], 16 * step, got7)
     (factor,) = call(
         factor_kernel,
         [panel],
@@ -387,22 +410,22 @@
         inverse_here,
     )
     factor_other = exchange(factor, mesh)
+    *far_rows, own_part = call(split_kernel, [*halves, *turned, children], 1, factor, factor_other, inverse_here)
     own_half, sent_a, sent_b = call(
         own_half_kernel,
-        [square, shape(half_rows // 2, half_rows), shape(half_rows // 2, half_rows)],
+        [square] + [shape(half_rows // 2, own_columns)] * 2,
         36 * step,
-        mine_a, mine_b, got1, got2, got3, got4, got5, got6,
+        mine_a, mine_b, got1, got2, got3, got4, got5, got6, *far_rows[:2],
     )
     early_a, early_b = exchange(sent_a, mesh), exchange(sent_b, mesh)
-    *far_rows, own_part = call(split_kernel, [*halves, *turned, children], 1, factor, factor_other, inverse_here)
-    partial, near = call(near_kernel, [panel, children], 1, own_half, factor, factor_other, *far_rows[2:])
+    partial, near = call(near_kernel, [panel, children], 1, own_half, factor, factor_other, *far_rows[2:], own_part)
     near_other = exchange(near, mesh)
     late = exchange(got7, mesh)
-    (far,) = call(
+    far, first = call(
         far_kernel,
-        [children],
-        16 * step,
-        got1, got2, got5, got7, *far_rows,
+        [children, panel],
+        1,
+        got1, got2, got5, got7, early_a, *far_rows,
         scratch=[pltpu.VMEM(square.shape, f32)],
     )
     return tuple(
@@ -410,7 +433,7 @@
             panel_kernel,
             [panel, children],
             1,
-            early_a, early_b, late, partial, *far_rows, own_part, near, near_other, far,
+            early_a, early_b, late, partial, *far_rows, near, near_other, far, first,
             out_specs=[anywhere] * 2,
             scratch=[
                 pltpu.VMEM(square.shape, f32),

time: 25.7 us -> 24.6 us (0.957)
  waiting for transfers between devices: 5.83 us -> 4.24 us
  Pallas kernels: 7.39 us -> 8.89 us
  starting transfers between devices: 11.6 us -> 10.6 us
    ppermute x5, starting transfers between devices: 5.13 us -> 2.83 us  [exchange(): lax.ppermute(value, AXES, [(d, d ^ 1) for d in range(cfgs * prows * cores)])]
    pallas_call x8 -> x9, Pallas kernels: 7.39 us -> 8.89 us  [call(): pl.pallas_call(kernel, out_shape=out_shapes, in_specs=specs or [VMEM] * l...]
    ppermute x5, waiting for transfers between devices: 1.6 us -> 0.27 us  [exchange(): lax.ppermute(value, AXES, [(d, d ^ 1) for d in range(cfgs * prows * cores)])]
    ppermute x7, starting transfers between devices: 6.47 us -> 7.79 us  [permute(): return lax.ppermute(value, AXES, pairs)]
  transfers between devices with their start and end apart: 12 -> 12, of which waited for: 4 -> 4; matrix products, arithmetic and copies ran while one was open for 0% -> 0% of each run, Pallas kernels for 13% -> 21%
where the time goes in v5:
time: 24.6 us; the launch traced here: 24.5 us
  starting transfers between devices  10.6 us (43%)
  Pallas kernels  8.89 us (36%)
  waiting for transfers between devices  4.24 us (17%)
  between operations  0.7 us (3%)
    pallas_call x9, Pallas kernels, call(): pl.pallas_call(kernel, out_shape=out_shapes, in_specs=specs or [VMEM] * l...  8.89 us
    ppermute x7, starting transfers between devices, permute(): return lax.ppermute(value, AXES, pairs)  7.79 us
    ppermute x7, waiting for transfers between devices, permute(): return lax.ppermute(value, AXES, pairs)  3.98 us
    ppermute x5, starting transfers between devices, exchange(): lax.ppermute(value, AXES, [(d, d ^ 1) for d in range(cfgs * prows * cores)])  2.83 us
  transfers between devices with their start and end apart: 12, of which 4 were waited for; matrix products, arithmetic and copies ran while one was open for 0% of the time, Pallas kernels for 21%

profile of v5, /device:TPU:1, one launch (start us, length us, event | category | flops | bytes accessed | tf_op | source)
XLA Modules:
  0.0 24.5 jit_solution(2603384715463362412)
XLA Ops:
  0.6 1.5 %shard_map.59 = (f32[264,128]{1,0:T(8,128)S(1)}, f32[264,128]{1,0:T(8,128)S(1)}, f32[8,256]{1,0:T(8,128)S(1)}, f32[512,512]{1,0:T(8,128)S(1)}, f32[2,256,256]{2,1,0:T(8,128)S(1)}) custom-call(f32[128,512]{1,0:T(8,128)} %sigma_top.1, s32[2,8]{1,0:T(2,128)} %pattern.1, f32[512,512]{1,0:T(8,128)} %panel.1, f32[2,256,256]{2,1,0:T(8,128)} %diag_inv.1), custom_call_target="tpu_custom_call" | custom-call | flops 1 | bytes 3686464 | tf_op jit(solution)/shard_map/pallas_call | solution.py:338
  2.1 2.1 %collective-permute-start = (f32[264,128]{1,0:T(8,128)S(1)}, f32[264,128]{1,0:T(8,128)S(1)}, u32[]{:S(2)}, u32[]{:S(2)}) collective-permute-start(f32[264,128]{1,0:T(8,128)S(1)} %get-tuple-element.19.mine_a), channel_id=1, source_target_pairs={{0,9},{1,3},{2,11},{3,1},{4,13},{5,7},{6,15},{7,5},{8,10},{9,0},{1... | collective-permute-start | bytes 405512 | tf_op jit(solution)/shard_map/ppermute | solution.py:358
  4.2 0.1 collective-permute-start.3
  4.3 1.5 %collective-permute-start.1 = (f32[264,128]{1,0:T(8,128)S(1)}, f32[264,128]{1,0:T(8,128)S(1)}, u32[]{:S(2)}, u32[]{:S(2)}) collective-permute-start(f32[264,128]{1,0:T(8,128)S(1)} %get-tuple-element.19.mine_a), channel_id=1, source_target_pairs={{0,13},{1,5},{2,15},{3,7},{4,9},{5,1},{6,11},{7,3},{8,12},{9,4},{1... | collective-permute-start | bytes 405512 | tf_op jit(solution)/shard_map/ppermute | solution.py:358
  5.8 0.6 %shard_map.60.factor = f32[512,512]{1,0:T(8,128)S(1)} custom-call(f32[8,256]{1,0:T(8,128)S(1)} %get-tuple-element.21.mask, f32[512,512]{1,0:T(8,128)S(1)} %get-tuple-element.22.panel, f32[2,256,256]{2,1,0:T(8,128)S(1)} %get-tuple-element.23.diag_inv), custom_call_target="tpu_custom_call" | custom-call | flops 1 | bytes 2629632 | tf_op jit(solution)/shard_map/pallas_call | solution.py:338
  6.4 1.6 %collective-permute-start.6 = (f32[512,512]{1,0:T(8,128)S(1)}, f32[512,512]{1,0:T(8,128)S(1)}, u32[]{:S(2)}, u32[]{:S(2)}) collective-permute-start(f32[512,512]{1,0:T(8,128)S(1)} %shard_map.60.factor), channel_id=1, source_target_pairs={{0,1},{1,0},{2,3},{3,2},{4,5},{5,4},{6,7},{7,6},{8,9},{9,8},{10,11... | collective-permute-start | bytes 3145736 | tf_op jit(solution)/shard_map/ppermute | solution.py:363
  8.0 0.6 %collective-permute-start.2 = (f32[264,128]{1,0:T(8,128)S(1)}, f32[264,128]{1,0:T(8,128)S(1)}, u32[]{:S(2)}, u32[]{:S(2)}) collective-permute-start(f32[264,128]{1,0:T(8,128)S(1)} %get-tuple-element.20.mine_b), channel_id=1, source_target_pairs={{0,2},{1,5},{2,0},{3,7},{4,6},{5,1},{6,4},{7,3},{8,12},{9,11},{10,... | collective-permute-start | bytes 405512 | tf_op jit(solution)/shard_map/ppermute | solution.py:358
  8.6 0.0 collective-permute-done.got1
  8.6 0.9 %collective-permute-start.4 = (f32[264,128]{1,0:T(8,128)S(1)}, f32[264,128]{1,0:T(8,128)S(1)}, u32[]{:S(2)}, u32[]{:S(2)}) collective-permute-start(f32[264,128]{1,0:T(8,128)S(1)} %collective-permute-done.got1), channel_id=1, source_target_pairs={{0,2},{1,5},{2,0},{3,7},{4,6},{5,1},{6,4},{7,3},{8,12},{9,11},{10,... | collective-permute-start | bytes 405512 | tf_op jit(solution)/shard_map/ppermute | solution.py:358
  9.5 0.0 collective-permute-done.3.got4
  9.5 0.6 %collective-permute-start.5 = (f32[264,128]{1,0:T(8,128)S(1)}, f32[264,128]{1,0:T(8,128)S(1)}, u32[]{:S(2)}, u32[]{:S(2)}) collective-permute-start(f32[264,128]{1,0:T(8,128)S(1)} %collective-permute-done.3.got4), channel_id=1, source_target_pairs={{0,2},{1,5},{2,0},{3,7},{4,6},{5,1},{6,4},{7,3},{8,12},{9,11},{10,... | collective-permute-start | bytes 405512 | tf_op jit(solution)/shard_map/ppermute | solution.py:358
  10.1 0.0 collective-permute-done.1.got2.got
  10.1 2.1 %collective-permute-start.9 = (f32[264,128]{1,0:T(8,128)S(1)}, f32[264,128]{1,0:T(8,128)S(1)}, u32[]{:S(2)}, u32[]{:S(2)}) collective-permute-start(f32[264,128]{1,0:T(8,128)S(1)} %shard_map.63), channel_id=1, source_target_pairs={{0,2},{1,17},{2,0},{3,19},{4,6},{5,21},{6,4},{7,23},{8,24},{9,11},... | collective-permute-start | bytes 405512 | tf_op jit(solution)/shard_map/ppermute | solution.py:358
  12.2 0.0 collective-permute-done.6.factor_other
  12.2 0.5 %shard_map.61 = (bf16[512,512]{1,0:T(8,128)(2,1)S(1)}, bf16[512,512]{1,0:T(8,128)(2,1)S(1)}, bf16[512,512]{1,0:T(8,128)(2,1)S(1)}, bf16[512,512]{1,0:T(8,128)(2,1)S(1)}, f32[2,256,256]{2,1,0:T(8,128)S(1)}) custom-call(f32[512,512]{1,0:T(8,128)S(1)} %shard_map.60.factor, f32[512,512]{1,0:T(8,128)S(1)} %collective-permute-done.6.factor_other, ...), custom_call_target="tpu_custom_call" | custom-call | flops 1 | bytes 5242880 | tf_op jit(solution)/shard_map/pallas_call | solution.py:338
  12.7 0.3 %collective-permute-done.2.got3 = f32[264,128]{1,0:T(8,128)S(1)} collective-permute-done((f32[264,128]{1,0:T(8,128)S(1)}, f32[264,128]{1,0:T(8,128)S(1)}, u32[]{:S(2)}, u32[]{:S(2)}) %collective-permute-start.2) | collective-permute-done | bytes 135200 | tf_op jit(solution)/shard_map/ppermute | solution.py:358
  13.1 1.9 %collective-permute-done.4.got5 = f32[264,128]{1,0:T(8,128)S(1)} collective-permute-done((f32[264,128]{1,0:T(8,128)S(1)}, f32[264,128]{1,0:T(8,128)S(1)}, u32[]{:S(2)}, u32[]{:S(2)}) %collective-permute-start.4) | collective-permute-done | bytes 135200 | tf_op jit(solution)/shard_map/ppermute | solution.py:358
  15.0 1.7 %collective-permute-done.5.got6 = f32[264,128]{1,0:T(8,128)S(1)} collective-permute-done((f32[264,128]{1,0:T(8,128)S(1)}, f32[264,128]{1,0:T(8,128)S(1)}, u32[]{:S(2)}, u32[]{:S(2)}) %collective-permute-start.5) | collective-permute-done | bytes 135200 | tf_op jit(solution)/shard_map/ppermute | solution.py:358
  16.7 1.1 %shard_map.62 = (f32[512,512]{1,0:T(8,128)S(1)}, f32[256,512]{1,0:T(8,128)S(1)}, f32[256,512]{1,0:T(8,128)S(1)}) custom-call(f32[264,128]{1,0:T(8,128)S(1)} %get-tuple-element.19.mine_a, f32[264,128]{1,0:T(8,128)S(1)} %get-tuple-element.20.mine_b, f32[264,128]{1,0:T(8,128)S(1)} %collective-permute-done.got1, f32[264,128]{1,0:T(8,128)S(1)} %collective-permute-done.1.got2.got, ...), custom_call_target="tpu_custom_call" | custom-call | flops 9663676416 | bytes 4227072 | tf_op jit(solution)/shard_map/pallas_call | solution.py:338
  17.8 0.2 collective-permute-start.7
  18.0 0.4 %collective-permute-start.8 = (f32[256,512]{1,0:T(8,128)S(1)}, f32[256,512]{1,0:T(8,128)S(1)}, u32[]{:S(2)}, u32[]{:S(2)}) collective-permute-start(f32[256,512]{1,0:T(8,128)S(1)} %get-tuple-element.27), channel_id=1, source_target_pairs={{0,1},{1,0},{2,3},{3,2},{4,5},{5,4},{6,7},{7,6},{8,9},{9,8},{10,11... | collective-permute-start | bytes 1572872 | tf_op jit(solution)/shard_map/ppermute | solution.py:363
  18.4 1.7 %shard_map.65 = (f32[512,512]{1,0:T(8,128)S(1)}, f32[2,256,256]{2,1,0:T(8,128)S(1)}) custom-call(f32[512,512]{1,0:T(8,128)S(1)} %get-tuple-element.28.quadrant, f32[512,512]{1,0:T(8,128)S(1)} %shard_map.60.factor, f32[512,512]{1,0:T(8,128)S(1)} %collective-permute-done.6.factor_other, bf16[512,512]{1,0:T(8,128)(2,1)S(1)} %get-tuple-element.29.turned_high, ...), custom_call_target="tpu_custom_call" | custom-call | flops 1 | bytes 6291456 | tf_op jit(solution)/shard_map/pallas_call | solution.py:338
  20.0 0.1 collective-permute-start.11
  20.1 0.0 collective-permute-done.9.got
  20.1 0.6 %collective-permute-start.10 = (f32[264,128]{1,0:T(8,128)S(1)}, f32[264,128]{1,0:T(8,128)S(1)}, u32[]{:S(2)}, u32[]{:S(2)}) collective-permute-start(f32[264,128]{1,0:T(8,128)S(1)} %shard_map.64.got7), channel_id=1, source_target_pairs={{0,1},{1,0},{2,3},{3,2},{4,5},{5,4},{6,7},{7,6},{8,9},{9,8},{10,11... | collective-permute-start | bytes 405512 | tf_op jit(solution)/shard_map/ppermute | solution.py:363
  20.7 0.0 collective-permute-done.7.early.early_a
  20.7 1.2 %shard_map.66 = (f32[2,256,256]{2,1,0:T(8,128)S(1)}, f32[512,512]{1,0:T(8,128)S(1)}) custom-call(f32[264,128]{1,0:T(8,128)S(1)} %collective-permute-done.got1, f32[264,128]{1,0:T(8,128)S(1)} %collective-permute-done.1.got2.got, f32[264,128]{1,0:T(8,128)S(1)} %collective-permute-done.4.got5, f32[264,128]{1,0:T(8,128)S(1)} %shard_map.64.got7, ...), custom_call_target="tpu_custom_call" | custom-call | flops 1 | bytes 4734976 | tf_op jit(solution)/shard_map/pallas_call | solution.py:338
  21.9 0.3 %collective-permute-done.10.late = f32[264,128]{1,0:T(8,128)S(1)} collective-permute-done((f32[264,128]{1,0:T(8,128)S(1)}, f32[264,128]{1,0:T(8,128)S(1)}, u32[]{:S(2)}, u32[]{:S(2)}) %collective-permute-start.10) | collective-permute-done | bytes 135200 | tf_op jit(solution)/shard_map/ppermute | solution.py:363
  22.2 0.0 collective-permute-done.8.early_b
  22.2 0.0 collective-permute-done.11.near_other
  22.2 2.3 %shard_map.67 = (f32[512,512]{1,0:T(8,128)}, f32[2,256,256]{2,1,0:T(8,128)}) custom-call(f32[256,512]{1,0:T(8,128)S(1)} %collective-permute-done.7.early.early_a, f32[256,512]{1,0:T(8,128)S(1)} %collective-permute-done.8.early_b, f32[264,128]{1,0:T(8,128)S(1)} %collective-permute-done.10.late, f32[512,512]{1,0:T(8,128)S(1)} %get-tuple-element.32.partial, ...), custom_call_target="tpu_custom_call" | custom-call | flops 1 | bytes 8523776 | tf_op jit(solution)/shard_map/pallas_call | solution.py:338
  (2 shorter events, 0.0 us)
Async XLA Ops:
  2.1 6.5 %collective-permute-start = (f32[264,128]{1,0:T(8,128)S(1)}, f32[264,128]{1,0:T(8,128)S(1)}, u32[]{:S(2)}, u32[]{:S(2)}) collective-permute-start(f32[264,128]{1,0:T(8,128)S(1)} %get-tuple-element.19.mine_a), channel_id=1, source_target_pairs={{0,9},{1,3},{2,11},{3,1},{4,13},{5,7},{6,15},{7,5},{8,10},{9,0},{1... | collective-permute-start | bytes 405512 | tf_op jit(solution)/shard_map/ppermute | solution.py:358
  4.2 5.3 %collective-permute-start.3 = (f32[264,128]{1,0:T(8,128)S(1)}, f32[264,128]{1,0:T(8,128)S(1)}, u32[]{:S(2)}, u32[]{:S(2)}) collective-permute-start(f32[264,128]{1,0:T(8,128)S(1)} %get-tuple-element.20.mine_b), channel_id=1, source_target_pairs={{0,4},{1,3},{2,6},{3,1},{4,0},{5,7},{6,2},{7,5},{8,10},{9,13},{10,... | collective-permute-start | bytes 405512 | tf_op jit(solution)/shard_map/ppermute | solution.py:358
  4.3 5.8 %collective-permute-start.1 = (f32[264,128]{1,0:T(8,128)S(1)}, f32[264,128]{1,0:T(8,128)S(1)}, u32[]{:S(2)}, u32[]{:S(2)}) collective-permute-start(f32[264,128]{1,0:T(8,128)S(1)} %get-tuple-element.19.mine_a), channel_id=1, source_target_pairs={{0,13},{1,5},{2,15},{3,7},{4,9},{5,1},{6,11},{7,3},{8,12},{9,4},{1... | collective-permute-start | bytes 405512 | tf_op jit(solution)/shard_map/ppermute | solution.py:358
  6.4 5.8 %collective-permute-start.6 = (f32[512,512]{1,0:T(8,128)S(1)}, f32[512,512]{1,0:T(8,128)S(1)}, u32[]{:S(2)}, u32[]{:S(2)}) collective-permute-start(f32[512,512]{1,0:T(8,128)S(1)} %shard_map.60.factor), channel_id=1, source_target_pairs={{0,1},{1,0},{2,3},{3,2},{4,5},{5,4},{6,7},{7,6},{8,9},{9,8},{10,11... | collective-permute-start | bytes 3145736 | tf_op jit(solution)/shard_map/ppermute | solution.py:363
  8.0 5.0 %collective-permute-start.2 = (f32[264,128]{1,0:T(8,128)S(1)}, f32[264,128]{1,0:T(8,128)S(1)}, u32[]{:S(2)}, u32[]{:S(2)}) collective-permute-start(f32[264,128]{1,0:T(8,128)S(1)} %get-tuple-element.20.mine_b), channel_id=1, source_target_pairs={{0,2},{1,5},{2,0},{3,7},{4,6},{5,1},{6,4},{7,3},{8,12},{9,11},{10,... | collective-permute-start | bytes 405512 | tf_op jit(solution)/shard_map/ppermute | solution.py:358
  8.6 6.4 %collective-permute-start.4 = (f32[264,128]{1,0:T(8,128)S(1)}, f32[264,128]{1,0:T(8,128)S(1)}, u32[]{:S(2)}, u32[]{:S(2)}) collective-permute-start(f32[264,128]{1,0:T(8,128)S(1)} %collective-permute-done.got1), channel_id=1, source_target_pairs={{0,2},{1,5},{2,0},{3,7},{4,6},{5,1},{6,4},{7,3},{8,12},{9,11},{10,... | collective-permute-start | bytes 405512 | tf_op jit(solution)/shard_map/ppermute | solution.py:358
  9.5 7.2 %collective-permute-start.5 = (f32[264,128]{1,0:T(8,128)S(1)}, f32[264,128]{1,0:T(8,128)S(1)}, u32[]{:S(2)}, u32[]{:S(2)}) collective-permute-start(f32[264,128]{1,0:T(8,128)S(1)} %collective-permute-done.3.got4), channel_id=1, source_target_pairs={{0,2},{1,5},{2,0},{3,7},{4,6},{5,1},{6,4},{7,3},{8,12},{9,11},{10,... | collective-permute-start | bytes 405512 | tf_op jit(solution)/shard_map/ppermute | solution.py:358
  10.1 10.0 %collective-permute-start.9 = (f32[264,128]{1,0:T(8,128)S(1)}, f32[264,128]{1,0:T(8,128)S(1)}, u32[]{:S(2)}, u32[]{:S(2)}) collective-permute-start(f32[264,128]{1,0:T(8,128)S(1)} %shard_map.63), channel_id=1, source_target_pairs={{0,2},{1,17},{2,0},{3,19},{4,6},{5,21},{6,4},{7,23},{8,24},{9,11},... | collective-permute-start | bytes 405512 | tf_op jit(solution)/shard_map/ppermute | solution.py:358
  17.8 2.9 %collective-permute-start.7 = (f32[256,512]{1,0:T(8,128)S(1)}, f32[256,512]{1,0:T(8,128)S(1)}, u32[]{:S(2)}, u32[]{:S(2)}) collective-permute-start(f32[256,512]{1,0:T(8,128)S(1)} %get-tuple-element.26), channel_id=1, source_target_pairs={{0,1},{1,0},{2,3},{3,2},{4,5},{5,4},{6,7},{7,6},{8,9},{9,8},{10,11... | collective-permute-start | bytes 1572872 | tf_op jit(solution)/shard_map/ppermute | solution.py:363
  18.0 4.2 %collective-permute-start.8 = (f32[256,512]{1,0:T(8,128)S(1)}, f32[256,512]{1,0:T(8,128)S(1)}, u32[]{:S(2)}, u32[]{:S(2)}) collective-permute-start(f32[256,512]{1,0:T(8,128)S(1)} %get-tuple-element.27), channel_id=1, source_target_pairs={{0,1},{1,0},{2,3},{3,2},{4,5},{5,4},{6,7},{7,6},{8,9},{9,8},{10,11... | collective-permute-start | bytes 1572872 | tf_op jit(solution)/shard_map/ppermute | solution.py:363
  20.0 2.2 %collective-permute-start.11 = (f32[2,256,256]{2,1,0:T(8,128)S(1)}, f32[2,256,256]{2,1,0:T(8,128)S(1)}, u32[]{:S(2)}, u32[]{:S(2)}) collective-permute-start(f32[2,256,256]{2,1,0:T(8,128)S(1)} %get-tuple-element.33.near), channel_id=1, source_target_pairs={{0,1},{1,0},{2,3},{3,2},{4,5},{5,4},{6,7},{7,6},{8,9},{9,8},{10,11... | collective-permute-start | bytes 1572872 | tf_op jit(solution)/shard_map/ppermute | solution.py:363
  20.1 2.1 %collective-permute-start.10 = (f32[264,128]{1,0:T(8,128)S(1)}, f32[264,128]{1,0:T(8,128)S(1)}, u32[]{:S(2)}, u32[]{:S(2)}) collective-permute-start(f32[264,128]{1,0:T(8,128)S(1)} %shard_map.64.got7), channel_id=1, source_target_pairs={{0,1},{1,0},{2,3},{3,2},{4,5},{5,4},{6,7},{7,6},{8,9},{9,8},{10,11... | collective-permute-start | bytes 405512 | tf_op jit(solution)/shard_map/ppermute | solution.py:363

commit v6 on v5

--- a/solution.py
+++ b/solution.py
@@ -80,14 +80,12 @@
     return jnp.concatenate([upper, jnp.where(lane < half, turned[half:], own)], axis=0)
 
 
-def pieces_kernel(
-    sigma_top, pattern, panel, diag_inv, first, second, mask, panel_here, inverse_here, own, pattern_here, sems
-):
+def pieces_kernel(sigma_top, pattern, first, second, mask, own, pattern_here, sems):
     place, diagonal = own_place()
     loads = [
         pltpu.make_async_copy(source, here, sems.at[n])
         for n, (source, here) in enumerate(
-            ((sigma_top, own), (pattern, pattern_here), (panel, panel_here), (diag_inv, inverse_here))
+            ((sigma_top, own), (pattern, pattern_here))
         )
     ]
     for load in loads:
@@ -131,8 +129,6 @@
         for r in range(here):
             kept = pattern_here[j, core * here + r].astype(jnp.float32)
             mask[pl.ds(j * here + r, 1), :] = jnp.full((1, mask.shape[1]), kept, jnp.float32)
-    loads[2].wait()
-    loads[3].wait()
 
 
 def symmetric(quadrant, pieces):
@@ -159,7 +155,7 @@
             quadrant[at(where, block), pl.ds((2 * n + b) * block, block)] = piece[pl.ds(b * block, block), :]
 
 
-def own_half_kernel(mine_a, mine_b, got1, got2, got3, got4, got5, got6, far_high, far_low, quadrant, sent_a, sent_b):
+def own_half_kernel(mine_a, got1, got2, got3, got4, got5, got6, products, far_high, far_low, quadrant, sent_a, sent_b):
     place, diagonal = own_place()
     beside, over, across = places(place)
     rows, block = sent_a.shape[0], quadrant.shape[0] // 4
@@ -177,21 +173,28 @@
 
     @pl.when(jnp.logical_not(diagonal))
     def _():
-        row_blocks(quadrant, place, (mine_a, mine_b))
-        row_blocks(quadrant, beside, (got1, got4))
-        row_blocks(quadrant, over, (got2, got3))
-        row_blocks(quadrant, across, (got5, got6))
-        result = product(split(quadrant[...]), (far_high[...], far_low[...]), PLAIN)
-        sent_a[...] = result[:rows]
-        sent_b[...] = result[rows:]
+        last = product(split(row_of(got5, got6)), (far_high[...], far_low[...]), PLAIN)
+        sent_a[...] = products[pl.ds(0, rows), :]
+        sent_b[pl.ds(0, block), :] = products[pl.ds(rows, block), :]
+        sent_b[pl.ds(block, block), :] = last
 
 
 def columns_of(value, j, width):
     return tuple(part[:, j * width : (j + 1) * width] for part in value)
 
 
-def split_kernel(factor, factor_other, diag_inv, far_high, far_low, turned_high, turned_low, own_part):
-    _, diagonal = own_place()
+def row_of(first, second):
+    block = first.shape[1]
+    return jnp.concatenate([piece[pl.ds(b * block, block), :] for piece in (first, second) for b in range(2)], axis=1)
+
+
+def prepare_kernel(
+    mine_a, mine_b, got1, got2, got3, got4, factor, factor_other, diag_inv,
+    far_high, far_low, turned_high, turned_low, own_part, products, partial,
+):
+    place, diagonal = own_place()
+    beside, over, _ = places(place)
+    block = mine_a.shape[1]
 
     def write(rows):
         far_high[...], far_low[...] = split(rows)
@@ -204,14 +207,20 @@
     @pl.when(jnp.logical_not(diagonal))
     def _():
         write(factor[...])
-
         for j in range(own_part.shape[0]):
             inverse = split(diag_inv[j])
             own_part[j] = product(inverse, inverse, FIRST)
-
-
-def near_kernel(quadrant, factor, factor_other, turned_high, turned_low, own_part, partial, cross):
-    _, diagonal = own_place()
+        rows = split(jnp.concatenate([row_of(mine_a, mine_b), row_of(got1, got4), row_of(got2, got3)], axis=0))
+        products[...] = product(rows, (far_high[...], far_low[...]), PLAIN)
+        factors = jnp.concatenate([factor_other[at(where, block), :] for where in (place, beside, over)], axis=0)
+        partial[...] = product(rows, split(factors), FIRST)
+
+
+def near_kernel(
+    quadrant, got5, got6, most, factor, factor_other, turned_high, turned_low, own_part, partial, cross
+):
+    place, diagonal = own_place()
+    across = places(place)[2]
     width = cross.shape[1]
 
     @pl.when(diagonal)
@@ -224,7 +233,8 @@
 
     @pl.when(jnp.logical_not(diagonal))
     def _():
-        partial[...] = product(split(quadrant[...]), split(factor_other[...]), FIRST)
+        factors = split(factor_other[at(across, got5.shape[1]), :])
+        partial[...] = most[...] + product(split(row_of(got5, got6)), factors, FIRST)
         value = split(partial[...])
         for j in range(cross.shape[0]):
             rows = pl.ds(j * width, width)
@@ -234,6 +244,16 @@
 
 def again_kernel(got, same):
     same[...] = got[...]
+
+
+def joined(left, right, dims):
+    (over,), (under,) = dims
+    return lax.dot_general(
+        jnp.concatenate([left[0], left[0], left[1]], axis=over),
+        jnp.concatenate([right[0], right[1], right[0]], axis=under),
+        (dims, ((), ())),
+        preferred_element_type=jnp.float32,
+    )
 
 
 def early_parts(early, block):
@@ -281,9 +301,10 @@
     children = range(diag.shape[0])
     chunk = sigma.shape[0] // sigma_sems.shape[0]
     chunks = [pl.ds(c * chunk, chunk) for c in range(sigma_sems.shape[0])]
-    sigma_stores = [
-        pltpu.make_async_copy(sigma_here.at[rows], sigma.at[rows], sigma_sems.at[c]) for c, rows in enumerate(chunks)
-    ]
+
+    def store(rows, c):
+        return pltpu.make_async_copy(sigma_here.at[rows], sigma.at[rows], sigma_sems.at[c])
+
     diag_stores = [pltpu.make_async_copy(diag_here.at[j], diag.at[j], diag_sems.at[j]) for j in children]
 
     @pl.when(diagonal)
@@ -292,9 +313,10 @@
             diag_here[j] = (near[j] + near_other[j]) + far[j]
             diag_stores[j].start()
         early = [ref[pl.ds(c * chunk, chunk), :] for ref in (early_a, early_b) for c in range(ref.shape[0] // chunk)]
-        for rows, store, here in zip(chunks, sigma_stores, early):
+        for n, here in enumerate(early):
+            rows = at((place, beside, over, across)[n], chunk)
             sigma_here[rows, :] = -(partial[rows, :] + here)
-            store.start()
+            store(rows, n).start()
 
     @pl.when(jnp.logical_not(diagonal))
     def _():
@@ -310,17 +332,17 @@
         own = split(unfolded(top[...], ends[pl.ds(0, 1), :]))
         following, opposite = split(following[...]), split(opposite[...])
         total[...] = first[...]
-        total[at(across, block), :] += product(own, factors(at(across, block)), PLAIN) + product(
+        total[at(across, block), :] += joined(own, factors(at(across, block)), PLAIN) + joined(
             following, factors(at(after, block)), PLAIN
         )
-        total[at(after, block), :] += product(following, factors(at(across, block)), FIRST)
-        total[piece_rows, :] += product(opposite, factors(at(low + 2, block)), PLAIN)
-        total[at(low + 2, block), :] += product(opposite, factors(piece_rows), FIRST)
+        total[at(after, block), :] += joined(following, factors(at(across, block)), FIRST)
+        total[piece_rows, :] += joined(opposite, factors(at(low + 2, block)), PLAIN)
+        total[at(low + 2, block), :] += joined(opposite, factors(piece_rows), FIRST)
         values = []
-        for rows, store in zip(chunks, sigma_stores):
+        for c, rows in enumerate(chunks):
             last = total[rows, :]
             sigma_here[rows, :] = -(partial[rows, :] + last)
-            store.start()
+            store(rows, c).start()
             values.append(split(last))
         value = tuple(jnp.concatenate(rows, axis=0) for rows in zip(*values))
         for j in children:
@@ -329,8 +351,8 @@
             diag_here[j] = (near[j] + near_other[j]) + inner
             diag_stores[j].start()
 
-    for store in (*sigma_stores, *diag_stores):
-        store.wait()
+    for copy in (*(store(rows, c) for c, rows in enumerate(chunks)), *diag_stores):
+        copy.wait()
 
 
 def call(kernel, out_shapes, flops, *args, specs=None, out_specs=None, scratch=()):
@@ -377,19 +399,17 @@
     anywhere = pl.BlockSpec(memory_space=pl.ANY)
     in_hbm = lambda value: pltpu.with_memory_space_constraint(value, pltpu.HBM)
     step = 2 * half_rows * half_rows * own_columns
-    mine_a, mine_b, mask, panel_here, inverse_here = call(
+    mine_a, mine_b, mask = call(
         pieces_kernel,
-        [shape(size, block)] * 2 + [shape(local_sn * (half_rows // block), width), panel, children],
-        1,
+        [shape(size, block)] * 2 + [shape(local_sn * (half_rows // block), width)],
+        40 * step,
         in_hbm(sigma_top),
         in_hbm(pattern),
-        in_hbm(panel_l),
-        in_hbm(diag_inv),
-        specs=[anywhere] * 4,
+        specs=[anywhere] * 2,
         scratch=[
             pltpu.VMEM(sigma_top.shape, f32),
             pltpu.SMEM(pattern.shape, jnp.int32),
-            pltpu.SemaphoreType.DMA((4,)),
+            pltpu.SemaphoreType.DMA((2,)),
         ],
     )
     got1 = permute(mine_a, mesh, 4, 1)
@@ -406,19 +426,29 @@
         [panel],
         1,
         mask,
-        panel_here,
-        inverse_here,
+        panel_l,
+        diag_inv,
     )
     factor_other = exchange(factor, mesh)
-    *far_rows, own_part = call(split_kernel, [*halves, *turned, children], 1, factor, factor_other, inverse_here)
+    *far_rows, own_part, products, most = call(
+        prepare_kernel,
+        [*halves, *turned, children, shape(3 * block, own_columns), panel],
+        1,
+        mine_a, mine_b, got1, got2, got3, got4, factor, factor_other, diag_inv,
+    )
     own_half, sent_a, sent_b = call(
         own_half_kernel,
         [square] + [shape(half_rows // 2, own_columns)] * 2,
         36 * step,
-        mine_a, mine_b, got1, got2, got3, got4, got5, got6, *far_rows[:2],
+        mine_a, got1, got2, got3, got4, got5, got6, products, *far_rows[:2],
     )
     early_a, early_b = exchange(sent_a, mesh), exchange(sent_b, mesh)
-    partial, near = call(near_kernel, [panel, children], 1, own_half, factor, factor_other, *far_rows[2:], own_part)
+    partial, near = call(
+        near_kernel,
+        [panel, children],
+        4 * step,
+        own_half, got5, got6, most, factor, factor_other, *far_rows[2:], own_part,
+    )
     near_other = exchange(near, mesh)
     late = exchange(got7, mesh)
     far, first = call(

time: 24.6 us -> 23.6 us (0.959)
  waiting for transfers between devices: 4.24 us -> 2.68 us
  starting transfers between devices: 10.6 us -> 11.4 us
    ppermute x7, waiting for transfers between devices: 3.98 us -> 2.66 us  [permute(): return lax.ppermute(value, AXES, pairs)]
    ppermute x5, starting transfers between devices: 2.83 us -> 3.74 us  [exchange(): lax.ppermute(value, AXES, [(d, d ^ 1) for d in range(cfgs * prows * cores)])]
  transfers between devices with their start and end apart: 12 -> 12, of which waited for: 4 -> 3; matrix products, arithmetic and copies ran while one was open for 0% -> 0% of each run, Pallas kernels for 21% -> 23%
where the time goes in v6:
time: 23.6 us; the launch traced here: 23.4 us
  starting transfers between devices  11.4 us (48%)
  Pallas kernels  8.65 us (37%)
  waiting for transfers between devices  2.68 us (11%)
  between operations  0.71 us (3%)
    pallas_call x9, Pallas kernels, call(): pl.pallas_call(kernel, out_shape=out_shapes, in_specs=specs or [VMEM] * l...  8.65 us
    ppermute x7, starting transfers between devices, permute(): return lax.ppermute(value, AXES, pairs)  7.62 us
    ppermute x5, starting transfers between devices, exchange(): lax.ppermute(value, AXES, [(d, d ^ 1) for d in range(cfgs * prows * cores)])  3.74 us
    ppermute x7, waiting for transfers between devices, permute(): return lax.ppermute(value, AXES, pairs)  2.66 us
  transfers between devices with their start and end apart: 12, of which 3 were waited for; matrix products, arithmetic and copies ran while one was open for 0% of the time, Pallas kernels for 23%

profile of v6, /device:TPU:1, one launch (start us, length us, event | category | flops | bytes accessed | tf_op | source)
XLA Modules:
  0.0 23.4 jit_solution(9754127774464426719)
XLA Ops:
  0.7 1.1 %shard_map.59 = (f32[264,128]{1,0:T(8,128)S(1)}, f32[264,128]{1,0:T(8,128)S(1)}, f32[8,256]{1,0:T(8,128)S(1)}) custom-call(f32[128,512]{1,0:T(8,128)} %sigma_top.1, s32[2,8]{1,0:T(2,128)} %pattern.1), custom_call_target="tpu_custom_call" | custom-call | flops 10737418240 | bytes 540736 | tf_op jit(solution)/shard_map/pallas_call | solution.py:360
  1.8 2.1 %collective-permute-start = (f32[264,128]{1,0:T(8,128)S(1)}, f32[264,128]{1,0:T(8,128)S(1)}, u32[]{:S(2)}, u32[]{:S(2)}) collective-permute-start(f32[264,128]{1,0:T(8,128)S(1)} %get-tuple-element.19.mine_a), channel_id=1, source_target_pairs={{0,9},{1,3},{2,11},{3,1},{4,13},{5,7},{6,15},{7,5},{8,10},{9,0},{1... | collective-permute-start | bytes 405512 | tf_op jit(solution)/shard_map/ppermute | solution.py:380
  3.9 0.1 collective-permute-start.3
  4.0 1.5 %collective-permute-start.1 = (f32[264,128]{1,0:T(8,128)S(1)}, f32[264,128]{1,0:T(8,128)S(1)}, u32[]{:S(2)}, u32[]{:S(2)}) collective-permute-start(f32[264,128]{1,0:T(8,128)S(1)} %get-tuple-element.19.mine_a), channel_id=1, source_target_pairs={{0,13},{1,5},{2,15},{3,7},{4,9},{5,1},{6,11},{7,3},{8,12},{9,4},{1... | collective-permute-start | bytes 405512 | tf_op jit(solution)/shard_map/ppermute | solution.py:380
  5.4 0.0 copy-done
  5.4 0.6 %shard_map.60.factor = f32[512,512]{1,0:T(8,128)S(1)} custom-call(f32[8,256]{1,0:T(8,128)S(1)} %get-tuple-element.21.mask, f32[512,512]{1,0:T(8,128)S(1)} %copy-done.1, f32[2,256,256]{2,1,0:T(8,128)S(1)} %copy-done), custom_call_target="tpu_custom_call" | custom-call | flops 1 | bytes 2629632 | tf_op jit(solution)/shard_map/pallas_call | solution.py:360
  6.1 1.8 %collective-permute-start.6 = (f32[512,512]{1,0:T(8,128)S(1)}, f32[512,512]{1,0:T(8,128)S(1)}, u32[]{:S(2)}, u32[]{:S(2)}) collective-permute-start(f32[512,512]{1,0:T(8,128)S(1)} %shard_map.60.factor), channel_id=1, source_target_pairs={{0,1},{1,0},{2,3},{3,2},{4,5},{5,4},{6,7},{7,6},{8,9},{9,8},{10,11... | collective-permute-start | bytes 3145736 | tf_op jit(solution)/shard_map/ppermute | solution.py:385
  7.9 0.6 %collective-permute-start.2 = (f32[264,128]{1,0:T(8,128)S(1)}, f32[264,128]{1,0:T(8,128)S(1)}, u32[]{:S(2)}, u32[]{:S(2)}) collective-permute-start(f32[264,128]{1,0:T(8,128)S(1)} %get-tuple-element.20.mine_b), channel_id=1, source_target_pairs={{0,2},{1,5},{2,0},{3,7},{4,6},{5,1},{6,4},{7,3},{8,12},{9,11},{10,... | collective-permute-start | bytes 405512 | tf_op jit(solution)/shard_map/ppermute | solution.py:380
  8.4 0.0 collective-permute-done.got1
  8.4 0.9 %collective-permute-start.4 = (f32[264,128]{1,0:T(8,128)S(1)}, f32[264,128]{1,0:T(8,128)S(1)}, u32[]{:S(2)}, u32[]{:S(2)}) collective-permute-start(f32[264,128]{1,0:T(8,128)S(1)} %collective-permute-done.got1), channel_id=1, source_target_pairs={{0,2},{1,5},{2,0},{3,7},{4,6},{5,1},{6,4},{7,3},{8,12},{9,11},{10,... | collective-permute-start | bytes 405512 | tf_op jit(solution)/shard_map/ppermute | solution.py:380
  9.3 0.0 collective-permute-done.3.got4
  9.3 0.6 %collective-permute-start.5 = (f32[264,128]{1,0:T(8,128)S(1)}, f32[264,128]{1,0:T(8,128)S(1)}, u32[]{:S(2)}, u32[]{:S(2)}) collective-permute-start(f32[264,128]{1,0:T(8,128)S(1)} %collective-permute-done.3.got4), channel_id=1, source_target_pairs={{0,2},{1,5},{2,0},{3,7},{4,6},{5,1},{6,4},{7,3},{8,12},{9,11},{10,... | collective-permute-start | bytes 405512 | tf_op jit(solution)/shard_map/ppermute | solution.py:380
  9.9 0.0 collective-permute-done.1.got2.got
  9.9 1.9 %collective-permute-start.9 = (f32[264,128]{1,0:T(8,128)S(1)}, f32[264,128]{1,0:T(8,128)S(1)}, u32[]{:S(2)}, u32[]{:S(2)}) collective-permute-start(f32[264,128]{1,0:T(8,128)S(1)} %shard_map.63), channel_id=1, source_target_pairs={{0,2},{1,17},{2,0},{3,19},{4,6},{5,21},{6,4},{7,23},{8,24},{9,11},... | collective-permute-start | bytes 405512 | tf_op jit(solution)/shard_map/ppermute | solution.py:380
  11.9 0.8 %collective-permute-done.2.got3 = f32[264,128]{1,0:T(8,128)S(1)} collective-permute-done((f32[264,128]{1,0:T(8,128)S(1)}, f32[264,128]{1,0:T(8,128)S(1)}, u32[]{:S(2)}, u32[]{:S(2)}) %collective-permute-start.2) | collective-permute-done | bytes 135200 | tf_op jit(solution)/shard_map/ppermute | solution.py:380
  12.7 0.0 collective-permute-done.6.factor_other
  12.7 1.9 %shard_map.61 = (bf16[512,512]{1,0:T(8,128)(2,1)S(1)}, bf16[512,512]{1,0:T(8,128)(2,1)S(1)}, bf16[512,512]{1,0:T(8,128)(2,1)S(1)}, bf16[512,512]{1,0:T(8,128)(2,...) custom-call(f32[264,128]{1,0:T(8,128)S(1)} %get-tuple-element.19.mine_a, ...), custom_call_target="tpu_custom_call" | custom-call | flops 1 | bytes 7888896 | tf_op jit(solution)/shard_map/pallas_call | solution.py:360
  14.6 0.1 collective-permute-done.4.got5
  14.7 1.7 %collective-permute-done.5.got6 = f32[264,128]{1,0:T(8,128)S(1)} collective-permute-done((f32[264,128]{1,0:T(8,128)S(1)}, f32[264,128]{1,0:T(8,128)S(1)}, u32[]{:S(2)}, u32[]{:S(2)}) %collective-permute-start.5) | collective-permute-done | bytes 135200 | tf_op jit(solution)/shard_map/ppermute | solution.py:380
  16.4 0.4 %shard_map.62 = (f32[512,512]{1,0:T(8,128)S(1)}, f32[256,512]{1,0:T(8,128)S(1)}, f32[256,512]{1,0:T(8,128)S(1)}) custom-call(f32[264,128]{1,0:T(8,128)S(1)} %get-tuple-element.19.mine_a, f32[264,128]{1,0:T(8,128)S(1)} %collective-permute-done.got1, f32[264,128]{1,0:T(8,128)S(1)} %collective-permute-done.1.got2.got, ...), custom_call_target="tpu_custom_call" | custom-call | flops 9663676416 | bytes 4878336 | tf_op jit(solution)/shard_map/pallas_call | solution.py:360
  16.8 0.7 %collective-permute-start.7 = (f32[256,512]{1,0:T(8,128)S(1)}, f32[256,512]{1,0:T(8,128)S(1)}, u32[]{:S(2)}, u32[]{:S(2)}) collective-permute-start(f32[256,512]{1,0:T(8,128)S(1)} %get-tuple-element.25), channel_id=1, source_target_pairs={{0,1},{1,0},{2,3},{3,2},{4,5},{5,4},{6,7},{7,6},{8,9},{9,8},{10,11... | collective-permute-start | bytes 1572872 | tf_op jit(solution)/shard_map/ppermute | solution.py:385
  17.5 0.1 collective-permute-start.8
  17.6 1.2 %shard_map.65 = (f32[512,512]{1,0:T(8,128)S(1)}, f32[2,256,256]{2,1,0:T(8,128)S(1)}) custom-call(f32[512,512]{1,0:T(8,128)S(1)} %get-tuple-element.27.quadrant, f32[264,128]{1,0:T(8,128)S(1)} %collective-permute-done.4.got5, f32[264,128]{1,0:T(8,128)S(1)} %collective-permute-done.5.got6, f32[512,512]{1,0:T(8,128)S(1)} %get-tuple-element.28.most, ...), custom_call_target="tpu_custom_call" | custom-call | flops 1073741824 | bytes 7610368 | tf_op jit(solution)/shard_map/pallas_call | solution.py:360
  18.8 0.8 %collective-permute-start.11 = (f32[2,256,256]{2,1,0:T(8,128)S(1)}, f32[2,256,256]{2,1,0:T(8,128)S(1)}, u32[]{:S(2)}, u32[]{:S(2)}) collective-permute-start(f32[2,256,256]{2,1,0:T(8,128)S(1)} %get-tuple-element.33.near), channel_id=1, source_target_pairs={{0,1},{1,0},{2,3},{3,2},{4,5},{5,4},{6,7},{7,6},{8,9},{9,8},{10,11... | collective-permute-start | bytes 1572872 | tf_op jit(solution)/shard_map/ppermute | solution.py:385
  19.6 0.0 collective-permute-done.9.got
  19.6 0.4 %collective-permute-start.10 = (f32[264,128]{1,0:T(8,128)S(1)}, f32[264,128]{1,0:T(8,128)S(1)}, u32[]{:S(2)}, u32[]{:S(2)}) collective-permute-start(f32[264,128]{1,0:T(8,128)S(1)} %shard_map.64.got7), channel_id=1, source_target_pairs={{0,1},{1,0},{2,3},{3,2},{4,5},{5,4},{6,7},{7,6},{8,9},{9,8},{10,11... | collective-permute-start | bytes 405512 | tf_op jit(solution)/shard_map/ppermute | solution.py:385
  20.0 0.0 collective-permute-done.7.early.early_a
  20.0 1.3 %shard_map.66 = (f32[2,256,256]{2,1,0:T(8,128)S(1)}, f32[512,512]{1,0:T(8,128)S(1)}) custom-call(f32[264,128]{1,0:T(8,128)S(1)} %collective-permute-done.got1, f32[264,128]{1,0:T(8,128)S(1)} %collective-permute-done.1.got2.got, f32[264,128]{1,0:T(8,128)S(1)} %collective-permute-done.4.got5, f32[264,128]{1,0:T(8,128)S(1)} %shard_map.64.got7, ...), custom_call_target="tpu_custom_call" | custom-call | flops 1 | bytes 4734976 | tf_op jit(solution)/shard_map/pallas_call | solution.py:360
  21.3 0.0 collective-permute-done.10.late
  21.3 0.0 collective-permute-done.8.early_b
  21.3 0.0 collective-permute-done.11.near_other
  21.3 2.1 %shard_map.67 = (f32[512,512]{1,0:T(8,128)}, f32[2,256,256]{2,1,0:T(8,128)}) custom-call(f32[256,512]{1,0:T(8,128)S(1)} %collective-permute-done.7.early.early_a, f32[256,512]{1,0:T(8,128)S(1)} %collective-permute-done.8.early_b, f32[264,128]{1,0:T(8,128)S(1)} %collective-permute-done.10.late, f32[512,512]{1,0:T(8,128)S(1)} %get-tuple-element.32.partial, ...), custom_call_target="tpu_custom_call" | custom-call | flops 1 | bytes 8523776 | tf_op jit(solution)/shard_map/pallas_call | solution.py:360
  (5 shorter events, 0.0 us)
Async XLA Ops:
  0.6 4.8 %copy-start.1 = (f32[512,512]{1,0:T(8,128)S(1)}, f32[512,512]{1,0:T(8,128)}, u32[]{:S(2)}) copy-start(f32[512,512]{1,0:T(8,128)} %panel.1) | copy-start | bytes 3145732
  0.6 4.8 %copy-start = (f32[2,256,256]{2,1,0:T(8,128)S(1)}, f32[2,256,256]{2,1,0:T(8,128)}, u32[]{:S(2)}) copy-start(f32[2,256,256]{2,1,0:T(8,128)} %diag_inv.3) | copy-start | bytes 1572868
  1.8 6.7 %collective-permute-start = (f32[264,128]{1,0:T(8,128)S(1)}, f32[264,128]{1,0:T(8,128)S(1)}, u32[]{:S(2)}, u32[]{:S(2)}) collective-permute-start(f32[264,128]{1,0:T(8,128)S(1)} %get-tuple-element.19.mine_a), channel_id=1, source_target_pairs={{0,9},{1,3},{2,11},{3,1},{4,13},{5,7},{6,15},{7,5},{8,10},{9,0},{1... | collective-permute-start | bytes 405512 | tf_op jit(solution)/shard_map/ppermute | solution.py:380
  3.9 5.5 %collective-permute-start.3 = (f32[264,128]{1,0:T(8,128)S(1)}, f32[264,128]{1,0:T(8,128)S(1)}, u32[]{:S(2)}, u32[]{:S(2)}) collective-permute-start(f32[264,128]{1,0:T(8,128)S(1)} %get-tuple-element.20.mine_b), channel_id=1, source_target_pairs={{0,4},{1,3},{2,6},{3,1},{4,0},{5,7},{6,2},{7,5},{8,10},{9,13},{10,... | collective-permute-start | bytes 405512 | tf_op jit(solution)/shard_map/ppermute | solution.py:380
  4.0 5.9 %collective-permute-start.1 = (f32[264,128]{1,0:T(8,128)S(1)}, f32[264,128]{1,0:T(8,128)S(1)}, u32[]{:S(2)}, u32[]{:S(2)}) collective-permute-start(f32[264,128]{1,0:T(8,128)S(1)} %get-tuple-element.19.mine_a), channel_id=1, source_target_pairs={{0,13},{1,5},{2,15},{3,7},{4,9},{5,1},{6,11},{7,3},{8,12},{9,4},{1... | collective-permute-start | bytes 405512 | tf_op jit(solution)/shard_map/ppermute | solution.py:380
  6.1 6.6 %collective-permute-start.6 = (f32[512,512]{1,0:T(8,128)S(1)}, f32[512,512]{1,0:T(8,128)S(1)}, u32[]{:S(2)}, u32[]{:S(2)}) collective-permute-start(f32[512,512]{1,0:T(8,128)S(1)} %shard_map.60.factor), channel_id=1, source_target_pairs={{0,1},{1,0},{2,3},{3,2},{4,5},{5,4},{6,7},{7,6},{8,9},{9,8},{10,11... | collective-permute-start | bytes 3145736 | tf_op jit(solution)/shard_map/ppermute | solution.py:385
  7.9 4.8 %collective-permute-start.2 = (f32[264,128]{1,0:T(8,128)S(1)}, f32[264,128]{1,0:T(8,128)S(1)}, u32[]{:S(2)}, u32[]{:S(2)}) collective-permute-start(f32[264,128]{1,0:T(8,128)S(1)} %get-tuple-element.20.mine_b), channel_id=1, source_target_pairs={{0,2},{1,5},{2,0},{3,7},{4,6},{5,1},{6,4},{7,3},{8,12},{9,11},{10,... | collective-permute-start | bytes 405512 | tf_op jit(solution)/shard_map/ppermute | solution.py:380
  8.4 6.3 %collective-permute-start.4 = (f32[264,128]{1,0:T(8,128)S(1)}, f32[264,128]{1,0:T(8,128)S(1)}, u32[]{:S(2)}, u32[]{:S(2)}) collective-permute-start(f32[264,128]{1,0:T(8,128)S(1)} %collective-permute-done.got1), channel_id=1, source_target_pairs={{0,2},{1,5},{2,0},{3,7},{4,6},{5,1},{6,4},{7,3},{8,12},{9,11},{10,... | collective-permute-start | bytes 405512 | tf_op jit(solution)/shard_map/ppermute | solution.py:380
  9.3 7.1 %collective-permute-start.5 = (f32[264,128]{1,0:T(8,128)S(1)}, f32[264,128]{1,0:T(8,128)S(1)}, u32[]{:S(2)}, u32[]{:S(2)}) collective-permute-start(f32[264,128]{1,0:T(8,128)S(1)} %collective-permute-done.3.got4), channel_id=1, source_target_pairs={{0,2},{1,5},{2,0},{3,7},{4,6},{5,1},{6,4},{7,3},{8,12},{9,11},{10,... | collective-permute-start | bytes 405512 | tf_op jit(solution)/shard_map/ppermute | solution.py:380
  9.9 9.7 %collective-permute-start.9 = (f32[264,128]{1,0:T(8,128)S(1)}, f32[264,128]{1,0:T(8,128)S(1)}, u32[]{:S(2)}, u32[]{:S(2)}) collective-permute-start(f32[264,128]{1,0:T(8,128)S(1)} %shard_map.63), channel_id=1, source_target_pairs={{0,2},{1,17},{2,0},{3,19},{4,6},{5,21},{6,4},{7,23},{8,24},{9,11},... | collective-permute-start | bytes 405512 | tf_op jit(solution)/shard_map/ppermute | solution.py:380
  16.8 3.2 %collective-permute-start.7 = (f32[256,512]{1,0:T(8,128)S(1)}, f32[256,512]{1,0:T(8,128)S(1)}, u32[]{:S(2)}, u32[]{:S(2)}) collective-permute-start(f32[256,512]{1,0:T(8,128)S(1)} %get-tuple-element.25), channel_id=1, source_target_pairs={{0,1},{1,0},{2,3},{3,2},{4,5},{5,4},{6,7},{7,6},{8,9},{9,8},{10,11... | collective-permute-start | bytes 1572872 | tf_op jit(solution)/shard_map/ppermute | solution.py:385
  17.5 3.8 %collective-permute-start.8 = (f32[256,512]{1,0:T(8,128)S(1)}, f32[256,512]{1,0:T(8,128)S(1)}, u32[]{:S(2)}, u32[]{:S(2)}) collective-permute-start(f32[256,512]{1,0:T(8,128)S(1)} %get-tuple-element.26), channel_id=1, source_target_pairs={{0,1},{1,0},{2,3},{3,2},{4,5},{5,4},{6,7},{7,6},{8,9},{9,8},{10,11... | collective-permute-start | bytes 1572872 | tf_op jit(solution)/shard_map/ppermute | solution.py:385
  18.8 2.5 %collective-permute-start.11 = (f32[2,256,256]{2,1,0:T(8,128)S(1)}, f32[2,256,256]{2,1,0:T(8,128)S(1)}, u32[]{:S(2)}, u32[]{:S(2)}) collective-permute-start(f32[2,256,256]{2,1,0:T(8,128)S(1)} %get-tuple-element.33.near), channel_id=1, source_target_pairs={{0,1},{1,0},{2,3},{3,2},{4,5},{5,4},{6,7},{7,6},{8,9},{9,8},{10,11... | collective-permute-start | bytes 1572872 | tf_op jit(solution)/shard_map/ppermute | solution.py:385
  19.6 1.7 %collective-permute-start.10 = (f32[264,128]{1,0:T(8,128)S(1)}, f32[264,128]{1,0:T(8,128)S(1)}, u32[]{:S(2)}, u32[]{:S(2)}) collective-permute-start(f32[264,128]{1,0:T(8,128)S(1)} %shard_map.64.got7), channel_id=1, source_target_pairs={{0,1},{1,0},{2,3},{3,2},{4,5},{5,4},{6,7},{7,6},{8,9},{9,8},{10,11... | collective-permute-start | bytes 405512 | tf_op jit(solution)/shard_map/ppermute | solution.py:385

commit v7 on v6

--- a/solution.py
+++ b/solution.py
@@ -30,7 +30,7 @@
 FIRST = ((0,), (0,))
 
 
-def factor_kernel(mask, panel, diag_inv, factor):
+def factor_kernel(mask, panel, diag_inv, factor, own_high, own_low):
     children, width = diag_inv.shape[:2]
     here = mask.shape[0] // children
     block = panel.shape[0] // here
@@ -39,7 +39,9 @@
         masked = jnp.concatenate(
             [panel[pl.ds(r * block, block), columns] * mask[pl.ds(j * here + r, 1), :] for r in range(here)], axis=0
         )
-        factor[:, columns] = product(split(masked), split(diag_inv[j]), PLAIN)
+        rows = product(split(masked), split(diag_inv[j]), PLAIN)
+        factor[:, columns] = rows
+        own_high[:, columns], own_low[:, columns] = split(rows)
 
 
 def own_place():
@@ -173,7 +175,7 @@
 
     @pl.when(jnp.logical_not(diagonal))
     def _():
-        last = product(split(row_of(got5, got6)), (far_high[...], far_low[...]), PLAIN)
+        last = joined(split(row_of(got5, got6)), (far_high[...], far_low[...]), PLAIN)
         sent_a[...] = products[pl.ds(0, rows), :]
         sent_b[pl.ds(0, block), :] = products[pl.ds(rows, block), :]
         sent_b[pl.ds(block, block), :] = last
@@ -217,7 +219,7 @@
 
 
 def near_kernel(
-    quadrant, got5, got6, most, factor, factor_other, turned_high, turned_low, own_part, partial, cross
+    quadrant, got5, got6, most, own_high, own_low, factor_other, turned_high, turned_low, own_part, partial, cross
 ):
     place, diagonal = own_place()
     across = places(place)[2]
@@ -225,7 +227,7 @@
 
     @pl.when(diagonal)
     def _():
-        own = split(factor[...])
+        own = own_high[...], own_low[...]
         partial[...] = product(split(quadrant[...]), own, PLAIN)
         value = split(partial[...])
         for j in range(cross.shape[0]):
@@ -234,7 +236,7 @@
     @pl.when(jnp.logical_not(diagonal))
     def _():
         factors = split(factor_other[at(across, got5.shape[1]), :])
-        partial[...] = most[...] + product(split(row_of(got5, got6)), factors, FIRST)
+        partial[...] = most[...] + joined(split(row_of(got5, got6)), factors, FIRST)
         value = split(partial[...])
         for j in range(cross.shape[0]):
             rows = pl.ds(j * width, width)
@@ -331,20 +333,25 @@
         following, opposite, top, ends = parts(late)
         own = split(unfolded(top[...], ends[pl.ds(0, 1), :]))
         following, opposite = split(following[...]), split(opposite[...])
-        total[...] = first[...]
-        total[at(across, block), :] += joined(own, factors(at(across, block)), PLAIN) + joined(
-            following, factors(at(after, block)), PLAIN
-        )
-        total[at(after, block), :] += joined(following, factors(at(across, block)), FIRST)
+        def finish(where, c, last):
+            rows = at(where, block)
+            sigma_here[rows, :] = -(partial[rows, :] + last)
+            store(rows, c).start()
+            total[rows, :] = last
+
+        beyond, facing = lax.rem(across + 3, 4), lax.rem(across + 2, 4)
+        finish(beyond, 0, first[at(beyond, block), :])
+        here = factors(at(across, block))
+        finish(after, 1, first[at(after, block), :] + joined(following, here, FIRST))
+        rows = tuple(jnp.concatenate(pair, axis=1) for pair in zip(own, following))
+        there = tuple(jnp.concatenate(pair, axis=0) for pair in zip(here, factors(at(after, block))))
+        total[at(across, block), :] = first[at(across, block), :] + joined(rows, there, PLAIN)
+        total[at(facing, block), :] = first[at(facing, block), :]
         total[piece_rows, :] += joined(opposite, factors(at(low + 2, block)), PLAIN)
         total[at(low + 2, block), :] += joined(opposite, factors(piece_rows), FIRST)
-        values = []
-        for c, rows in enumerate(chunks):
-            last = total[rows, :]
-            sigma_here[rows, :] = -(partial[rows, :] + last)
-            store(rows, c).start()
-            values.append(split(last))
-        value = tuple(jnp.concatenate(rows, axis=0) for rows in zip(*values))
+        finish(across, 2, total[at(across, block), :])
+        finish(facing, 3, total[at(facing, block), :])
+        value = split(total[...])
         for j in children:
             turned = pl.ds(j * width, width)
             inner = product((turned_high[turned, :], turned_low[turned, :]), columns_of(value, j, width), PLAIN)
@@ -420,10 +427,10 @@
     got6 = permute(got4, mesh, 1, 2)
     (got2_again,) = call(again_kernel, [shape(size, block)], 40 * step, got2)
     got7 = permute(got2_again, mesh, 1)
-    (got7,) = call(again_kernel, [shape(size, block)], 16 * step, got7)
-    (factor,) = call(
+    (got7_again,) = call(again_kernel, [shape(size, block)], 16 * step, got7)
+    factor, *own_factor = call(
         factor_kernel,
-        [panel],
+        [panel, *halves],
         1,
         mask,
         panel_l,
@@ -447,7 +454,7 @@
         near_kernel,
         [panel, children],
         4 * step,
-        own_half, got5, got6, most, factor, factor_other, *far_rows[2:], own_part,
+        own_half, got5, got6, most, *own_factor, factor_other, *far_rows[2:], own_part,
     )
     near_other = exchange(near, mesh)
     late = exchange(got7, mesh)
@@ -455,7 +462,7 @@
         far_kernel,
         [children, panel],
         1,
-        got1, got2, got5, got7, early_a, *far_rows,
+        got1, got2, got5, got7_again, early_a, *far_rows,
         scratch=[pltpu.VMEM(square.shape, f32)],
     )
     return tuple(

time: 23.6 us -> 23.6 us (level)
  no operation moved by 1% of the time
where the time goes in v7:
time: 23.6 us; the launch traced here: 23.4 us
  starting transfers between devices  11.4 us (48%)
  Pallas kernels  8.54 us (36%)
  waiting for transfers between devices  2.71 us (11%)
  between operations  0.71 us (3%)
    pallas_call x9, Pallas kernels, call(): pl.pallas_call(kernel, out_shape=out_shapes, in_specs=specs or [VMEM] * l...  8.54 us
    ppermute x7, starting transfers between devices, permute(): return lax.ppermute(value, AXES, pairs)  7.61 us
    ppermute x5, starting transfers between devices, exchange(): lax.ppermute(value, AXES, [(d, d ^ 1) for d in range(cfgs * prows * cores)])  3.8 us
    ppermute x7, waiting for transfers between devices, permute(): return lax.ppermute(value, AXES, pairs)  2.65 us
  transfers between devices with their start and end apart: 12, of which 3 were waited for; matrix products, arithmetic and copies ran while one was open for 0% of the time, Pallas kernels for 23%

profile of v7, /device:TPU:1, one launch (start us, length us, event | category | flops | bytes accessed | tf_op | source)
XLA Modules:
  0.0 23.4 jit_solution(11206264005816406252)
XLA Ops:
  0.6 0.0 copy-start.1
  0.7 1.1 %shard_map.59 = (f32[264,128]{1,0:T(8,128)S(1)}, f32[264,128]{1,0:T(8,128)S(1)}, f32[8,256]{1,0:T(8,128)S(1)}) custom-call(f32[128,512]{1,0:T(8,128)} %sigma_top.1, s32[2,8]{1,0:T(2,128)} %pattern.1), custom_call_target="tpu_custom_call" | custom-call | flops 10737418240 | bytes 540736 | tf_op jit(solution)/shard_map/pallas_call | solution.py:367
  1.8 2.1 %collective-permute-start = (f32[264,128]{1,0:T(8,128)S(1)}, f32[264,128]{1,0:T(8,128)S(1)}, u32[]{:S(2)}, u32[]{:S(2)}) collective-permute-start(f32[264,128]{1,0:T(8,128)S(1)} %get-tuple-element.22.mine_a), channel_id=1, source_target_pairs={{0,9},{1,3},{2,11},{3,1},{4,13},{5,7},{6,15},{7,5},{8,10},{9,0},{1... | collective-permute-start | bytes 405512 | tf_op jit(solution)/shard_map/ppermute | solution.py:387
  3.9 0.1 collective-permute-start.3
  4.0 1.5 %collective-permute-start.1 = (f32[264,128]{1,0:T(8,128)S(1)}, f32[264,128]{1,0:T(8,128)S(1)}, u32[]{:S(2)}, u32[]{:S(2)}) collective-permute-start(f32[264,128]{1,0:T(8,128)S(1)} %get-tuple-element.22.mine_a), channel_id=1, source_target_pairs={{0,13},{1,5},{2,15},{3,7},{4,9},{5,1},{6,11},{7,3},{8,12},{9,4},{1... | collective-permute-start | bytes 405512 | tf_op jit(solution)/shard_map/ppermute | solution.py:387
  5.4 0.6 %shard_map.60 = (f32[512,512]{1,0:T(8,128)S(1)}, bf16[512,512]{1,0:T(8,128)(2,1)S(1)}, bf16[512,512]{1,0:T(8,128)(2,1)S(1)}) custom-call(f32[8,256]{1,0:T(8,128)S(1)} %get-tuple-element.24.mask, f32[512,512]{1,0:T(8,128)S(1)} %copy-done.1, f32[2,256,256]{2,1,0:T(8,128)S(1)} %copy-done), custom_call_target="tpu_custom_call" | custom-call | flops 1 | bytes 3678208 | tf_op jit(solution)/shard_map/pallas_call | solution.py:367
  6.1 1.8 %collective-permute-start.6 = (f32[512,512]{1,0:T(8,128)S(1)}, f32[512,512]{1,0:T(8,128)S(1)}, u32[]{:S(2)}, u32[]{:S(2)}) collective-permute-start(f32[512,512]{1,0:T(8,128)S(1)} %get-tuple-element.25.factor), channel_id=1, source_target_pairs={{0,1},{1,0},{2,3},{3,2},{4,5},{5,4},{6,7},{7,6},{8,9},{9,8},{10,11... | collective-permute-start | bytes 3145736 | tf_op jit(solution)/shard_map/ppermute | solution.py:392
  7.9 0.6 %collective-permute-start.2 = (f32[264,128]{1,0:T(8,128)S(1)}, f32[264,128]{1,0:T(8,128)S(1)}, u32[]{:S(2)}, u32[]{:S(2)}) collective-permute-start(f32[264,128]{1,0:T(8,128)S(1)} %get-tuple-element.23.mine_b), channel_id=1, source_target_pairs={{0,2},{1,5},{2,0},{3,7},{4,6},{5,1},{6,4},{7,3},{8,12},{9,11},{10,... | collective-permute-start | bytes 405512 | tf_op jit(solution)/shard_map/ppermute | solution.py:387
  8.4 0.0 collective-permute-done.got1
  8.5 0.9 %collective-permute-start.4 = (f32[264,128]{1,0:T(8,128)S(1)}, f32[264,128]{1,0:T(8,128)S(1)}, u32[]{:S(2)}, u32[]{:S(2)}) collective-permute-start(f32[264,128]{1,0:T(8,128)S(1)} %collective-permute-done.got1), channel_id=1, source_target_pairs={{0,2},{1,5},{2,0},{3,7},{4,6},{5,1},{6,4},{7,3},{8,12},{9,11},{10,... | collective-permute-start | bytes 405512 | tf_op jit(solution)/shard_map/ppermute | solution.py:387
  9.4 0.0 collective-permute-done.3.got4
  9.4 0.6 %collective-permute-start.5 = (f32[264,128]{1,0:T(8,128)S(1)}, f32[264,128]{1,0:T(8,128)S(1)}, u32[]{:S(2)}, u32[]{:S(2)}) collective-permute-start(f32[264,128]{1,0:T(8,128)S(1)} %collective-permute-done.3.got4), channel_id=1, source_target_pairs={{0,2},{1,5},{2,0},{3,7},{4,6},{5,1},{6,4},{7,3},{8,12},{9,11},{10,... | collective-permute-start | bytes 405512 | tf_op jit(solution)/shard_map/ppermute | solution.py:387
  9.9 0.0 collective-permute-done.1.got2.got
  9.9 1.9 %collective-permute-start.9 = (f32[264,128]{1,0:T(8,128)S(1)}, f32[264,128]{1,0:T(8,128)S(1)}, u32[]{:S(2)}, u32[]{:S(2)}) collective-permute-start(f32[264,128]{1,0:T(8,128)S(1)} %shard_map.63), channel_id=1, source_target_pairs={{0,2},{1,17},{2,0},{3,19},{4,6},{5,21},{6,4},{7,23},{8,24},{9,11},... | collective-permute-start | bytes 405512 | tf_op jit(solution)/shard_map/ppermute | solution.py:387
  11.9 0.8 %collective-permute-done.2.got3 = f32[264,128]{1,0:T(8,128)S(1)} collective-permute-done((f32[264,128]{1,0:T(8,128)S(1)}, f32[264,128]{1,0:T(8,128)S(1)}, u32[]{:S(2)}, u32[]{:S(2)}) %collective-permute-start.2) | collective-permute-done | bytes 135200 | tf_op jit(solution)/shard_map/ppermute | solution.py:387
  12.7 0.0 collective-permute-done.6.factor_other
  12.7 1.9 %shard_map.61 = (bf16[512,512]{1,0:T(8,128)(2,1)S(1)}, bf16[512,512]{1,0:T(8,128)(2,1)S(1)}, bf16[512,512]{1,0:T(8,128)(2,1)S(1)}, bf16[512,512]{1,0:T(8,128)(2,...) custom-call(f32[264,128]{1,0:T(8,128)S(1)} %get-tuple-element.22.mine_a, ...), custom_call_target="tpu_custom_call" | custom-call | flops 1 | bytes 7888896 | tf_op jit(solution)/shard_map/pallas_call | solution.py:367
  14.6 0.1 collective-permute-done.4.got5
  14.7 1.7 %collective-permute-done.5.got6 = f32[264,128]{1,0:T(8,128)S(1)} collective-permute-done((f32[264,128]{1,0:T(8,128)S(1)}, f32[264,128]{1,0:T(8,128)S(1)}, u32[]{:S(2)}, u32[]{:S(2)}) %collective-permute-start.5) | collective-permute-done | bytes 135200 | tf_op jit(solution)/shard_map/ppermute | solution.py:387
  16.4 0.4 %shard_map.62 = (f32[512,512]{1,0:T(8,128)S(1)}, f32[256,512]{1,0:T(8,128)S(1)}, f32[256,512]{1,0:T(8,128)S(1)}) custom-call(f32[264,128]{1,0:T(8,128)S(1)} %get-tuple-element.22.mine_a, f32[264,128]{1,0:T(8,128)S(1)} %collective-permute-done.got1, f32[264,128]{1,0:T(8,128)S(1)} %collective-permute-done.1.got2.got, ...), custom_call_target="tpu_custom_call" | custom-call | flops 9663676416 | bytes 4878336 | tf_op jit(solution)/shard_map/pallas_call | solution.py:367
  16.8 0.7 %collective-permute-start.7 = (f32[256,512]{1,0:T(8,128)S(1)}, f32[256,512]{1,0:T(8,128)S(1)}, u32[]{:S(2)}, u32[]{:S(2)}) collective-permute-start(f32[256,512]{1,0:T(8,128)S(1)} %get-tuple-element.29), channel_id=1, source_target_pairs={{0,1},{1,0},{2,3},{3,2},{4,5},{5,4},{6,7},{7,6},{8,9},{9,8},{10,11... | collective-permute-start | bytes 1572872 | tf_op jit(solution)/shard_map/ppermute | solution.py:392
  17.5 0.1 collective-permute-start.8
  17.6 1.1 %shard_map.64 = (f32[512,512]{1,0:T(8,128)S(1)}, f32[2,256,256]{2,1,0:T(8,128)S(1)}) custom-call(f32[512,512]{1,0:T(8,128)S(1)} %get-tuple-element.31.quadrant, f32[264,128]{1,0:T(8,128)S(1)} %collective-permute-done.4.got5, f32[264,128]{1,0:T(8,128)S(1)} %collective-permute-done.5.got6, f32[512,512]{1,0:T(8,128)S(1)} %get-tuple-element.32.most, ...), custom_call_target="tpu_custom_call" | custom-call | flops 1073741824 | bytes 7610368 | tf_op jit(solution)/shard_map/pallas_call | solution.py:367
  18.7 0.9 %collective-permute-start.11 = (f32[2,256,256]{2,1,0:T(8,128)S(1)}, f32[2,256,256]{2,1,0:T(8,128)S(1)}, u32[]{:S(2)}, u32[]{:S(2)}) collective-permute-start(f32[2,256,256]{2,1,0:T(8,128)S(1)} %get-tuple-element.39.near), channel_id=1, source_target_pairs={{0,1},{1,0},{2,3},{3,2},{4,5},{5,4},{6,7},{7,6},{8,9},{9,8},{10,11... | collective-permute-start | bytes 1572872 | tf_op jit(solution)/shard_map/ppermute | solution.py:392
  19.6 0.0 collective-permute-done.9.got
  19.6 0.4 %collective-permute-start.10 = (f32[264,128]{1,0:T(8,128)S(1)}, f32[264,128]{1,0:T(8,128)S(1)}, u32[]{:S(2)}, u32[]{:S(2)}) collective-permute-start(f32[264,128]{1,0:T(8,128)S(1)} %collective-permute-done.9.got), channel_id=1, source_target_pairs={{0,1},{1,0},{2,3},{3,2},{4,5},{5,4},{6,7},{7,6},{8,9},{9,8},{10,11... | collective-permute-start | bytes 405512 | tf_op jit(solution)/shard_map/ppermute | solution.py:392
  20.0 0.0 collective-permute-done.7.early.early_a
  20.0 1.3 %shard_map.66 = (f32[2,256,256]{2,1,0:T(8,128)S(1)}, f32[512,512]{1,0:T(8,128)S(1)}) custom-call(f32[264,128]{1,0:T(8,128)S(1)} %collective-permute-done.got1, f32[264,128]{1,0:T(8,128)S(1)} %collective-permute-done.1.got2.got, f32[264,128]{1,0:T(8,128)S(1)} %collective-permute-done.4.got5, f32[264,128]{1,0:T(8,128)S(1)} %shard_map.65.got7, ...), custom_call_target="tpu_custom_call" | custom-call | flops 1 | bytes 4734976 | tf_op jit(solution)/shard_map/pallas_call | solution.py:367
  21.2 0.0 collective-permute-done.10.late
  21.3 0.0 collective-permute-done.8.early_b
  21.3 0.0 collective-permute-done.11.near_other
  21.3 2.1 %shard_map.67 = (f32[512,512]{1,0:T(8,128)}, f32[2,256,256]{2,1,0:T(8,128)}) custom-call(f32[256,512]{1,0:T(8,128)S(1)} %collective-permute-done.7.early.early_a, f32[256,512]{1,0:T(8,128)S(1)} %collective-permute-done.8.early_b, f32[264,128]{1,0:T(8,128)S(1)} %collective-permute-done.10.late, f32[512,512]{1,0:T(8,128)S(1)} %get-tuple-element.38.partial, ...), custom_call_target="tpu_custom_call" | custom-call | flops 1 | bytes 8523776 | tf_op jit(solution)/shard_map/pallas_call | solution.py:367
  (5 shorter events, 0.0 us)
Async XLA Ops:
  0.6 4.8 %copy-start.1 = (f32[512,512]{1,0:T(8,128)S(1)}, f32[512,512]{1,0:T(8,128)}, u32[]{:S(2)}) copy-start(f32[512,512]{1,0:T(8,128)} %panel.1) | copy-start | bytes 3145732
  0.6 4.8 %copy-start = (f32[2,256,256]{2,1,0:T(8,128)S(1)}, f32[2,256,256]{2,1,0:T(8,128)}, u32[]{:S(2)}) copy-start(f32[2,256,256]{2,1,0:T(8,128)} %diag_inv.3) | copy-start | bytes 1572868
  1.8 6.7 %collective-permute-start = (f32[264,128]{1,0:T(8,128)S(1)}, f32[264,128]{1,0:T(8,128)S(1)}, u32[]{:S(2)}, u32[]{:S(2)}) collective-permute-start(f32[264,128]{1,0:T(8,128)S(1)} %get-tuple-element.22.mine_a), channel_id=1, source_target_pairs={{0,9},{1,3},{2,11},{3,1},{4,13},{5,7},{6,15},{7,5},{8,10},{9,0},{1... | collective-permute-start | bytes 405512 | tf_op jit(solution)/shard_map/ppermute | solution.py:387
  3.9 5.5 %collective-permute-start.3 = (f32[264,128]{1,0:T(8,128)S(1)}, f32[264,128]{1,0:T(8,128)S(1)}, u32[]{:S(2)}, u32[]{:S(2)}) collective-permute-start(f32[264,128]{1,0:T(8,128)S(1)} %get-tuple-element.23.mine_b), channel_id=1, source_target_pairs={{0,4},{1,3},{2,6},{3,1},{4,0},{5,7},{6,2},{7,5},{8,10},{9,13},{10,... | collective-permute-start | bytes 405512 | tf_op jit(solution)/shard_map/ppermute | solution.py:387
  4.0 6.0 %collective-permute-start.1 = (f32[264,128]{1,0:T(8,128)S(1)}, f32[264,128]{1,0:T(8,128)S(1)}, u32[]{:S(2)}, u32[]{:S(2)}) collective-permute-start(f32[264,128]{1,0:T(8,128)S(1)} %get-tuple-element.22.mine_a), channel_id=1, source_target_pairs={{0,13},{1,5},{2,15},{3,7},{4,9},{5,1},{6,11},{7,3},{8,12},{9,4},{1... | collective-permute-start | bytes 405512 | tf_op jit(solution)/shard_map/ppermute | solution.py:387
  6.1 6.6 %collective-permute-start.6 = (f32[512,512]{1,0:T(8,128)S(1)}, f32[512,512]{1,0:T(8,128)S(1)}, u32[]{:S(2)}, u32[]{:S(2)}) collective-permute-start(f32[512,512]{1,0:T(8,128)S(1)} %get-tuple-element.25.factor), channel_id=1, source_target_pairs={{0,1},{1,0},{2,3},{3,2},{4,5},{5,4},{6,7},{7,6},{8,9},{9,8},{10,11... | collective-permute-start | bytes 3145736 | tf_op jit(solution)/shard_map/ppermute | solution.py:392
  7.9 4.8 %collective-permute-start.2 = (f32[264,128]{1,0:T(8,128)S(1)}, f32[264,128]{1,0:T(8,128)S(1)}, u32[]{:S(2)}, u32[]{:S(2)}) collective-permute-start(f32[264,128]{1,0:T(8,128)S(1)} %get-tuple-element.23.mine_b), channel_id=1, source_target_pairs={{0,2},{1,5},{2,0},{3,7},{4,6},{5,1},{6,4},{7,3},{8,12},{9,11},{10,... | collective-permute-start | bytes 405512 | tf_op jit(solution)/shard_map/ppermute | solution.py:387
  8.5 6.2 %collective-permute-start.4 = (f32[264,128]{1,0:T(8,128)S(1)}, f32[264,128]{1,0:T(8,128)S(1)}, u32[]{:S(2)}, u32[]{:S(2)}) collective-permute-start(f32[264,128]{1,0:T(8,128)S(1)} %collective-permute-done.got1), channel_id=1, source_target_pairs={{0,2},{1,5},{2,0},{3,7},{4,6},{5,1},{6,4},{7,3},{8,12},{9,11},{10,... | collective-permute-start | bytes 405512 | tf_op jit(solution)/shard_map/ppermute | solution.py:387
  9.4 7.1 %collective-permute-start.5 = (f32[264,128]{1,0:T(8,128)S(1)}, f32[264,128]{1,0:T(8,128)S(1)}, u32[]{:S(2)}, u32[]{:S(2)}) collective-permute-start(f32[264,128]{1,0:T(8,128)S(1)} %collective-permute-done.3.got4), channel_id=1, source_target_pairs={{0,2},{1,5},{2,0},{3,7},{4,6},{5,1},{6,4},{7,3},{8,12},{9,11},{10,... | collective-permute-start | bytes 405512 | tf_op jit(solution)/shard_map/ppermute | solution.py:387
  9.9 9.6 %collective-permute-start.9 = (f32[264,128]{1,0:T(8,128)S(1)}, f32[264,128]{1,0:T(8,128)S(1)}, u32[]{:S(2)}, u32[]{:S(2)}) collective-permute-start(f32[264,128]{1,0:T(8,128)S(1)} %shard_map.63), channel_id=1, source_target_pairs={{0,2},{1,17},{2,0},{3,19},{4,6},{5,21},{6,4},{7,23},{8,24},{9,11},... | collective-permute-start | bytes 405512 | tf_op jit(solution)/shard_map/ppermute | solution.py:387
  16.8 3.1 %collective-permute-start.7 = (f32[256,512]{1,0:T(8,128)S(1)}, f32[256,512]{1,0:T(8,128)S(1)}, u32[]{:S(2)}, u32[]{:S(2)}) collective-permute-start(f32[256,512]{1,0:T(8,128)S(1)} %get-tuple-element.29), channel_id=1, source_target_pairs={{0,1},{1,0},{2,3},{3,2},{4,5},{5,4},{6,7},{7,6},{8,9},{9,8},{10,11... | collective-permute-start | bytes 1572872 | tf_op jit(solution)/shard_map/ppermute | solution.py:392
  17.5 3.8 %collective-permute-start.8 = (f32[256,512]{1,0:T(8,128)S(1)}, f32[256,512]{1,0:T(8,128)S(1)}, u32[]{:S(2)}, u32[]{:S(2)}) collective-permute-start(f32[256,512]{1,0:T(8,128)S(1)} %get-tuple-element.30), channel_id=1, source_target_pairs={{0,1},{1,0},{2,3},{3,2},{4,5},{5,4},{6,7},{7,6},{8,9},{9,8},{10,11... | collective-permute-start | bytes 1572872 | tf_op jit(solution)/shard_map/ppermute | solution.py:392
  18.7 2.6 %collective-permute-start.11 = (f32[2,256,256]{2,1,0:T(8,128)S(1)}, f32[2,256,256]{2,1,0:T(8,128)S(1)}, u32[]{:S(2)}, u32[]{:S(2)}) collective-permute-start(f32[2,256,256]{2,1,0:T(8,128)S(1)} %get-tuple-element.39.near), channel_id=1, source_target_pairs={{0,1},{1,0},{2,3},{3,2},{4,5},{5,4},{6,7},{7,6},{8,9},{9,8},{10,11... | collective-permute-start | bytes 1572872 | tf_op jit(solution)/shard_map/ppermute | solution.py:392
  19.6 1.7 %collective-permute-start.10 = (f32[264,128]{1,0:T(8,128)S(1)}, f32[264,128]{1,0:T(8,128)S(1)}, u32[]{:S(2)}, u32[]{:S(2)}) collective-permute-start(f32[264,128]{1,0:T(8,128)S(1)} %collective-permute-done.9.got), channel_id=1, source_target_pairs={{0,1},{1,0},{2,3},{3,2},{4,5},{5,4},{6,7},{7,6},{8,9},{9,8},{10,11... | collective-permute-start | bytes 405512 | tf_op jit(solution)/shard_map/ppermute | solution.py:392

commit v8 on v7

--- a/solution.py
+++ b/solution.py
@@ -288,7 +288,14 @@
 
     @pl.when(jnp.logical_not(diagonal))
     def _():
-        quadrant[...] = jnp.zeros_like(quadrant)
+        block = got1.shape[1]
+        half, low = block // 2, lax.rem(across, 2)
+        nothing = jnp.zeros((block, block), jnp.float32)
+        quadrant[at(across, block), at(across, block)] = nothing
+        quadrant[at(across, block), at(lax.rem(across + 1, 4), block)] = nothing
+        quadrant[
+            pl.ds(pl.multiple_of(low * block + lax.div(across, 2) * half, half), half), at(low + 2, block)
+        ] = nothing[:half]
         symmetric(quadrant, zip(early_parts(early, got1.shape[1]), (place, beside, over)))
         first[...] = product(split(quadrant[...]), (far_high[...], far_low[...]), PLAIN)
 

time: 23.6 us -> 23.6 us (level)
  no operation moved by 1% of the time
where the time goes in v8:
time: 23.6 us; the launch traced here: 23.4 us
  starting transfers between devices  11.4 us (48%)
  Pallas kernels  8.55 us (36%)
  waiting for transfers between devices  2.7 us (11%)
  between operations  0.71 us (3%)
    pallas_call x9, Pallas kernels, call(): pl.pallas_call(kernel, out_shape=out_shapes, in_specs=specs or [VMEM] * l...  8.55 us
    ppermute x7, starting transfers between devices, permute(): return lax.ppermute(value, AXES, pairs)  7.61 us
    ppermute x5, starting transfers between devices, exchange(): lax.ppermute(value, AXES, [(d, d ^ 1) for d in range(cfgs * prows * cores)])  3.8 us
    ppermute x7, waiting for transfers between devices, permute(): return lax.ppermute(value, AXES, pairs)  2.65 us
  transfers between devices with their start and end apart: 12, of which 3 were waited for; matrix products, arithmetic and copies ran while one was open for 0% of the time, Pallas kernels for 23%

profile of v8, /device:TPU:1, one launch (start us, length us, event | category | flops | bytes accessed | tf_op | source)
XLA Modules:
  0.0 23.4 jit_solution(10420040726230949234)
XLA Ops:
  0.7 1.1 %shard_map.59 = (f32[264,128]{1,0:T(8,128)S(1)}, f32[264,128]{1,0:T(8,128)S(1)}, f32[8,256]{1,0:T(8,128)S(1)}) custom-call(f32[128,512]{1,0:T(8,128)} %sigma_top.1, s32[2,8]{1,0:T(2,128)} %pattern.1), custom_call_target="tpu_custom_call" | custom-call | flops 10737418240 | bytes 540736 | tf_op jit(solution)/shard_map/pallas_call | solution.py:374
  1.8 2.1 %collective-permute-start = (f32[264,128]{1,0:T(8,128)S(1)}, f32[264,128]{1,0:T(8,128)S(1)}, u32[]{:S(2)}, u32[]{:S(2)}) collective-permute-start(f32[264,128]{1,0:T(8,128)S(1)} %get-tuple-element.22.mine_a), channel_id=1, source_target_pairs={{0,9},{1,3},{2,11},{3,1},{4,13},{5,7},{6,15},{7,5},{8,10},{9,0},{1... | collective-permute-start | bytes 405512 | tf_op jit(solution)/shard_map/ppermute | solution.py:394
  3.9 0.1 collective-permute-start.3
  4.0 1.5 %collective-permute-start.1 = (f32[264,128]{1,0:T(8,128)S(1)}, f32[264,128]{1,0:T(8,128)S(1)}, u32[]{:S(2)}, u32[]{:S(2)}) collective-permute-start(f32[264,128]{1,0:T(8,128)S(1)} %get-tuple-element.22.mine_a), channel_id=1, source_target_pairs={{0,13},{1,5},{2,15},{3,7},{4,9},{5,1},{6,11},{7,3},{8,12},{9,4},{1... | collective-permute-start | bytes 405512 | tf_op jit(solution)/shard_map/ppermute | solution.py:394
  5.4 0.0 copy-done.1
  5.4 0.6 %shard_map.60 = (f32[512,512]{1,0:T(8,128)S(1)}, bf16[512,512]{1,0:T(8,128)(2,1)S(1)}, bf16[512,512]{1,0:T(8,128)(2,1)S(1)}) custom-call(f32[8,256]{1,0:T(8,128)S(1)} %get-tuple-element.24.mask, f32[512,512]{1,0:T(8,128)S(1)} %copy-done.1, f32[2,256,256]{2,1,0:T(8,128)S(1)} %copy-done), custom_call_target="tpu_custom_call" | custom-call | flops 1 | bytes 3678208 | tf_op jit(solution)/shard_map/pallas_call | solution.py:374
  6.1 1.8 %collective-permute-start.6 = (f32[512,512]{1,0:T(8,128)S(1)}, f32[512,512]{1,0:T(8,128)S(1)}, u32[]{:S(2)}, u32[]{:S(2)}) collective-permute-start(f32[512,512]{1,0:T(8,128)S(1)} %get-tuple-element.25.factor), channel_id=1, source_target_pairs={{0,1},{1,0},{2,3},{3,2},{4,5},{5,4},{6,7},{7,6},{8,9},{9,8},{10,11... | collective-permute-start | bytes 3145736 | tf_op jit(solution)/shard_map/ppermute | solution.py:399
  7.9 0.6 %collective-permute-start.2 = (f32[264,128]{1,0:T(8,128)S(1)}, f32[264,128]{1,0:T(8,128)S(1)}, u32[]{:S(2)}, u32[]{:S(2)}) collective-permute-start(f32[264,128]{1,0:T(8,128)S(1)} %get-tuple-element.23.mine_b), channel_id=1, source_target_pairs={{0,2},{1,5},{2,0},{3,7},{4,6},{5,1},{6,4},{7,3},{8,12},{9,11},{10,... | collective-permute-start | bytes 405512 | tf_op jit(solution)/shard_map/ppermute | solution.py:394
  8.4 0.0 collective-permute-done.got1
  8.5 0.9 %collective-permute-start.4 = (f32[264,128]{1,0:T(8,128)S(1)}, f32[264,128]{1,0:T(8,128)S(1)}, u32[]{:S(2)}, u32[]{:S(2)}) collective-permute-start(f32[264,128]{1,0:T(8,128)S(1)} %collective-permute-done.got1), channel_id=1, source_target_pairs={{0,2},{1,5},{2,0},{3,7},{4,6},{5,1},{6,4},{7,3},{8,12},{9,11},{10,... | collective-permute-start | bytes 405512 | tf_op jit(solution)/shard_map/ppermute | solution.py:394
  9.4 0.0 collective-permute-done.3.got4
  9.4 0.6 %collective-permute-start.5 = (f32[264,128]{1,0:T(8,128)S(1)}, f32[264,128]{1,0:T(8,128)S(1)}, u32[]{:S(2)}, u32[]{:S(2)}) collective-permute-start(f32[264,128]{1,0:T(8,128)S(1)} %collective-permute-done.3.got4), channel_id=1, source_target_pairs={{0,2},{1,5},{2,0},{3,7},{4,6},{5,1},{6,4},{7,3},{8,12},{9,11},{10,... | collective-permute-start | bytes 405512 | tf_op jit(solution)/shard_map/ppermute | solution.py:394
  9.9 0.0 collective-permute-done.1.got2.got
  9.9 1.9 %collective-permute-start.9 = (f32[264,128]{1,0:T(8,128)S(1)}, f32[264,128]{1,0:T(8,128)S(1)}, u32[]{:S(2)}, u32[]{:S(2)}) collective-permute-start(f32[264,128]{1,0:T(8,128)S(1)} %shard_map.63), channel_id=1, source_target_pairs={{0,2},{1,17},{2,0},{3,19},{4,6},{5,21},{6,4},{7,23},{8,24},{9,11},... | collective-permute-start | bytes 405512 | tf_op jit(solution)/shard_map/ppermute | solution.py:394
  11.9 0.8 %collective-permute-done.2.got3 = f32[264,128]{1,0:T(8,128)S(1)} collective-permute-done((f32[264,128]{1,0:T(8,128)S(1)}, f32[264,128]{1,0:T(8,128)S(1)}, u32[]{:S(2)}, u32[]{:S(2)}) %collective-permute-start.2) | collective-permute-done | bytes 135200 | tf_op jit(solution)/shard_map/ppermute | solution.py:394
  12.7 0.0 collective-permute-done.6.factor_other
  12.7 1.9 %shard_map.61 = (bf16[512,512]{1,0:T(8,128)(2,1)S(1)}, bf16[512,512]{1,0:T(8,128)(2,1)S(1)}, bf16[512,512]{1,0:T(8,128)(2,1)S(1)}, bf16[512,512]{1,0:T(8,128)(2,...) custom-call(f32[264,128]{1,0:T(8,128)S(1)} %get-tuple-element.22.mine_a, ...), custom_call_target="tpu_custom_call" | custom-call | flops 1 | bytes 7888896 | tf_op jit(solution)/shard_map/pallas_call | solution.py:374
  14.6 0.1 collective-permute-done.4.got5
  14.7 1.7 %collective-permute-done.5.got6 = f32[264,128]{1,0:T(8,128)S(1)} collective-permute-done((f32[264,128]{1,0:T(8,128)S(1)}, f32[264,128]{1,0:T(8,128)S(1)}, u32[]{:S(2)}, u32[]{:S(2)}) %collective-permute-start.5) | collective-permute-done | bytes 135200 | tf_op jit(solution)/shard_map/ppermute | solution.py:394
  16.4 0.4 %shard_map.62 = (f32[512,512]{1,0:T(8,128)S(1)}, f32[256,512]{1,0:T(8,128)S(1)}, f32[256,512]{1,0:T(8,128)S(1)}) custom-call(f32[264,128]{1,0:T(8,128)S(1)} %get-tuple-element.22.mine_a, f32[264,128]{1,0:T(8,128)S(1)} %collective-permute-done.got1, f32[264,128]{1,0:T(8,128)S(1)} %collective-permute-done.1.got2.got, ...), custom_call_target="tpu_custom_call" | custom-call | flops 9663676416 | bytes 4878336 | tf_op jit(solution)/shard_map/pallas_call | solution.py:374
  16.8 0.7 %collective-permute-start.7 = (f32[256,512]{1,0:T(8,128)S(1)}, f32[256,512]{1,0:T(8,128)S(1)}, u32[]{:S(2)}, u32[]{:S(2)}) collective-permute-start(f32[256,512]{1,0:T(8,128)S(1)} %get-tuple-element.29), channel_id=1, source_target_pairs={{0,1},{1,0},{2,3},{3,2},{4,5},{5,4},{6,7},{7,6},{8,9},{9,8},{10,11... | collective-permute-start | bytes 1572872 | tf_op jit(solution)/shard_map/ppermute | solution.py:399
  17.5 0.1 collective-permute-start.8
  17.6 1.1 %shard_map.64 = (f32[512,512]{1,0:T(8,128)S(1)}, f32[2,256,256]{2,1,0:T(8,128)S(1)}) custom-call(f32[512,512]{1,0:T(8,128)S(1)} %get-tuple-element.31.quadrant, f32[264,128]{1,0:T(8,128)S(1)} %collective-permute-done.4.got5, f32[264,128]{1,0:T(8,128)S(1)} %collective-permute-done.5.got6, f32[512,512]{1,0:T(8,128)S(1)} %get-tuple-element.32.most, ...), custom_call_target="tpu_custom_call" | custom-call | flops 1073741824 | bytes 7610368 | tf_op jit(solution)/shard_map/pallas_call | solution.py:374
  18.7 0.9 %collective-permute-start.11 = (f32[2,256,256]{2,1,0:T(8,128)S(1)}, f32[2,256,256]{2,1,0:T(8,128)S(1)}, u32[]{:S(2)}, u32[]{:S(2)}) collective-permute-start(f32[2,256,256]{2,1,0:T(8,128)S(1)} %get-tuple-element.39.near), channel_id=1, source_target_pairs={{0,1},{1,0},{2,3},{3,2},{4,5},{5,4},{6,7},{7,6},{8,9},{9,8},{10,11... | collective-permute-start | bytes 1572872 | tf_op jit(solution)/shard_map/ppermute | solution.py:399
  19.6 0.0 collective-permute-done.9.got
  19.6 0.4 %collective-permute-start.10 = (f32[264,128]{1,0:T(8,128)S(1)}, f32[264,128]{1,0:T(8,128)S(1)}, u32[]{:S(2)}, u32[]{:S(2)}) collective-permute-start(f32[264,128]{1,0:T(8,128)S(1)} %collective-permute-done.9.got), channel_id=1, source_target_pairs={{0,1},{1,0},{2,3},{3,2},{4,5},{5,4},{6,7},{7,6},{8,9},{9,8},{10,11... | collective-permute-start | bytes 405512 | tf_op jit(solution)/shard_map/ppermute | solution.py:399
  20.0 0.0 collective-permute-done.7.early.early_a
  20.0 1.3 %shard_map.66 = (f32[2,256,256]{2,1,0:T(8,128)S(1)}, f32[512,512]{1,0:T(8,128)S(1)}) custom-call(f32[264,128]{1,0:T(8,128)S(1)} %collective-permute-done.got1, f32[264,128]{1,0:T(8,128)S(1)} %collective-permute-done.1.got2.got, f32[264,128]{1,0:T(8,128)S(1)} %collective-permute-done.4.got5, f32[264,128]{1,0:T(8,128)S(1)} %shard_map.65.got7, ...), custom_call_target="tpu_custom_call" | custom-call | flops 1 | bytes 4734976 | tf_op jit(solution)/shard_map/pallas_call | solution.py:374
  21.2 0.0 collective-permute-done.10.late
  21.3 0.0 collective-permute-done.8.early_b
  21.3 0.0 collective-permute-done.11.near_other
  21.3 2.1 %shard_map.67 = (f32[512,512]{1,0:T(8,128)}, f32[2,256,256]{2,1,0:T(8,128)}) custom-call(f32[256,512]{1,0:T(8,128)S(1)} %collective-permute-done.7.early.early_a, f32[256,512]{1,0:T(8,128)S(1)} %collective-permute-done.8.early_b, f32[264,128]{1,0:T(8,128)S(1)} %collective-permute-done.10.late, f32[512,512]{1,0:T(8,128)S(1)} %get-tuple-element.38.partial, ...), custom_call_target="tpu_custom_call" | custom-call | flops 1 | bytes 8523776 | tf_op jit(solution)/shard_map/pallas_call | solution.py:374
  (5 shorter events, 0.0 us)
Async XLA Ops:
  0.6 4.8 %copy-start.1 = (f32[512,512]{1,0:T(8,128)S(1)}, f32[512,512]{1,0:T(8,128)}, u32[]{:S(2)}) copy-start(f32[512,512]{1,0:T(8,128)} %panel.1) | copy-start | bytes 3145732
  0.6 4.8 %copy-start = (f32[2,256,256]{2,1,0:T(8,128)S(1)}, f32[2,256,256]{2,1,0:T(8,128)}, u32[]{:S(2)}) copy-start(f32[2,256,256]{2,1,0:T(8,128)} %diag_inv.3) | copy-start | bytes 1572868
  1.8 6.7 %collective-permute-start = (f32[264,128]{1,0:T(8,128)S(1)}, f32[264,128]{1,0:T(8,128)S(1)}, u32[]{:S(2)}, u32[]{:S(2)}) collective-permute-start(f32[264,128]{1,0:T(8,128)S(1)} %get-tuple-element.22.mine_a), channel_id=1, source_target_pairs={{0,9},{1,3},{2,11},{3,1},{4,13},{5,7},{6,15},{7,5},{8,10},{9,0},{1... | collective-permute-start | bytes 405512 | tf_op jit(solution)/shard_map/ppermute | solution.py:394
  3.9 5.5 %collective-permute-start.3 = (f32[264,128]{1,0:T(8,128)S(1)}, f32[264,128]{1,0:T(8,128)S(1)}, u32[]{:S(2)}, u32[]{:S(2)}) collective-permute-start(f32[264,128]{1,0:T(8,128)S(1)} %get-tuple-element.23.mine_b), channel_id=1, source_target_pairs={{0,4},{1,3},{2,6},{3,1},{4,0},{5,7},{6,2},{7,5},{8,10},{9,13},{10,... | collective-permute-start | bytes 405512 | tf_op jit(solution)/shard_map/ppermute | solution.py:394
  4.0 6.0 %collective-permute-start.1 = (f32[264,128]{1,0:T(8,128)S(1)}, f32[264,128]{1,0:T(8,128)S(1)}, u32[]{:S(2)}, u32[]{:S(2)}) collective-permute-start(f32[264,128]{1,0:T(8,128)S(1)} %get-tuple-element.22.mine_a), channel_id=1, source_target_pairs={{0,13},{1,5},{2,15},{3,7},{4,9},{5,1},{6,11},{7,3},{8,12},{9,4},{1... | collective-permute-start | bytes 405512 | tf_op jit(solution)/shard_map/ppermute | solution.py:394
  6.1 6.6 %collective-permute-start.6 = (f32[512,512]{1,0:T(8,128)S(1)}, f32[512,512]{1,0:T(8,128)S(1)}, u32[]{:S(2)}, u32[]{:S(2)}) collective-permute-start(f32[512,512]{1,0:T(8,128)S(1)} %get-tuple-element.25.factor), channel_id=1, source_target_pairs={{0,1},{1,0},{2,3},{3,2},{4,5},{5,4},{6,7},{7,6},{8,9},{9,8},{10,11... | collective-permute-start | bytes 3145736 | tf_op jit(solution)/shard_map/ppermute | solution.py:399
  7.9 4.8 %collective-permute-start.2 = (f32[264,128]{1,0:T(8,128)S(1)}, f32[264,128]{1,0:T(8,128)S(1)}, u32[]{:S(2)}, u32[]{:S(2)}) collective-permute-start(f32[264,128]{1,0:T(8,128)S(1)} %get-tuple-element.23.mine_b), channel_id=1, source_target_pairs={{0,2},{1,5},{2,0},{3,7},{4,6},{5,1},{6,4},{7,3},{8,12},{9,11},{10,... | collective-permute-start | bytes 405512 | tf_op jit(solution)/shard_map/ppermute | solution.py:394
  8.5 6.2 %collective-permute-start.4 = (f32[264,128]{1,0:T(8,128)S(1)}, f32[264,128]{1,0:T(8,128)S(1)}, u32[]{:S(2)}, u32[]{:S(2)}) collective-permute-start(f32[264,128]{1,0:T(8,128)S(1)} %collective-permute-done.got1), channel_id=1, source_target_pairs={{0,2},{1,5},{2,0},{3,7},{4,6},{5,1},{6,4},{7,3},{8,12},{9,11},{10,... | collective-permute-start | bytes 405512 | tf_op jit(solution)/shard_map/ppermute | solution.py:394
  9.4 7.1 %collective-permute-start.5 = (f32[264,128]{1,0:T(8,128)S(1)}, f32[264,128]{1,0:T(8,128)S(1)}, u32[]{:S(2)}, u32[]{:S(2)}) collective-permute-start(f32[264,128]{1,0:T(8,128)S(1)} %collective-permute-done.3.got4), channel_id=1, source_target_pairs={{0,2},{1,5},{2,0},{3,7},{4,6},{5,1},{6,4},{7,3},{8,12},{9,11},{10,... | collective-permute-start | bytes 405512 | tf_op jit(solution)/shard_map/ppermute | solution.py:394
  9.9 9.6 %collective-permute-start.9 = (f32[264,128]{1,0:T(8,128)S(1)}, f32[264,128]{1,0:T(8,128)S(1)}, u32[]{:S(2)}, u32[]{:S(2)}) collective-permute-start(f32[264,128]{1,0:T(8,128)S(1)} %shard_map.63), channel_id=1, source_target_pairs={{0,2},{1,17},{2,0},{3,19},{4,6},{5,21},{6,4},{7,23},{8,24},{9,11},... | collective-permute-start | bytes 405512 | tf_op jit(solution)/shard_map/ppermute | solution.py:394
  16.8 3.1 %collective-permute-start.7 = (f32[256,512]{1,0:T(8,128)S(1)}, f32[256,512]{1,0:T(8,128)S(1)}, u32[]{:S(2)}, u32[]{:S(2)}) collective-permute-start(f32[256,512]{1,0:T(8,128)S(1)} %get-tuple-element.29), channel_id=1, source_target_pairs={{0,1},{1,0},{2,3},{3,2},{4,5},{5,4},{6,7},{7,6},{8,9},{9,8},{10,11... | collective-permute-start | bytes 1572872 | tf_op jit(solution)/shard_map/ppermute | solution.py:399
  17.5 3.8 %collective-permute-start.8 = (f32[256,512]{1,0:T(8,128)S(1)}, f32[256,512]{1,0:T(8,128)S(1)}, u32[]{:S(2)}, u32[]{:S(2)}) collective-permute-start(f32[256,512]{1,0:T(8,128)S(1)} %get-tuple-element.30), channel_id=1, source_target_pairs={{0,1},{1,0},{2,3},{3,2},{4,5},{5,4},{6,7},{7,6},{8,9},{9,8},{10,11... | collective-permute-start | bytes 1572872 | tf_op jit(solution)/shard_map/ppermute | solution.py:399
  18.7 2.6 %collective-permute-start.11 = (f32[2,256,256]{2,1,0:T(8,128)S(1)}, f32[2,256,256]{2,1,0:T(8,128)S(1)}, u32[]{:S(2)}, u32[]{:S(2)}) collective-permute-start(f32[2,256,256]{2,1,0:T(8,128)S(1)} %get-tuple-element.39.near), channel_id=1, source_target_pairs={{0,1},{1,0},{2,3},{3,2},{4,5},{5,4},{6,7},{7,6},{8,9},{9,8},{10,11... | collective-permute-start | bytes 1572872 | tf_op jit(solution)/shard_map/ppermute | solution.py:399
  19.6 1.7 %collective-permute-start.10 = (f32[264,128]{1,0:T(8,128)S(1)}, f32[264,128]{1,0:T(8,128)S(1)}, u32[]{:S(2)}, u32[]{:S(2)}) collective-permute-start(f32[264,128]{1,0:T(8,128)S(1)} %collective-permute-done.9.got), channel_id=1, source_target_pairs={{0,1},{1,0},{2,3},{3,2},{4,5},{5,4},{6,7},{7,6},{8,9},{9,8},{10,11... | collective-permute-start | bytes 405512 | tf_op jit(solution)/shard_map/ppermute | solution.py:399

commit v9 on v7

--- a/solution.py
+++ b/solution.py
@@ -311,14 +311,14 @@
 
     @pl.when(diagonal)
     def _():
-        for j in children:
-            diag_here[j] = (near[j] + near_other[j]) + far[j]
-            diag_stores[j].start()
         early = [ref[pl.ds(c * chunk, chunk), :] for ref in (early_a, early_b) for c in range(ref.shape[0] // chunk)]
         for n, here in enumerate(early):
             rows = at((place, beside, over, across)[n], chunk)
             sigma_here[rows, :] = -(partial[rows, :] + here)
             store(rows, n).start()
+        for j in children:
+            diag_here[j] = (near[j] + near_other[j]) + far[j]
+            diag_stores[j].start()
 
     @pl.when(jnp.logical_not(diagonal))
     def _():

time: 23.6 us -> 23.6 us (level)
  no operation moved by 1% of the time
where the time goes in v9:
time: 23.6 us; the launch traced here: 23.4 us
  starting transfers between devices  11.4 us (48%)
  Pallas kernels  8.54 us (36%)
  waiting for transfers between devices  2.71 us (11%)
  between operations  0.71 us (3%)
    pallas_call x9, Pallas kernels, call(): pl.pallas_call(kernel, out_shape=out_shapes, in_specs=specs or [VMEM] * l...  8.54 us
    ppermute x7, starting transfers between devices, permute(): return lax.ppermute(value, AXES, pairs)  7.61 us
    ppermute x5, starting transfers between devices, exchange(): lax.ppermute(value, AXES, [(d, d ^ 1) for d in range(cfgs * prows * cores)])  3.8 us
    ppermute x7, waiting for transfers between devices, permute(): return lax.ppermute(value, AXES, pairs)  2.65 us
  transfers between devices with their start and end apart: 12, of which 3 were waited for; matrix products, arithmetic and copies ran while one was open for 0% of the time, Pallas kernels for 23%

profile of v9, /device:TPU:1, one launch (start us, length us, event | category | flops | bytes accessed | tf_op | source)
XLA Modules:
  0.0 23.4 jit_solution(5132372312867701718)
XLA Ops:
  0.6 0.0 copy-start.1
  0.7 1.1 %shard_map.59 = (f32[264,128]{1,0:T(8,128)S(1)}, f32[264,128]{1,0:T(8,128)S(1)}, f32[8,256]{1,0:T(8,128)S(1)}) custom-call(f32[128,512]{1,0:T(8,128)} %sigma_top.1, s32[2,8]{1,0:T(2,128)} %pattern.1), custom_call_target="tpu_custom_call" | custom-call | flops 10737418240 | bytes 540736 | tf_op jit(solution)/shard_map/pallas_call | solution.py:367
  1.8 2.1 %collective-permute-start = (f32[264,128]{1,0:T(8,128)S(1)}, f32[264,128]{1,0:T(8,128)S(1)}, u32[]{:S(2)}, u32[]{:S(2)}) collective-permute-start(f32[264,128]{1,0:T(8,128)S(1)} %get-tuple-element.22.mine_a), channel_id=1, source_target_pairs={{0,9},{1,3},{2,11},{3,1},{4,13},{5,7},{6,15},{7,5},{8,10},{9,0},{1... | collective-permute-start | bytes 405512 | tf_op jit(solution)/shard_map/ppermute | solution.py:387
  3.9 0.1 collective-permute-start.3
  4.0 1.5 %collective-permute-start.1 = (f32[264,128]{1,0:T(8,128)S(1)}, f32[264,128]{1,0:T(8,128)S(1)}, u32[]{:S(2)}, u32[]{:S(2)}) collective-permute-start(f32[264,128]{1,0:T(8,128)S(1)} %get-tuple-element.22.mine_a), channel_id=1, source_target_pairs={{0,13},{1,5},{2,15},{3,7},{4,9},{5,1},{6,11},{7,3},{8,12},{9,4},{1... | collective-permute-start | bytes 405512 | tf_op jit(solution)/shard_map/ppermute | solution.py:387
  5.4 0.6 %shard_map.60 = (f32[512,512]{1,0:T(8,128)S(1)}, bf16[512,512]{1,0:T(8,128)(2,1)S(1)}, bf16[512,512]{1,0:T(8,128)(2,1)S(1)}) custom-call(f32[8,256]{1,0:T(8,128)S(1)} %get-tuple-element.24.mask, f32[512,512]{1,0:T(8,128)S(1)} %copy-done.1, f32[2,256,256]{2,1,0:T(8,128)S(1)} %copy-done), custom_call_target="tpu_custom_call" | custom-call | flops 1 | bytes 3678208 | tf_op jit(solution)/shard_map/pallas_call | solution.py:367
  6.1 1.8 %collective-permute-start.6 = (f32[512,512]{1,0:T(8,128)S(1)}, f32[512,512]{1,0:T(8,128)S(1)}, u32[]{:S(2)}, u32[]{:S(2)}) collective-permute-start(f32[512,512]{1,0:T(8,128)S(1)} %get-tuple-element.25.factor), channel_id=1, source_target_pairs={{0,1},{1,0},{2,3},{3,2},{4,5},{5,4},{6,7},{7,6},{8,9},{9,8},{10,11... | collective-permute-start | bytes 3145736 | tf_op jit(solution)/shard_map/ppermute | solution.py:392
  7.9 0.6 %collective-permute-start.2 = (f32[264,128]{1,0:T(8,128)S(1)}, f32[264,128]{1,0:T(8,128)S(1)}, u32[]{:S(2)}, u32[]{:S(2)}) collective-permute-start(f32[264,128]{1,0:T(8,128)S(1)} %get-tuple-element.23.mine_b), channel_id=1, source_target_pairs={{0,2},{1,5},{2,0},{3,7},{4,6},{5,1},{6,4},{7,3},{8,12},{9,11},{10,... | collective-permute-start | bytes 405512 | tf_op jit(solution)/shard_map/ppermute | solution.py:387
  8.4 0.0 collective-permute-done.got1
  8.5 0.9 %collective-permute-start.4 = (f32[264,128]{1,0:T(8,128)S(1)}, f32[264,128]{1,0:T(8,128)S(1)}, u32[]{:S(2)}, u32[]{:S(2)}) collective-permute-start(f32[264,128]{1,0:T(8,128)S(1)} %collective-permute-done.got1), channel_id=1, source_target_pairs={{0,2},{1,5},{2,0},{3,7},{4,6},{5,1},{6,4},{7,3},{8,12},{9,11},{10,... | collective-permute-start | bytes 405512 | tf_op jit(solution)/shard_map/ppermute | solution.py:387
  9.4 0.0 collective-permute-done.3.got4
  9.4 0.6 %collective-permute-start.5 = (f32[264,128]{1,0:T(8,128)S(1)}, f32[264,128]{1,0:T(8,128)S(1)}, u32[]{:S(2)}, u32[]{:S(2)}) collective-permute-start(f32[264,128]{1,0:T(8,128)S(1)} %collective-permute-done.3.got4), channel_id=1, source_target_pairs={{0,2},{1,5},{2,0},{3,7},{4,6},{5,1},{6,4},{7,3},{8,12},{9,11},{10,... | collective-permute-start | bytes 405512 | tf_op jit(solution)/shard_map/ppermute | solution.py:387
  9.9 0.0 collective-permute-done.1.got2.got
  9.9 1.9 %collective-permute-start.9 = (f32[264,128]{1,0:T(8,128)S(1)}, f32[264,128]{1,0:T(8,128)S(1)}, u32[]{:S(2)}, u32[]{:S(2)}) collective-permute-start(f32[264,128]{1,0:T(8,128)S(1)} %shard_map.63), channel_id=1, source_target_pairs={{0,2},{1,17},{2,0},{3,19},{4,6},{5,21},{6,4},{7,23},{8,24},{9,11},... | collective-permute-start | bytes 405512 | tf_op jit(solution)/shard_map/ppermute | solution.py:387
  11.9 0.8 %collective-permute-done.2.got3 = f32[264,128]{1,0:T(8,128)S(1)} collective-permute-done((f32[264,128]{1,0:T(8,128)S(1)}, f32[264,128]{1,0:T(8,128)S(1)}, u32[]{:S(2)}, u32[]{:S(2)}) %collective-permute-start.2) | collective-permute-done | bytes 135200 | tf_op jit(solution)/shard_map/ppermute | solution.py:387
  12.7 0.0 collective-permute-done.6.factor_other
  12.7 1.9 %shard_map.61 = (bf16[512,512]{1,0:T(8,128)(2,1)S(1)}, bf16[512,512]{1,0:T(8,128)(2,1)S(1)}, bf16[512,512]{1,0:T(8,128)(2,1)S(1)}, bf16[512,512]{1,0:T(8,128)(2,...) custom-call(f32[264,128]{1,0:T(8,128)S(1)} %get-tuple-element.22.mine_a, ...), custom_call_target="tpu_custom_call" | custom-call | flops 1 | bytes 7888896 | tf_op jit(solution)/shard_map/pallas_call | solution.py:367
  14.6 0.1 collective-permute-done.4.got5
  14.7 1.7 %collective-permute-done.5.got6 = f32[264,128]{1,0:T(8,128)S(1)} collective-permute-done((f32[264,128]{1,0:T(8,128)S(1)}, f32[264,128]{1,0:T(8,128)S(1)}, u32[]{:S(2)}, u32[]{:S(2)}) %collective-permute-start.5) | collective-permute-done | bytes 135200 | tf_op jit(solution)/shard_map/ppermute | solution.py:387
  16.4 0.4 %shard_map.62 = (f32[512,512]{1,0:T(8,128)S(1)}, f32[256,512]{1,0:T(8,128)S(1)}, f32[256,512]{1,0:T(8,128)S(1)}) custom-call(f32[264,128]{1,0:T(8,128)S(1)} %get-tuple-element.22.mine_a, f32[264,128]{1,0:T(8,128)S(1)} %collective-permute-done.got1, f32[264,128]{1,0:T(8,128)S(1)} %collective-permute-done.1.got2.got, ...), custom_call_target="tpu_custom_call" | custom-call | flops 9663676416 | bytes 4878336 | tf_op jit(solution)/shard_map/pallas_call | solution.py:367
  16.8 0.7 %collective-permute-start.7 = (f32[256,512]{1,0:T(8,128)S(1)}, f32[256,512]{1,0:T(8,128)S(1)}, u32[]{:S(2)}, u32[]{:S(2)}) collective-permute-start(f32[256,512]{1,0:T(8,128)S(1)} %get-tuple-element.29), channel_id=1, source_target_pairs={{0,1},{1,0},{2,3},{3,2},{4,5},{5,4},{6,7},{7,6},{8,9},{9,8},{10,11... | collective-permute-start | bytes 1572872 | tf_op jit(solution)/shard_map/ppermute | solution.py:392
  17.5 0.1 collective-permute-start.8
  17.6 1.1 %shard_map.64 = (f32[512,512]{1,0:T(8,128)S(1)}, f32[2,256,256]{2,1,0:T(8,128)S(1)}) custom-call(f32[512,512]{1,0:T(8,128)S(1)} %get-tuple-element.31.quadrant, f32[264,128]{1,0:T(8,128)S(1)} %collective-permute-done.4.got5, f32[264,128]{1,0:T(8,128)S(1)} %collective-permute-done.5.got6, f32[512,512]{1,0:T(8,128)S(1)} %get-tuple-element.32.most, ...), custom_call_target="tpu_custom_call" | custom-call | flops 1073741824 | bytes 7610368 | tf_op jit(solution)/shard_map/pallas_call | solution.py:367
  18.7 0.9 %collective-permute-start.11 = (f32[2,256,256]{2,1,0:T(8,128)S(1)}, f32[2,256,256]{2,1,0:T(8,128)S(1)}, u32[]{:S(2)}, u32[]{:S(2)}) collective-permute-start(f32[2,256,256]{2,1,0:T(8,128)S(1)} %get-tuple-element.39.near), channel_id=1, source_target_pairs={{0,1},{1,0},{2,3},{3,2},{4,5},{5,4},{6,7},{7,6},{8,9},{9,8},{10,11... | collective-permute-start | bytes 1572872 | tf_op jit(solution)/shard_map/ppermute | solution.py:392
  19.6 0.0 collective-permute-done.9.got
  19.6 0.4 %collective-permute-start.10 = (f32[264,128]{1,0:T(8,128)S(1)}, f32[264,128]{1,0:T(8,128)S(1)}, u32[]{:S(2)}, u32[]{:S(2)}) collective-permute-start(f32[264,128]{1,0:T(8,128)S(1)} %collective-permute-done.9.got), channel_id=1, source_target_pairs={{0,1},{1,0},{2,3},{3,2},{4,5},{5,4},{6,7},{7,6},{8,9},{9,8},{10,11... | collective-permute-start | bytes 405512 | tf_op jit(solution)/shard_map/ppermute | solution.py:392
  20.0 0.0 collective-permute-done.7.early.early_a
  20.0 1.3 %shard_map.66 = (f32[2,256,256]{2,1,0:T(8,128)S(1)}, f32[512,512]{1,0:T(8,128)S(1)}) custom-call(f32[264,128]{1,0:T(8,128)S(1)} %collective-permute-done.got1, f32[264,128]{1,0:T(8,128)S(1)} %collective-permute-done.1.got2.got, f32[264,128]{1,0:T(8,128)S(1)} %collective-permute-done.4.got5, f32[264,128]{1,0:T(8,128)S(1)} %shard_map.65.got7, ...), custom_call_target="tpu_custom_call" | custom-call | flops 1 | bytes 4734976 | tf_op jit(solution)/shard_map/pallas_call | solution.py:367
  21.2 0.0 collective-permute-done.10.late
  21.3 0.0 collective-permute-done.8.early_b
  21.3 0.0 collective-permute-done.11.near_other
  21.3 2.1 %shard_map.67 = (f32[512,512]{1,0:T(8,128)}, f32[2,256,256]{2,1,0:T(8,128)}) custom-call(f32[256,512]{1,0:T(8,128)S(1)} %collective-permute-done.7.early.early_a, f32[256,512]{1,0:T(8,128)S(1)} %collective-permute-done.8.early_b, f32[264,128]{1,0:T(8,128)S(1)} %collective-permute-done.10.late, f32[512,512]{1,0:T(8,128)S(1)} %get-tuple-element.38.partial, ...), custom_call_target="tpu_custom_call" | custom-call | flops 1 | bytes 8523776 | tf_op jit(solution)/shard_map/pallas_call | solution.py:367
  (5 shorter events, 0.0 us)
Async XLA Ops:
  0.6 4.8 %copy-start.1 = (f32[512,512]{1,0:T(8,128)S(1)}, f32[512,512]{1,0:T(8,128)}, u32[]{:S(2)}) copy-start(f32[512,512]{1,0:T(8,128)} %panel.1) | copy-start | bytes 3145732
  0.6 4.8 %copy-start = (f32[2,256,256]{2,1,0:T(8,128)S(1)}, f32[2,256,256]{2,1,0:T(8,128)}, u32[]{:S(2)}) copy-start(f32[2,256,256]{2,1,0:T(8,128)} %diag_inv.3) | copy-start | bytes 1572868
  1.8 6.7 %collective-permute-start = (f32[264,128]{1,0:T(8,128)S(1)}, f32[264,128]{1,0:T(8,128)S(1)}, u32[]{:S(2)}, u32[]{:S(2)}) collective-permute-start(f32[264,128]{1,0:T(8,128)S(1)} %get-tuple-element.22.mine_a), channel_id=1, source_target_pairs={{0,9},{1,3},{2,11},{3,1},{4,13},{5,7},{6,15},{7,5},{8,10},{9,0},{1... | collective-permute-start | bytes 405512 | tf_op jit(solution)/shard_map/ppermute | solution.py:387
  3.9 5.5 %collective-permute-start.3 = (f32[264,128]{1,0:T(8,128)S(1)}, f32[264,128]{1,0:T(8,128)S(1)}, u32[]{:S(2)}, u32[]{:S(2)}) collective-permute-start(f32[264,128]{1,0:T(8,128)S(1)} %get-tuple-element.23.mine_b), channel_id=1, source_target_pairs={{0,4},{1,3},{2,6},{3,1},{4,0},{5,7},{6,2},{7,5},{8,10},{9,13},{10,... | collective-permute-start | bytes 405512 | tf_op jit(solution)/shard_map/ppermute | solution.py:387
  4.0 6.0 %collective-permute-start.1 = (f32[264,128]{1,0:T(8,128)S(1)}, f32[264,128]{1,0:T(8,128)S(1)}, u32[]{:S(2)}, u32[]{:S(2)}) collective-permute-start(f32[264,128]{1,0:T(8,128)S(1)} %get-tuple-element.22.mine_a), channel_id=1, source_target_pairs={{0,13},{1,5},{2,15},{3,7},{4,9},{5,1},{6,11},{7,3},{8,12},{9,4},{1... | collective-permute-start | bytes 405512 | tf_op jit(solution)/shard_map/ppermute | solution.py:387
  6.1 6.6 %collective-permute-start.6 = (f32[512,512]{1,0:T(8,128)S(1)}, f32[512,512]{1,0:T(8,128)S(1)}, u32[]{:S(2)}, u32[]{:S(2)}) collective-permute-start(f32[512,512]{1,0:T(8,128)S(1)} %get-tuple-element.25.factor), channel_id=1, source_target_pairs={{0,1},{1,0},{2,3},{3,2},{4,5},{5,4},{6,7},{7,6},{8,9},{9,8},{10,11... | collective-permute-start | bytes 3145736 | tf_op jit(solution)/shard_map/ppermute | solution.py:392
  7.9 4.8 %collective-permute-start.2 = (f32[264,128]{1,0:T(8,128)S(1)}, f32[264,128]{1,0:T(8,128)S(1)}, u32[]{:S(2)}, u32[]{:S(2)}) collective-permute-start(f32[264,128]{1,0:T(8,128)S(1)} %get-tuple-element.23.mine_b), channel_id=1, source_target_pairs={{0,2},{1,5},{2,0},{3,7},{4,6},{5,1},{6,4},{7,3},{8,12},{9,11},{10,... | collective-permute-start | bytes 405512 | tf_op jit(solution)/shard_map/ppermute | solution.py:387
  8.5 6.2 %collective-permute-start.4 = (f32[264,128]{1,0:T(8,128)S(1)}, f32[264,128]{1,0:T(8,128)S(1)}, u32[]{:S(2)}, u32[]{:S(2)}) collective-permute-start(f32[264,128]{1,0:T(8,128)S(1)} %collective-permute-done.got1), channel_id=1, source_target_pairs={{0,2},{1,5},{2,0},{3,7},{4,6},{5,1},{6,4},{7,3},{8,12},{9,11},{10,... | collective-permute-start | bytes 405512 | tf_op jit(solution)/shard_map/ppermute | solution.py:387
  9.4 7.1 %collective-permute-start.5 = (f32[264,128]{1,0:T(8,128)S(1)}, f32[264,128]{1,0:T(8,128)S(1)}, u32[]{:S(2)}, u32[]{:S(2)}) collective-permute-start(f32[264,128]{1,0:T(8,128)S(1)} %collective-permute-done.3.got4), channel_id=1, source_target_pairs={{0,2},{1,5},{2,0},{3,7},{4,6},{5,1},{6,4},{7,3},{8,12},{9,11},{10,... | collective-permute-start | bytes 405512 | tf_op jit(solution)/shard_map/ppermute | solution.py:387
  9.9 9.6 %collective-permute-start.9 = (f32[264,128]{1,0:T(8,128)S(1)}, f32[264,128]{1,0:T(8,128)S(1)}, u32[]{:S(2)}, u32[]{:S(2)}) collective-permute-start(f32[264,128]{1,0:T(8,128)S(1)} %shard_map.63), channel_id=1, source_target_pairs={{0,2},{1,17},{2,0},{3,19},{4,6},{5,21},{6,4},{7,23},{8,24},{9,11},... | collective-permute-start | bytes 405512 | tf_op jit(solution)/shard_map/ppermute | solution.py:387
  16.8 3.1 %collective-permute-start.7 = (f32[256,512]{1,0:T(8,128)S(1)}, f32[256,512]{1,0:T(8,128)S(1)}, u32[]{:S(2)}, u32[]{:S(2)}) collective-permute-start(f32[256,512]{1,0:T(8,128)S(1)} %get-tuple-element.29), channel_id=1, source_target_pairs={{0,1},{1,0},{2,3},{3,2},{4,5},{5,4},{6,7},{7,6},{8,9},{9,8},{10,11... | collective-permute-start | bytes 1572872 | tf_op jit(solution)/shard_map/ppermute | solution.py:392
  17.5 3.8 %collective-permute-start.8 = (f32[256,512]{1,0:T(8,128)S(1)}, f32[256,512]{1,0:T(8,128)S(1)}, u32[]{:S(2)}, u32[]{:S(2)}) collective-permute-start(f32[256,512]{1,0:T(8,128)S(1)} %get-tuple-element.30), channel_id=1, source_target_pairs={{0,1},{1,0},{2,3},{3,2},{4,5},{5,4},{6,7},{7,6},{8,9},{9,8},{10,11... | collective-permute-start | bytes 1572872 | tf_op jit(solution)/shard_map/ppermute | solution.py:392
  18.7 2.6 %collective-permute-start.11 = (f32[2,256,256]{2,1,0:T(8,128)S(1)}, f32[2,256,256]{2,1,0:T(8,128)S(1)}, u32[]{:S(2)}, u32[]{:S(2)}) collective-permute-start(f32[2,256,256]{2,1,0:T(8,128)S(1)} %get-tuple-element.39.near), channel_id=1, source_target_pairs={{0,1},{1,0},{2,3},{3,2},{4,5},{5,4},{6,7},{7,6},{8,9},{9,8},{10,11... | collective-permute-start | bytes 1572872 | tf_op jit(solution)/shard_map/ppermute | solution.py:392
  19.6 1.7 %collective-permute-start.10 = (f32[264,128]{1,0:T(8,128)S(1)}, f32[264,128]{1,0:T(8,128)S(1)}, u32[]{:S(2)}, u32[]{:S(2)}) collective-permute-start(f32[264,128]{1,0:T(8,128)S(1)} %collective-permute-done.9.got), channel_id=1, source_target_pairs={{0,1},{1,0},{2,3},{3,2},{4,5},{5,4},{6,7},{7,6},{8,9},{9,8},{10,11... | collective-permute-start | bytes 405512 | tf_op jit(solution)/shard_map/ppermute | solution.py:392
